TPU v7x, 128 devices: a whole 4x4x4 slice. The times are simulated.
128 devices in a mesh: section: 8 (over x, z_hi), ctx: 4 (over z_lo, core), tp: 4 (over y).
Axes of the slice: x: 4, y: 4, z: 4 (z_hi: 2, z_lo: 2; z = z_hi * 2 + z_lo), core: 2. Of those that a mesh axis runs over, the one named last changes fastest.
Arguments:
- boundary: bfloat16 [4, 16, 160, 768], P('ctx', 'section'), may hold values from -6 to 6
- routes: int32 [4, 16, 160, 2], P('ctx', 'section'), may hold values from 0 to 3, all different within a row; in each aligned block of 160 rows (0 to 159, 160 to 319, ..., all dimensions but the last counted through in order) at most 120 rows name the same one
- lengths: int32 [4], replicated, may hold values from 1 to 160, 577 in all
- ln_gains: bfloat16 [2, 2, 768], P(None, None, ('section', 'ctx')), may hold values from 0.5 to 1.5
- ln_biases: bfloat16 [2, 2, 768], P(None, None, ('section', 'ctx')), may hold values from -1 to 1
- w_qkv: bfloat16 [2, 768, 3, 768], P(None, ('section', 'ctx'), None, 'tp'), may hold values from -0.21875 to 0.21875
- w_out: bfloat16 [2, 768, 768], P(None, 'tp', ('section', 'ctx')), may hold values from -0.625 to 0.625
- w_router: bfloat16 [2, 768, 4], P(None, ('section', 'ctx')), may hold values from -0.15625 to 0.15625
- w_in: bfloat16 [2, 4, 768, 3072], P(None, None, ('section', 'ctx'), 'tp'), may hold values from -0.21875 to 0.21875
- w_exp_out: bfloat16 [2, 4, 3072, 768], P(None, None, 'tp', ('section', 'ctx')), may hold values from -0.3125 to 0.3125
Outputs:
- ends_out: float32 [4, 16, 160, 768], P('ctx', 'section')
- grad_ln_gains: float32 [2, 2, 768], P(None, None, ('section', 'ctx'))
- grad_ln_biases: float32 [2, 2, 768], P(None, None, ('section', 'ctx'))
- grad_w_qkv: float32 [2, 768, 3, 768], P(None, ('section', 'ctx'), None, 'tp')
- grad_w_out: float32 [2, 768, 768], P(None, 'tp', ('section', 'ctx'))
- grad_w_router: float32 [2, 768, 4], P(None, ('section', 'ctx'))
- grad_w_in: float32 [2, 4, 768, 3072], P(None, None, ('section', 'ctx'), 'tp')
- grad_w_exp_out: float32 [2, 4, 3072, 768], P(None, None, 'tp', ('section', 'ctx'))
Inputs may be any that keep to these rules, and one draw needn't show every extreme that they name: `routes`: each row names two different experts. In each aligned block of 160 rows (rows taken in the order of the array's dimensions: the rows of one device for one micro-batch) no expert is named more than 120 times. The blocks' lengths sum to 577; the largest equals 160.
All inputs are finite; a program needn't handle non-finite values.
Results may differ from a plain program's by a relative error of at most 0.028.
Values may be sent and summed in bfloat16 or wider, within the bound.
A program may use at most 192 MiB of HBM per device.

v0:
```python
import jax
import jax.numpy as jnp
from jax import lax
from jax.sharding import PartitionSpec as P

HD = 64
CBLK = 160
MICRO = 2
IMGS = 1
CAP = 120


highest = lax.Precision.HIGHEST
eps = 1e-06


def shifted(shard, axis, by):
    peers = lax.axis_size(axis)
    pairs = [(i, i + by) for i in range(peers) if 0 <= i + by < peers]
    return lax.ppermute(shard, axis, pairs)


def normalize(values, scales, offset):
    average = jnp.mean(values, axis=-1, keepdims=True)
    centered = values - average
    variance = jnp.mean(centered * centered, axis=-1, keepdims=True)
    return centered * lax.rsqrt(variance + eps) * scales + offset


def expert_tables(route_rows, expert_count, capacity):
    row_count = route_rows.shape[0]
    chosen = (
        route_rows[:, :, None] == jnp.arange(expert_count, dtype=jnp.int32)[None, None, :]
    ).astype(jnp.int32)
    flat_hits = chosen.reshape(row_count * 2, expert_count)
    earlier = jnp.cumsum(flat_hits, axis=0) - flat_hits
    places = jnp.sum(earlier * flat_hits, axis=1).reshape(row_count, 2)
    slot_hits = places[:, :, None] == jnp.arange(capacity, dtype=jnp.int32)[None, None, :]
    return (chosen.astype(jnp.float32), slot_hits.astype(jnp.float32), places)


def layer_forward(tokens, params, route_block, key_live):
    ln_scales, ln_offsets, w_qkv, w_out, w_router, w_in, w_exp_out = params
    images, block_len, width_dim = tokens.shape
    head_count = w_qkv.shape[-1] // HD
    normed = normalize(tokens, ln_scales[0], ln_offsets[0]).astype(jnp.bfloat16)
    projected = jnp.einsum(
        "ibd,dth->ibth", normed, w_qkv, preferred_element_type=jnp.float32
    ).astype(jnp.bfloat16)
    keys_all, values_all = (
        lax.all_gather(projected[:, :, 1], "ctx", axis=1, tiled=True),
        lax.all_gather(projected[:, :, 2], "ctx", axis=1, tiled=True),
    )
    queries = projected[:, :, 0].reshape(images, block_len, head_count, HD)
    keys_split = keys_all.reshape(images, -1, head_count, HD)
    values_split = values_all.reshape(images, -1, head_count, HD)
    scores = HD ** (-0.5) * jnp.einsum(
        "iqhe,ikhe->ihqk", queries, keys_split, preferred_element_type=jnp.float32
    )
    scores = jnp.where(key_live[None, None, None, :], scores, -1e30)
    attn_probs = jax.nn.softmax(scores, axis=-1)
    attn_weights = attn_probs.astype(jnp.bfloat16)
    mixed_heads = jnp.einsum(
        "ihqk,ikhe->iqhe", attn_weights, values_split, preferred_element_type=jnp.float32
    )
    mixed_heads = mixed_heads.astype(jnp.bfloat16).reshape(images * block_len, head_count * HD)
    attended = lax.psum(
        jnp.dot(mixed_heads, w_out, preferred_element_type=jnp.float32).astype(jnp.bfloat16), "tp"
    ).astype(jnp.float32)
    middle = tokens + attended.reshape(images, block_len, width_dim)
    normed_two = (
        normalize(middle, ln_scales[1], ln_offsets[1])
        .astype(jnp.bfloat16)
        .reshape(images * block_len, width_dim)
    )
    logits = jnp.dot(normed_two, w_router, preferred_element_type=jnp.float32)
    router_probs = jax.nn.softmax(logits, axis=-1)
    route_rows = route_block.reshape(-1, 2)
    chosen, slot_hits, places = expert_tables(route_rows, w_in.shape[0], CAP)
    flat_index = route_rows * CAP + places
    gate_values = jnp.sum(router_probs[:, None, :] * chosen, axis=-1)
    dispatch = jnp.einsum(
        "rke,rkc->ecr",
        chosen.astype(jnp.bfloat16),
        slot_hits.astype(jnp.bfloat16),
        preferred_element_type=jnp.float32,
    ).astype(jnp.bfloat16)
    expert_in = jnp.einsum(
        "ecr,rd->ecd", dispatch, normed_two, preferred_element_type=jnp.float32
    ).astype(jnp.bfloat16)
    hidden = jnp.einsum("ecd,edf->ecf", expert_in, w_in, preferred_element_type=jnp.float32)
    active = jax.nn.gelu(hidden).astype(jnp.bfloat16)
    expert_part = jnp.einsum("ecf,efd->ecd", active, w_exp_out, preferred_element_type=jnp.float32)
    picked = expert_part.reshape(-1, width_dim)[flat_index]
    expert_local = jnp.sum(gate_values[:, :, None] * picked, axis=1)
    expert_total = lax.psum(expert_local.astype(jnp.bfloat16), "tp").astype(jnp.float32)
    result = middle + expert_total.reshape(images, block_len, width_dim)
    saved = (
        normed,
        queries,
        keys_split,
        values_split,
        attn_probs,
        attn_weights,
        mixed_heads,
        middle,
        normed_two,
        router_probs,
        chosen,
        flat_index,
        gate_values,
        picked,
        expert_in,
        hidden,
        active,
    )
    return (result, saved)


def layer_backward(tokens, params, grad_out, saved):
    ln_scales, ln_offsets, w_qkv, w_out, w_router, w_in, w_exp_out = params
    (
        normed,
        queries,
        keys_split,
        values_split,
        attn_probs,
        attn_weights,
        mixed_heads,
        middle,
        normed_two,
        router_probs,
        chosen,
        flat_index,
        gate_values,
        picked,
        expert_in,
        hidden,
        active,
    ) = saved
    images, block_len, width_dim = tokens.shape
    head_count = w_qkv.shape[-1] // HD
    expert_count = w_in.shape[0]
    grad_rows = grad_out.reshape(images * block_len, width_dim)
    scaled_rows = gate_values[:, :, None] * grad_rows[:, None, :]
    grad_outputs = (
        jnp.zeros((expert_count * CAP, width_dim), jnp.float32)
        .at[flat_index.reshape(-1)]
        .add(scaled_rows.reshape(-1, width_dim))
    )
    grad_outputs = grad_outputs.reshape(expert_count, CAP, width_dim).astype(jnp.bfloat16)
    gate_part = jnp.sum(grad_rows[:, None, :] * picked, axis=-1)
    grad_exp_out = jnp.einsum(
        "ecf,ecd->efd", active, grad_outputs, preferred_element_type=jnp.float32
    )
    grad_active = jnp.einsum(
        "ecd,efd->ecf", grad_outputs, w_exp_out, preferred_element_type=jnp.float32
    )
    grad_hidden = jax.vjp(jax.nn.gelu, hidden)[1](grad_active)[0].astype(jnp.bfloat16)
    grad_w_in = jnp.einsum(
        "ecd,ecf->edf", expert_in, grad_hidden, preferred_element_type=jnp.float32
    )
    grad_expert_in = jnp.einsum(
        "ecf,edf->ecd", grad_hidden, w_in, preferred_element_type=jnp.float32
    )
    rows_part = jnp.sum(grad_expert_in.reshape(-1, width_dim)[flat_index], axis=1)
    grad_normed_two, grad_gates = (
        lax.psum(rows_part.astype(jnp.bfloat16), "tp").astype(jnp.float32),
        lax.psum(gate_part.astype(jnp.bfloat16), "tp").astype(jnp.float32),
    )
    grad_probs = jnp.sum(grad_gates[:, :, None] * chosen, axis=1)
    grad_logits = router_probs * (
        grad_probs - jnp.sum(router_probs * grad_probs, axis=-1, keepdims=True)
    )
    grad_router = jnp.dot(normed_two.astype(jnp.float32).T, grad_logits, precision=highest)
    grad_normed_two = grad_normed_two + jnp.dot(
        grad_logits, w_router.astype(jnp.float32).T, precision=highest
    )
    pull_two = jax.vjp(normalize, middle, ln_scales[1], ln_offsets[1])[1]
    grad_mid_norm, grad_scale_two, grad_offset_two = pull_two(
        grad_normed_two.reshape(images, block_len, width_dim)
    )
    grad_middle = grad_out + grad_mid_norm
    grad_attended = grad_middle.reshape(images * block_len, width_dim).astype(jnp.bfloat16)
    grad_out_proj = jnp.einsum(
        "rf,rd->fd", mixed_heads, grad_attended, preferred_element_type=jnp.float32
    )
    grad_mixed = jnp.dot(grad_attended, w_out.T, preferred_element_type=jnp.float32).astype(
        jnp.bfloat16
    )
    grad_mixed = grad_mixed.reshape(images, block_len, head_count, HD)
    grad_weights = jnp.einsum(
        "iqhe,ikhe->ihqk", grad_mixed, values_split, preferred_element_type=jnp.float32
    )
    grad_values_part = jnp.einsum(
        "ihqk,iqhe->ikhe", attn_weights, grad_mixed, preferred_element_type=jnp.float32
    )
    grad_scores = attn_probs * (
        grad_weights - jnp.sum(attn_probs * grad_weights, axis=-1, keepdims=True)
    )
    grad_scores = grad_scores.astype(jnp.bfloat16)
    grad_queries = HD ** (-0.5) * jnp.einsum(
        "ihqk,ikhe->iqhe", grad_scores, keys_split, preferred_element_type=jnp.float32
    )
    grad_keys_part = HD ** (-0.5) * jnp.einsum(
        "ihqk,iqhe->ikhe", grad_scores, queries, preferred_element_type=jnp.float32
    )
    grad_keys, grad_values = (
        lax.psum_scatter(
            grad_keys_part.reshape(images, -1, head_count * HD).astype(jnp.bfloat16),
            "ctx",
            scatter_dimension=1,
            tiled=True,
        ).astype(jnp.float32),
        lax.psum_scatter(
            grad_values_part.reshape(images, -1, head_count * HD).astype(jnp.bfloat16),
            "ctx",
            scatter_dimension=1,
            tiled=True,
        ).astype(jnp.float32),
    )
    grad_projected = jnp.stack(
        [grad_queries.reshape(images, block_len, -1), grad_keys, grad_values], axis=2
    ).astype(jnp.bfloat16)
    grad_qkv = jnp.einsum(
        "ibd,ibth->dth", normed, grad_projected, preferred_element_type=jnp.float32
    )
    normed_part = jnp.einsum(
        "ibth,dth->ibd", grad_projected, w_qkv, preferred_element_type=jnp.float32
    )
    grad_normed = lax.psum(normed_part.astype(jnp.bfloat16), "tp").astype(jnp.float32)
    pull_one = jax.vjp(normalize, tokens, ln_scales[0], ln_offsets[0])[1]
    grad_tok_norm, grad_scale_one, grad_offset_one = pull_one(grad_normed)
    grad_tokens = grad_middle + grad_tok_norm
    layer_grads = (
        jnp.stack([grad_scale_one, grad_scale_two]),
        jnp.stack([grad_offset_one, grad_offset_two]),
        grad_qkv,
        grad_out_proj,
        grad_router,
        grad_w_in,
        grad_exp_out,
    )
    return (grad_tokens, layer_grads)


def shards(boundary, routes, lengths, ln_gains, ln_biases, w_qkv, w_out, w_router, w_in, w_exp_out):
    groups = lax.axis_size("section") // 2
    pipe_rank = lax.axis_index("section") // groups
    first_rank = pipe_rank == 0
    gathered = (
        lax.all_gather(ln_gains, ("section", "ctx"), axis=2, tiled=True),
        lax.all_gather(ln_biases, ("section", "ctx"), axis=2, tiled=True),
        lax.all_gather(w_qkv, ("section", "ctx"), axis=1, tiled=True),
        lax.all_gather(w_out, ("section", "ctx"), axis=2, tiled=True),
        lax.all_gather(w_router, ("section", "ctx"), axis=1, tiled=True),
        lax.all_gather(w_in, ("section", "ctx"), axis=2, tiled=True),
        lax.all_gather(w_exp_out, ("section", "ctx"), axis=3, tiled=True),
    )
    chosen_layer = [
        lax.dynamic_index_in_dim(piece, pipe_rank, 0, keepdims=False) for piece in gathered
    ]
    layer_params = (
        chosen_layer[0].astype(jnp.float32),
        chosen_layer[1].astype(jnp.float32),
        chosen_layer[2],
        chosen_layer[3],
        chosen_layer[4],
        chosen_layer[5],
        chosen_layer[6],
    )
    live_slots = jnp.arange(CBLK, dtype=jnp.int32)[None, :] < lengths[:, None]
    key_live = live_slots.reshape(-1)
    own_live = lax.dynamic_index_in_dim(live_slots, lax.axis_index("ctx"), 0, keepdims=False)
    row_mask = own_live.astype(jnp.float32)[None, :, None]
    width_dim = boundary.shape[-1]
    local_data = boundary.reshape(MICRO, IMGS, CBLK, width_dim)
    route_local = routes.reshape(MICRO, IMGS, CBLK, 2)
    received = jnp.zeros((IMGS, CBLK, width_dim), jnp.bfloat16)
    inputs_saved = []
    finals = []
    for t in range(MICRO + 1):
        first_mb = min(t, MICRO - 1)
        second_mb = max(t - 1, 0)
        entering = jnp.where(first_rank, local_data[first_mb], received).astype(jnp.float32)
        route_now = jnp.where(first_rank, route_local[first_mb], route_local[second_mb])
        leaving, unused = layer_forward(entering, layer_params, route_now, key_live)
        inputs_saved.append(entering)
        if t >= 1:
            finals.append(leaving)
        if t < MICRO:
            received = shifted(leaving.astype(jnp.bfloat16), "section", groups)
    back_received = jnp.zeros((IMGS, CBLK, width_dim), jnp.bfloat16)
    grad_totals = None
    input_grads = []
    for t in range(MICRO + 1):
        first_mb = max(t - 1, 0)
        second_mb = min(t, MICRO - 1)
        entering = jnp.where(first_rank, inputs_saved[first_mb], inputs_saved[min(t + 1, MICRO)])
        route_now = jnp.where(first_rank, route_local[first_mb], route_local[second_mb])
        if t < MICRO:
            cot_second = local_data[t].astype(jnp.float32) * row_mask
        else:
            cot_second = jnp.zeros((IMGS, CBLK, width_dim), jnp.float32)
        grad_out = jnp.where(first_rank, back_received.astype(jnp.float32), cot_second)
        leaving, saved = layer_forward(entering, layer_params, route_now, key_live)
        grad_tokens, layer_grads = layer_backward(entering, layer_params, grad_out, saved)
        if grad_totals is None:
            grad_totals = layer_grads
        else:
            grad_totals = tuple((a + b for a, b in zip(grad_totals, layer_grads)))
        if t >= 1:
            input_grads.append(grad_tokens)
        if t < MICRO:
            back_received = shifted(grad_tokens.astype(jnp.bfloat16), "section", -groups)
    ends = jnp.where(first_rank, jnp.stack(input_grads), jnp.stack(finals)) * row_mask
    ends_out = ends.reshape(boundary.shape)
    placed = [
        lax.dynamic_update_index_in_dim(jnp.zeros((2,) + g.shape, jnp.float32), g, pipe_rank, 0)
        for g in grad_totals
    ]
    results = (
        lax.psum_scatter(
            placed[0].astype(jnp.bfloat16), ("section", "ctx"), scatter_dimension=2, tiled=True
        ).astype(jnp.float32),
        lax.psum_scatter(
            placed[1].astype(jnp.bfloat16), ("section", "ctx"), scatter_dimension=2, tiled=True
        ).astype(jnp.float32),
        lax.psum_scatter(
            placed[2].astype(jnp.bfloat16), ("section", "ctx"), scatter_dimension=1, tiled=True
        ).astype(jnp.float32),
        lax.psum_scatter(
            placed[3].astype(jnp.bfloat16), ("section", "ctx"), scatter_dimension=2, tiled=True
        ).astype(jnp.float32),
        lax.psum_scatter(
            placed[4].astype(jnp.bfloat16), ("section", "ctx"), scatter_dimension=1, tiled=True
        ).astype(jnp.float32),
        lax.psum_scatter(
            placed[5].astype(jnp.bfloat16), ("section", "ctx"), scatter_dimension=2, tiled=True
        ).astype(jnp.float32),
        lax.psum_scatter(
            placed[6].astype(jnp.bfloat16), ("section", "ctx"), scatter_dimension=3, tiled=True
        ).astype(jnp.float32),
    )
    return (
        ends_out,
        results[0],
        results[1],
        results[2],
        results[3],
        results[4],
        results[5],
        results[6],
    )


def solution(mesh):
    return jax.shard_map(
        shards,
        mesh=mesh,
        in_specs=(
            P("ctx", "section", None, None),
            P("ctx", "section", None, None),
            P(),
            P(None, None, ("section", "ctx")),
            P(None, None, ("section", "ctx")),
            P(None, ("section", "ctx"), None, "tp"),
            P(None, "tp", ("section", "ctx")),
            P(None, ("section", "ctx"), None),
            P(None, None, ("section", "ctx"), "tp"),
            P(None, None, "tp", ("section", "ctx")),
        ),
        out_specs=(
            P("ctx", "section", None, None),
            P(None, None, ("section", "ctx")),
            P(None, None, ("section", "ctx")),
            P(None, ("section", "ctx"), None, "tp"),
            P(None, "tp", ("section", "ctx")),
            P(None, ("section", "ctx"), None),
            P(None, None, ("section", "ctx"), "tp"),
            P(None, None, "tp", ("section", "ctx")),
        ),
        check_vma=False,
    )
```

profile of v0, /device:TPU:1, one launch (start us, length us, event | category | flops | bytes accessed | tf_op | source)
XLA Modules:
  0.0 1456.7 jit_solution(3413314979537306703)
XLA Ops:
  10.4 27.5 %all_gather.58 = bf16[2,2,768]{1,0,2:T(2,128)(2,1)S(1)} all-gather(bf16[2,2,24]{1,0,2:T(2,128)(2,1)S(1)} %copy.260), channel_id=1, replica_groups=mesh['section'=8,'ctx'=4,'tp'=4] {'section','ctx'}, dimensions={2}, use_global_device_ids=true | all-gather | bytes 6336 | tf_op jit(solution)/shard_map/all_gather | solution.py:253
  37.9 24.1 %all_gather.57 = bf16[2,2,768]{1,0,2:T(2,128)(2,1)S(1)} all-gather(bf16[2,2,24]{1,0,2:T(2,128)(2,1)S(1)} %copy.259), channel_id=1, replica_groups=mesh['section'=8,'ctx'=4,'tp'=4] {'section','ctx'}, dimensions={2}, use_global_device_ids=true | all-gather | bytes 6336 | tf_op jit(solution)/shard_map/all_gather | solution.py:252
  63.1 22.9 %all_gather.62 = bf16[2,192,768]{1,2,0:T(8,128)(2,1)S(1)} all-gather(bf16[2,192,24]{1,2,0:T(8,128)(2,1)S(1)} %copy-done.130), channel_id=1, replica_groups=mesh['section'=8,'ctx'=4,'tp'=4] {'section','ctx'}, dimensions={2}, use_global_device_ids=true | all-gather | bytes 608256 | tf_op jit(solution)/shard_map/all_gather | solution.py:255
  123.8 24.2 %all_gather.63 = bf16[2,768,4]{2,0,1:T(2,128)(2,1)S(1)} all-gather(bf16[2,24,4]{2,0,1:T(2,128)(2,1)S(1)} %copy.265), channel_id=1, replica_groups=mesh['section'=8,'ctx'=4,'tp'=4] {'section','ctx'}, dimensions={1}, use_global_device_ids=true | all-gather | bytes 12672 | tf_op jit(solution)/shard_map/all_gather | solution.py:256
  155.4 56.2 %all-gather.18.cloned.1.call-done = bf16[2,4,768,768]{3,2,1,0:T(8,128)(2,1)} async-done(((bf16[2,4,24,768]{3,2,1,0:T(8,128)(2,1)}), bf16[2,4,768,768]{3,2,1,0:T(8,128)(2,1)}) %all-gather.18.cloned.1.call-update) | async-done | bytes 9437200 | tf_op jit(solution)/shard_map/all_gather | solution.py:257
  216.0 53.1 %all-gather.20.cloned.1.call-done = bf16[2,4,768,768]{2,3,1,0:T(8,128)(2,1)} async-done(((bf16[2,4,768,24]{2,3,1,0:T(8,128)(2,1)}), bf16[2,4,768,768]{2,3,1,0:T(8,128)(2,1)}) %all-gather.20.cloned.1.call-update) | async-done | bytes 9437200 | tf_op jit(solution)/shard_map/all_gather | solution.py:258
  280.9 37.3 %all-reduce.31.cloned.1.call-done = bf16[160,768]{1,0:T(8,128)(2,1)} async-done(((bf16[160,768]{1,0:T(8,128)(2,1)}), bf16[160,768]{1,0:T(8,128)(2,1)}) %all-reduce.31.cloned.1.call-update) | async-done | bytes 245776 | tf_op jit(solution)/shard_map/psum | solution.py:96
  350.1 37.6 %all-reduce.33.cloned.1.call-done = bf16[1,160,768]{2,1,0:T(8,128)(2,1)} async-done(((bf16[1,160,768]{2,1,0:T(8,128)(2,1)}), bf16[1,160,768]{2,1,0:T(8,128)(2,1)}) %all-reduce.33.cloned.1.call-update) | async-done | bytes 245776 | tf_op jit(solution)/shard_map/psum | solution.py:67
  455.4 41.7 %all-reduce.35.cloned.1.call-done = bf16[160,768]{1,0:T(8,128)(2,1)} async-done(((bf16[160,768]{1,0:T(8,128)(2,1)}), bf16[160,768]{1,0:T(8,128)(2,1)}) %all-reduce.35.cloned.1.call-update) | async-done | bytes 245776 | tf_op jit(solution)/shard_map/psum | solution.py:168
  523.8 21.5 %reduce-scatter.15.cloned.1.call-done = bf16[1,160,192]{2,1,0:T(8,128)(2,1)} async-done(((bf16[1,640,192]{2,1,0:T(8,128)(2,1)}), bf16[1,160,192]{2,1,0:T(8,128)(2,1)}) %reduce-scatter.15.cloned.1.call-update) | async-done | bytes 61456 | tf_op jit(solution)/shard_map/reduce_scatter | solution.py:209
  551.0 38.5 %all-reduce.53.cloned.1.call-done = (bf16[1,160,768]{2,1,0:T(8,128)(2,1)}, bf16[1,160,768]{2,1,0:T(8,128)(2,1)}) async-done(((bf16[1,160,768]{2,1,0:T(8,128)(2,1)}, bf16[1,160,768]{2,1,0:T(8,128)(2,1)}), (bf16[1,160,768]{2,1,0:T(8,128)(2,1)}, bf16[1,160,768]{2,1,0:T(8,128)(2,1)})) %all-reduce.53.cloned.1.call-update) | async-done | bytes 491536 | tf_op jit(solution)/shard_map/psum | solution.py:67
  616.6 37.1 %all-reduce.37.cloned.1.call-done = bf16[1,160,768]{2,1,0:T(8,128)(2,1)} async-done(((bf16[1,160,768]{2,1,0:T(8,128)(2,1)}), bf16[1,160,768]{2,1,0:T(8,128)(2,1)}) %all-reduce.37.cloned.1.call-update) | async-done | bytes 245776 | tf_op jit(solution)/shard_map/psum | solution.py:96
  685.4 38.1 %all-reduce.45.cloned.1.call-done = bf16[1,160,768]{2,1,0:T(8,128)(2,1)} async-done(((bf16[1,160,768]{2,1,0:T(8,128)(2,1)}), bf16[1,160,768]{2,1,0:T(8,128)(2,1)}) %all-reduce.45.cloned.1.call-update) | async-done | bytes 245776 | tf_op jit(solution)/shard_map/psum | solution.py:67
  768.7 36.6 %all-reduce.39.cloned.1.call-done = bf16[1,160,768]{2,1,0:T(8,128)(2,1)} async-done(((bf16[1,160,768]{2,1,0:T(8,128)(2,1)}), bf16[1,160,768]{2,1,0:T(8,128)(2,1)}) %all-reduce.39.cloned.1.call-update) | async-done | bytes 245776 | tf_op jit(solution)/shard_map/psum | solution.py:67
  873.4 40.5 %all-reduce.41.cloned.1.call-done = bf16[160,768]{1,0:T(8,128)(2,1)} async-done(((bf16[160,768]{1,0:T(8,128)(2,1)}), bf16[160,768]{1,0:T(8,128)(2,1)}) %all-reduce.41.cloned.1.call-update) | async-done | bytes 245776 | tf_op jit(solution)/shard_map/psum | solution.py:168
  939.7 20.9 %reduce-scatter.19.cloned.1.call-done = bf16[1,160,192]{2,1,0:T(8,128)(2,1)} async-done(((bf16[1,640,192]{2,1,0:T(8,128)(2,1)}), bf16[1,160,192]{2,1,0:T(8,128)(2,1)}) %reduce-scatter.19.cloned.1.call-update) | async-done | bytes 61456 | tf_op jit(solution)/shard_map/reduce_scatter | solution.py:209
  967.1 37.7 %all-reduce.51.cloned.1.call-done = (bf16[1,160,768]{2,1,0:T(8,128)(2,1)}, bf16[1,160,768]{2,1,0:T(8,128)(2,1)}) async-done(((bf16[1,160,768]{2,1,0:T(8,128)(2,1)}, bf16[1,160,768]{2,1,0:T(8,128)(2,1)}), (bf16[1,160,768]{2,1,0:T(8,128)(2,1)}, bf16[1,160,768]{2,1,0:T(8,128)(2,1)})) %all-reduce.51.cloned.1.call-update) | async-done | bytes 491536 | tf_op jit(solution)/shard_map/psum | solution.py:67
  1031.4 13.8 psum.140
  1094.7 21.3 %all-reduce.43.cloned.1.call-done = bf16[160,768]{1,0:T(8,128)(2,1)} async-done(((bf16[160,768]{1,0:T(8,128)(2,1)}), bf16[160,768]{1,0:T(8,128)(2,1)}) %all-reduce.43.cloned.1.call-update) | async-done | bytes 245776 | tf_op jit(solution)/shard_map/psum | solution.py:168
  1144.0 20.9 %reduce-scatter.23.cloned.1.call-done = bf16[1,160,192]{2,1,0:T(8,128)(2,1)} async-done(((bf16[1,640,192]{2,1,0:T(8,128)(2,1)}), bf16[1,160,192]{2,1,0:T(8,128)(2,1)}) %reduce-scatter.23.cloned.1.call-update) | async-done | bytes 61456 | tf_op jit(solution)/shard_map/reduce_scatter | solution.py:209
  1206.8 19.4 %copy.333 = bf16[2,4,768,768]{2,1,0,3:T(4,128)(2,1)} copy(bf16[2,4,768,768]{3,1,0,2:T(4,128)(2,1)} %copy_dynamic-update-slice_fusion) | data formatting | bytes 18874368
  1226.2 15.4 %reshape.2392 = bf16[768,6144]{1,0:T(8,128)(2,1)} reshape(bf16[768,2,4,768]{3,2,1,0:T(4,128)(2,1)} %bitcast.791) | data formatting | bytes 18874368
  1246.7 123.7 %all-reduce.10 = (bf16[2,2,768]{2,1,0:T(2,128)(2,1)S(1)}, bf16[2,2,768]{2,1,0:T(2,128)(2,1)S(1)}, bf16[2,768,4]{1,2,0:T(4,128)(2,1)S(1)}) all-reduce(bf16[2,2,768]{2,1,0:T(2,128)(2,1)S(1)} %fusion.397, bf16[2,2,768]{2,1,0:T(2,128)(2,1)S(1)} %fusion.399, ...), channel_id=20, replica_groups=mesh['section'=8,'ctx'=4,'tp'=4] {'section','ctx'}, use_global_device_ids=true, to_apply=%region_129.130.clone | all-reduce | flops 12288 | bytes 49152
  1379.7 68.3 %reduce-scatter.27.cloned.1.call-done = bf16[24,6144]{1,0:T(8,128)(2,1)} async-done(((bf16[768,6144]{1,0:T(8,128)(2,1)}), bf16[24,6144]{1,0:T(8,128)(2,1)}) %reduce-scatter.27.cloned.1.call-update) | async-done | bytes 294928
  (788 shorter events, 560.4 us)
Async XLA Ops:
  7.2 88.1 %all-gather.16.cloned.1.call-start = ((), (), s32[]{:S(2)}) async-start(), calls=%async_computation.7 | async-start | bytes 2433024 | tf_op jit(solution)/shard_map/all_gather | solution.py:254
  7.9 143.3 %all-reduce.29.cloned.1.call-start = ((), (), s32[]{:S(2)}) async-start(), calls=%async_computation.8 | async-start | bytes 491520 | tf_op jit(solution)/shard_map/psum | solution.py:67
  112.5 99.1 %all-gather.18.cloned.1.call-start = ((), (), s32[]{:S(2)}) async-start(), calls=%async_computation.9 | async-start | bytes 9732096 | tf_op jit(solution)/shard_map/all_gather | solution.py:257
  113.2 155.8 %all-gather.20.cloned.1.call-start = ((), (), s32[]{:S(2)}) async-start(), calls=%async_computation.10 | async-start | bytes 9732096 | tf_op jit(solution)/shard_map/all_gather | solution.py:258
  113.8 204.3 %all-reduce.31.cloned.1.call-start = ((), (), s32[]{:S(2)}) async-start(), calls=%async_computation.11 | async-start | bytes 491520 | tf_op jit(solution)/shard_map/psum | solution.py:96
  279.4 108.4 %all-reduce.33.cloned.1.call-start = ((), (), s32[]{:S(2)}) async-start(), calls=%async_computation.12 | async-start | bytes 491520 | tf_op jit(solution)/shard_map/psum | solution.py:67
  347.9 149.3 %all-reduce.35.cloned.1.call-start = ((), (), s32[]{:S(2)}) async-start(), calls=%async_computation.13 | async-start | bytes 491520 | tf_op jit(solution)/shard_map/psum | solution.py:168
  454.7 69.2 %reduce-scatter.17.cloned.1.call-start = ((), (), s32[]{:S(2)}) async-start(), calls=%async_computation.15 | async-start | bytes 409600 | tf_op jit(solution)/shard_map/reduce_scatter | solution.py:215
  503.6 41.7 %reduce-scatter.15.cloned.1.call-start = ((), (), s32[]{:S(2)}) async-start(), calls=%async_computation.14 | async-start | bytes 409600 | tf_op jit(solution)/shard_map/reduce_scatter | solution.py:209
  507.7 81.9 %all-reduce.53.cloned.1.call-start = ((), (), s32[]{:S(2)}) async-start(), calls=%async_computation.29 | async-start | bytes 983040 | tf_op jit(solution)/shard_map/psum | solution.py:67
  548.0 105.7 %all-reduce.37.cloned.1.call-start = ((), (), s32[]{:S(2)}) async-start(), calls=%async_computation.16 | async-start | bytes 491520 | tf_op jit(solution)/shard_map/psum | solution.py:96
  611.4 112.1 %all-reduce.45.cloned.1.call-start = ((), (), s32[]{:S(2)}) async-start(), calls=%async_computation.24 | async-start | bytes 491520 | tf_op jit(solution)/shard_map/psum | solution.py:67
  683.6 121.7 %all-reduce.39.cloned.1.call-start = ((), (), s32[]{:S(2)}) async-start(), calls=%async_computation.17 | async-start | bytes 491520 | tf_op jit(solution)/shard_map/psum | solution.py:67
  745.8 22.9 %collective-permute-start.1 = (bf16[1,160,768]{2,1,0:T(8,128)(2,1)}, bf16[1,160,768]{2,1,0:T(8,128)(2,1)S(1)}, u32[]{:S(2)}, u32[]{:S(2)}) collective-permute-start(bf16[1,160,768]{2,1,0:T(8,128)(2,1)} %get-tuple-element.121), channel_id=1, source_target_pairs={{64,0},{80,16},{96,32},{112,48},{65,1},{81,17},{97,33},{113,49},{6... | collective-permute-start | bytes 737288 | tf_op jit(solution)/shard_map/ppermute | solution.py:20
  764.9 149.0 %all-reduce.41.cloned.1.call-start = ((), (), s32[]{:S(2)}) async-start(), calls=%async_computation.18 | async-start | bytes 491520 | tf_op jit(solution)/shard_map/psum | solution.py:168
  868.9 70.7 %reduce-scatter.21.cloned.1.call-start = ((), (), s32[]{:S(2)}) async-start(), calls=%async_computation.20 | async-start | bytes 409600 | tf_op jit(solution)/shard_map/reduce_scatter | solution.py:215
  919.4 41.1 %reduce-scatter.19.cloned.1.call-start = ((), (), s32[]{:S(2)}) async-start(), calls=%async_computation.19 | async-start | bytes 409600 | tf_op jit(solution)/shard_map/reduce_scatter | solution.py:209
  922.9 82.0 %all-reduce.51.cloned.1.call-start = ((), (), s32[]{:S(2)}) async-start(), calls=%async_computation.28 | async-start | bytes 983040 | tf_op jit(solution)/shard_map/psum | solution.py:67
  963.2 152.8 %all-reduce.43.cloned.1.call-start = ((), (), s32[]{:S(2)}) async-start(), calls=%async_computation.21 | async-start | bytes 491520 | tf_op jit(solution)/shard_map/psum | solution.py:168
  1069.5 74.6 %reduce-scatter.25.cloned.1.call-start = ((), (), s32[]{:S(2)}) async-start(), calls=%async_computation.23 | async-start | bytes 409600 | tf_op jit(solution)/shard_map/reduce_scatter | solution.py:215
  1123.8 41.2 %reduce-scatter.23.cloned.1.call-start = ((), (), s32[]{:S(2)}) async-start(), calls=%async_computation.22 | async-start | bytes 409600 | tf_op jit(solution)/shard_map/reduce_scatter | solution.py:209
  1126.5 118.1 %all-reduce.49.cloned.1.call-start = ((), (), s32[]{:S(2)}) async-start(), calls=%async_computation.27 | async-start | bytes 983040 | tf_op jit(solution)/shard_map/psum | solution.py:231
  1167.8 206.9 %all-reduce.47.cloned.1.call-start = ((), (), s32[]{:S(2)}) async-start(), calls=%async_computation.26 | async-start | bytes 25165824
  1177.6 270.3 %reduce-scatter.27.cloned.1.call-start = ((), (), s32[]{:S(2)}) async-start(), calls=%async_computation.25 | async-start | bytes 9732096
  (161 other events, 2811.2 us)
Sparse Core Ops, SparseCore 0:
  10.4 47.9 all-gather.15
  112.6 38.5 all-reduce.28
  153.9 57.6 all-gather.17
  214.2 54.8 all-gather.19
  279.5 38.5 all-reduce.30
  348.0 39.7 all-reduce.32
  454.8 42.3 all-reduce.34
  503.7 20.0 reduce-scatter.16
  526.8 18.4 reduce-scatter.14
  548.1 41.3 all-reduce.52
  611.5 42.1 all-reduce.36
  683.7 39.7 all-reduce.44
  765.0 40.2 all-reduce.38
  869.0 44.8 all-reduce.40
  919.5 20.0 reduce-scatter.20
  942.0 18.4 reduce-scatter.18
  963.5 41.3 all-reduce.50
  1069.6 46.3 all-reduce.42
  1123.9 20.0 reduce-scatter.24
  1146.4 18.5 reduce-scatter.22
  1168.1 41.3 all-reduce.48
  1213.2 137.0 all-reduce.46
  1354.5 93.3 reduce-scatter.26
where the time goes:
time: 1470 us; the launch traced here: 1460 us
  waiting for transfers between devices  645 us (44%)
  blocking collectives  349 us (24%)
  matrix products  175 us (12%)
  local copies, waits for them, and re-layouts  166 us (11%)
  other arithmetic  88.9 us (6%)
  between operations  18 us (1%)
    psum x6, waiting for transfers between devices, layer_forward(): lax.psum(jnp.dot(mixed_heads, w_out, preferred_element_type=jnp.float32)....  190 us
    unnamed x1, blocking collectives  124 us
    psum x3, waiting for transfers between devices, layer_backward(): lax.psum(rows_part.astype(jnp.bfloat16), 'tp').astype(jnp.float32)  104 us
    psum x2, waiting for transfers between devices, layer_forward(): lax.psum(expert_local.astype(jnp.bfloat16), 'tp').astype(jnp.float32)  74.3 us
    unnamed x25, waiting for transfers between devices  70.5 us
    reduce_scatter x3, waiting for transfers between devices, layer_backward(): lax.psum_scatter(grad_keys_part.reshape(images, -1, head_count * HD).asty...  63.4 us
    all_gather x1, waiting for transfers between devices, shards(): lax.all_gather(w_in, ('section', 'ctx'), axis=2, tiled=True)  56.2 us
    all_gather x1, waiting for transfers between devices, shards(): lax.all_gather(w_exp_out, ('section', 'ctx'), axis=3, tiled=True)  53.1 us
  transfers between devices with their start and end apart: 27, of which 22 were waited for; matrix products, arithmetic and copies ran while one was open for 15% of the time, Pallas kernels for 0%

commit v1 on v0

v1 whole, which is shorter than its diff:
```python
import functools

import jax
import jax.numpy as jnp
from jax import lax
from jax.experimental import pallas as pl
from jax.experimental.pallas import tpu as pltpu
from jax.sharding import Mesh
from jax.sharding import PartitionSpec as P

D = 768
HD = 64
HEADS = 3
ROWS = 160
PAIR = 320
KEYS = 640
FE = 384
EXPERTS = 4
EPS = 1e-06
MESH = pl.DeviceIdType.MESH
CHIPS = ("x", "zh", "zl")
f32, bf16 = jnp.float32, jnp.bfloat16
VMEM = pl.BlockSpec(memory_space=pltpu.VMEM)
SMEM = pl.BlockSpec(memory_space=pltpu.SMEM)
NN = (((1,), (0,)), ((), ()))
NT = (((1,), (1,)), ((), ()))
TN = (((0,), (0,)), ((), ()))


def dot(a, b, dims):
    return lax.dot_general(a, b, dims, preferred_element_type=f32)


def dot_exact(a, b, dims):
    return lax.dot_general(
        a, b, dims, preferred_element_type=f32, precision=lax.Precision.HIGHEST
    )


def enter(peers):
    barrier = pltpu.get_barrier_semaphore()
    for peer in peers:
        pl.semaphore_signal(barrier, inc=1, device_id=peer, device_id_type=MESH)
    pl.semaphore_wait(barrier, len(peers))


def remote(src, dst, send, recv, peer):
    return pltpu.make_async_remote_copy(
        src_ref=src, dst_ref=dst, send_sem=send, recv_sem=recv, device_id=peer, device_id_type=MESH
    )


def comm_params(cid):
    return pltpu.CompilerParams(
        collective_id=cid, has_side_effects=True, vmem_limit_bytes=40 * 2**20
    )


def reduce_kernel(both, part, out, landed, rs_send, rs_recv, ag_send, ag_recv, cx_send, cx_recv):
    core, tp = lax.axis_index("core"), lax.axis_index("tp")
    other = 1 - core
    offsets = [(k // 4, k % 4) for k in range(1, 8 if both else 4)]
    peers = [{"core": (core + dc) % 2, "tp": (tp + dt) % 4} for dc, dt in offsets]
    enter(peers if both else peers + [{"core": other}])
    sends = []
    for k, peer in enumerate(peers):
        block = peer["core"] if both else 0
        copy = remote(
            part.at[block, peer["tp"]], landed.at[k], rs_send.at[k], rs_recv.at[k], peer
        )
        copy.start()
        sends.append(copy)
    total = part[core if both else 0, tp].astype(f32)
    for k, copy in enumerate(sends):
        copy.wait_recv()
        total = total + landed[k].astype(f32)
    out[core, tp] = total.astype(bf16)
    gathers = []
    for k in range(3):
        peer = {"tp": (tp + k + 1) % 4}
        copy = remote(out.at[core, tp], out.at[core, tp], ag_send.at[k], ag_recv.at[k], peer)
        copy.start()
        gathers.append(copy)
    crosses = []
    for k in range(4):
        at = (tp + 4 - k) % 4
        if k > 0:
            gathers[k - 1].wait_recv()
        copy = remote(
            out.at[core, at], out.at[core, at], cx_send.at[k], cx_recv.at[k], {"core": other}
        )
        copy.start()
        crosses.append(copy)
    for copy in crosses:
        copy.wait()
    for copy in sends + gathers:
        copy.wait_send()


def reduce_rows(part, cid):
    blocks, _, rows, cols = part.shape
    both = blocks == 2
    count = 7 if both else 3
    return pl.pallas_call(
        functools.partial(reduce_kernel, both),
        out_shape=jax.ShapeDtypeStruct((2, 4, rows, cols), bf16),
        in_specs=[VMEM],
        out_specs=VMEM,
        scratch_shapes=[pltpu.VMEM((count, rows, cols), bf16)]
        + [pltpu.SemaphoreType.DMA((count,))] * 2
        + [pltpu.SemaphoreType.DMA((3,))] * 2
        + [pltpu.SemaphoreType.DMA((4,))] * 2,
        compiler_params=comm_params(cid),
        name="reduce_rows",
    )(part)


def ctx_peers():
    core, zl = lax.axis_index("core"), lax.axis_index("zl")
    return [
        {"zl": (zl + k // 2) % 2, "core": (core + k % 2) % 2} for k in range(1, 4)
    ], zl * 2 + core


def kv_kernel(kv, out, send, recv):
    peers, me = ctx_peers()
    enter(peers)
    copies = []
    for k, peer in enumerate(peers):
        copy = remote(kv, out.at[me], send.at[k], recv.at[k], peer)
        copy.start()
        copies.append(copy)
    out[me] = kv[...]
    for copy in copies:
        copy.wait()


def gather_kv(kv):
    return pl.pallas_call(
        kv_kernel,
        out_shape=jax.ShapeDtypeStruct((4, ROWS, 2 * HEADS * HD), bf16),
        in_specs=[VMEM],
        out_specs=VMEM,
        scratch_shapes=[pltpu.SemaphoreType.DMA((3,))] * 2,
        compiler_params=comm_params(5),
        name="gather_kv",
    )(kv)


def kv_sum_kernel(part, out, landed, send, recv):
    peers, me = ctx_peers()
    enter(peers)
    copies = []
    for k, peer in enumerate(peers):
        at = peer["zl"] * 2 + peer["core"]
        copy = remote(part.at[at], landed.at[k], send.at[k], recv.at[k], peer)
        copy.start()
        copies.append(copy)
    total = part[me].astype(f32)
    for k, copy in enumerate(copies):
        copy.wait_recv()
        total = total + landed[k].astype(f32)
    out[...] = total.astype(bf16)
    for copy in copies:
        copy.wait_send()


def scatter_kv(part):
    return pl.pallas_call(
        kv_sum_kernel,
        out_shape=jax.ShapeDtypeStruct((ROWS, 2 * HEADS * HD), bf16),
        in_specs=[VMEM],
        out_specs=VMEM,
        scratch_shapes=[pltpu.VMEM((3, ROWS, 2 * HEADS * HD), bf16)]
        + [pltpu.SemaphoreType.DMA((3,))] * 2,
        compiler_params=comm_params(6),
        name="scatter_kv",
    )(part)


def start_kernel(images, weights, out_images, out_weights, send, recv):
    core, x = lax.axis_index("core"), lax.axis_index("x")
    high = x // 2
    partner, other = {"x": (x + 2) % 4}, {"core": 1 - core}
    enter([partner, other])
    swap = remote(
        images.at[1 - high], out_images.at[core, high], send.at[0], recv.at[0], partner
    )
    swap.start()
    cross = remote(weights, out_weights, send.at[1], recv.at[1], other)
    cross.start()
    kept = remote(images.at[high], out_images.at[core, high], send.at[2], recv.at[2], other)
    kept.start()
    out_images[core, high] = images[high]
    swap.wait_recv()
    passed = remote(
        out_images.at[core, 1 - high],
        out_images.at[core, 1 - high],
        send.at[3],
        recv.at[3],
        other,
    )
    passed.start()
    for copy in (cross, kept, passed):
        copy.wait()
    swap.wait_send()


def start_exchange(images, weights):
    return pl.pallas_call(
        start_kernel,
        out_shape=(
            jax.ShapeDtypeStruct((2,) + images.shape, bf16),
            jax.ShapeDtypeStruct(weights.shape, bf16),
        ),
        in_specs=[VMEM, VMEM],
        out_specs=(VMEM, VMEM),
        scratch_shapes=[pltpu.SemaphoreType.DMA((4,))] * 2,
        compiler_params=comm_params(0),
        name="start_exchange",
    )(images, weights)


def chip_peer(k):
    x, zh, zl = (lax.axis_index(a) for a in CHIPS)
    dx, dh, dl = k // 4, (k // 2) % 2, k % 2
    ahead = ((x + dx) % 4, (zh + dh) % 2, (zl + dl) % 2)
    back = ((x + 4 - dx) % 4, (zh + 2 - dh) % 2, (zl + 2 - dl) % 2)
    return dict(zip(CHIPS, ahead)), *(c[0] * 4 + c[1] * 2 + c[2] for c in (ahead, back))


def gather_kernel(own, out, send, recv, cx_send, cx_recv):
    core = lax.axis_index("core")
    other = {"core": 1 - core}
    _, me, _ = chip_peer(0)
    enter([chip_peer(k)[0] for k in range(1, 16)] + [other])
    out[me, core] = own[...]

    def push(k):
        peer, _, _ = chip_peer(k)
        return remote(own, out.at[me, core], send.at[k], recv.at[k], peer)

    def cross(k):
        _, _, at = chip_peer(k)
        return remote(out.at[at, core], out.at[at, core], cx_send.at[k], cx_recv.at[k], other)

    def first(k, carry):
        push(k).start()
        return carry

    def onward(k, carry):
        push(k).wait_recv()
        cross(k).start()
        return carry

    def last(k, carry):
        push(k).wait_send()
        cross(k).wait()
        return carry

    lax.fori_loop(1, 16, first, 0)
    cross(0).start()
    lax.fori_loop(1, 16, onward, 0)
    cross(0).wait()
    lax.fori_loop(1, 16, last, 0)


def gather_small(own):
    return pl.pallas_call(
        gather_kernel,
        out_shape=jax.ShapeDtypeStruct((16, 2) + own.shape, bf16),
        in_specs=[VMEM],
        out_specs=VMEM,
        scratch_shapes=[pltpu.SemaphoreType.DMA((16,))] * 4,
        compiler_params=comm_params(1),
        name="gather_small",
    )(own)


def scatter_kernel(part, out, landed, sums, pieces, cx, send, recv):
    core = lax.axis_index("core")
    other = {"core": 1 - core}
    _, me, _ = chip_peer(0)
    enter([chip_peer(k)[0] for k in range(1, 16)] + [other])
    cross = remote(part.at[1 - core], landed, cx.at[0], cx.at[1], other)
    cross.start()
    cross.wait()

    def push(k):
        peer, at, _ = chip_peer(k)
        return remote(sums.at[at], pieces.at[k], send.at[k], recv.at[k], peer)

    def add(k, carry):
        _, at, _ = chip_peer(k)
        sums[at] = (part[core, at].astype(f32) + landed[at].astype(f32)).astype(bf16)
        push(k).start()
        return carry

    def collect(k, carry):
        push(k).wait_recv()
        out[...] += pieces[k].astype(f32)
        return carry

    def last(k, carry):
        push(k).wait_send()
        return carry

    lax.fori_loop(1, 16, add, 0)
    out[...] = part[core, me].astype(f32) + landed[me].astype(f32)
    lax.fori_loop(1, 16, collect, 0)
    lax.fori_loop(1, 16, last, 0)


def scatter_small(part):
    shape = part.shape[2:]
    return pl.pallas_call(
        scatter_kernel,
        out_shape=jax.ShapeDtypeStruct(shape, f32),
        in_specs=[VMEM],
        out_specs=VMEM,
        scratch_shapes=[pltpu.VMEM((16,) + shape, bf16)] * 3
        + [pltpu.SemaphoreType.DMA((2,))]
        + [pltpu.SemaphoreType.DMA((16,))] * 2,
        compiler_params=comm_params(7),
        name="scatter_small",
    )(part)


def compute_params():
    return pltpu.CompilerParams(vmem_limit_bytes=56 * 2**20)


def block_rows(ref, block):
    top = jnp.concatenate([ref[block, 0, 0:80], ref[block, 1, 0:80]], axis=1)
    low = jnp.concatenate([ref[block, 2, 0:80], ref[block, 3, 0:80]], axis=1)
    return jnp.concatenate([top, low], axis=0).astype(f32)


def pair_rows(ref):
    return jnp.concatenate([block_rows(ref, 0), block_rows(ref, 1)], axis=0)


def chunks(value):
    return [
        value[80 * (j // 2) : 80 * (j // 2) + 80, 384 * (j % 2) : 384 * (j % 2) + 384]
        for j in range(4)
    ]


def norm_parts(rows):
    centered = rows - jnp.mean(rows, axis=-1, keepdims=True)
    scale = lax.rsqrt(jnp.mean(centered * centered, axis=-1, keepdims=True) + EPS)
    return centered * scale, scale


def norm_back(grad, unit, scale, gain):
    inner = grad * gain
    return scale * (
        inner
        - jnp.mean(inner, axis=-1, keepdims=True)
        - unit * jnp.mean(inner * unit, axis=-1, keepdims=True)
    )


def softmax(logits, axis):
    top = jnp.max(logits, axis=axis, keepdims=True)
    powers = jnp.exp(logits - top)
    return powers / jnp.sum(powers, axis=axis, keepdims=True)


def project(rows, small, w_qkv, q, kv):
    unit, _ = norm_parts(rows)
    normed = (unit * small[0:1] + small[2:3]).astype(bf16)
    out = dot(normed, w_qkv[...], NN).astype(bf16)
    q[...] = out[:, : HEADS * HD]
    kv[...] = out[:, HEADS * HD :]


def first_kernel(core, x, small, w_qkv, q, kv):
    rows = x[pl.ds(pl.multiple_of(core[0] * ROWS, ROWS), ROWS)].astype(f32)
    project(rows, small, w_qkv, q, kv)


def next_kernel(core, x, att, moe, small, w_qkv, q, kv, x_next):
    x_next[...] = (x[...].astype(f32) + pair_rows(att) + pair_rows(moe)).astype(bf16)
    rows = x_next[pl.ds(pl.multiple_of(core[0] * ROWS, ROWS), ROWS)].astype(f32)
    project(rows, small, w_qkv, q, kv)


def call(kernel, out_shapes, *args, name):
    return pl.pallas_call(
        kernel,
        out_shape=[jax.ShapeDtypeStruct(s, t) for s, t in out_shapes],
        in_specs=[SMEM if a.dtype == jnp.int32 else VMEM for a in args],
        out_specs=[VMEM] * len(out_shapes),
        compiler_params=compute_params(),
        name=name,
    )(*args)


def head(value, h):
    return value[:, HD * h : HD * h + HD]


def attend_kernel(q, kv, dead, w_out_t, part, mixed):
    width = HEADS * HD
    keys = kv[...].reshape(KEYS, 2 * width)
    queries = q[...]
    outs = []
    for h in range(HEADS):
        scores = HD**-0.5 * dot(head(queries, h), head(keys, h), NT) + dead[...]
        probs = softmax(scores, -1).astype(bf16)
        outs.append(dot(probs, head(keys, HEADS + h), NN))
    mixed[...] = jnp.concatenate(outs, axis=1).astype(bf16)
    value = dot(mixed[...], w_out_t[...], NT).astype(bf16)
    for j, chunk in enumerate(chunks(value)):
        part[0, j] = chunk


def gelu_parts(u):
    c = 0.7978845608028654
    t = jnp.tanh(c * (u + 0.044715 * u * u * u))
    return 0.5 * u * (1.0 + t), t


def gelu_slope(u, t):
    c = 0.7978845608028654
    return 0.5 * (1.0 + t) + 0.5 * u * (1.0 - t * t) * (c * (1.0 + 3 * 0.044715 * u * u))


def expert_weights(weights):
    block = weights[...]
    return block[:, 0].reshape(D, FE), block[:, 1].reshape(D, FE)


def experts_setup(x, att, small, routes, b, gates):
    unit, _ = norm_parts(x[...].astype(f32) + pair_rows(att))
    b[...] = (unit * small[1:2] + small[3:4]).astype(bf16)
    probs = softmax(dot(b[...], small[4:8].astype(bf16), NT), -1)
    ids = lax.broadcasted_iota(jnp.int32, (PAIR, EXPERTS), 1).astype(f32)
    named = (routes[:, 0:1] == ids) | (routes[:, 1:2] == ids)
    gates[...] = jnp.where(named, probs, 0.0)


def gate_of(gates, expert):
    ids = lax.broadcasted_iota(jnp.int32, (PAIR, EXPERTS), 1)
    return jnp.sum(jnp.where(ids == expert, gates[...], 0.0), axis=1, keepdims=True)


def experts_kernel(x, att, small, routes, weights, part, b, gates, total):
    expert = pl.program_id(0)

    @pl.when(expert == 0)
    def _():
        experts_setup(x, att, small, routes, b, gates)
        total[...] = jnp.zeros_like(total)

    w_in, w_out_t = expert_weights(weights)
    u = dot(b[...], w_in, NN)
    active = gelu_parts(u)[0].astype(bf16).astype(f32)
    gated = (gate_of(gates, expert) * active).astype(bf16)
    total[...] += dot(gated, w_out_t, NT)

    @pl.when(expert == EXPERTS - 1)
    def _():
        for block in range(2):
            value = total[ROWS * block : ROWS * block + ROWS].astype(bf16)
            for j, chunk in enumerate(chunks(value)):
                part[block, j] = chunk


def experts_back_kernel(
    with_moe, x, att, small, routes, grad, weights, part, grad_w, b, gates, total, moe, gate_t
):
    expert = pl.program_id(0)

    @pl.when(expert == 0)
    def _():
        experts_setup(x, att, small, routes, b, gates)
        total[...] = jnp.zeros_like(total)
        if with_moe:
            moe[...] = jnp.zeros_like(moe)

    w_in, w_out_t = expert_weights(weights)
    u = dot(b[...], w_in, NN)
    act, t = gelu_parts(u)
    active = act.astype(bf16).astype(f32)
    gate = gate_of(gates, expert)
    gated = (gate * active).astype(bf16)
    if with_moe:
        moe[...] += dot(gated, w_out_t, NT)
    back = dot(grad[...], w_out_t, NN)
    ones = jnp.ones((8, FE), f32)
    gate_t[expert] = dot_exact(ones, back * active, NT)
    grad_u = (gate * back * gelu_slope(u, t)).astype(bf16)
    total[...] += dot(grad_u, w_in, NT)
    grad_w[:, 0] = dot(b[...], grad_u, TN).astype(bf16).reshape(16, 48, FE)
    grad_w[:, 1] = dot(grad[...], gated, TN).astype(bf16).reshape(16, 48, FE)

    @pl.when(expert == EXPERTS - 1)
    def _():
        part[...] = jnp.zeros_like(part)
        for block in range(2):
            value = total[ROWS * block : ROWS * block + ROWS].astype(bf16)
            for j, chunk in enumerate(chunks(value)):
                part[block, j, 0:80] = chunk
            table = jnp.concatenate(
                [gate_t[e, 0:1, ROWS * block : ROWS * block + ROWS] for e in range(EXPERTS)]
                + [jnp.zeros((12, ROWS), f32)],
                axis=0,
            )
            part[block, 0, 80:96, 0:ROWS] = table.astype(bf16)
            if with_moe:
                value = moe[ROWS * block : ROWS * block + ROWS].astype(bf16)
                for j, chunk in enumerate(chunks(value)):
                    part[block, j, 96:176] = chunk


def fixed(shape):
    return pl.BlockSpec(shape, lambda e: (0,) * len(shape))


EXPERT_BLOCK = pl.BlockSpec((16, 2, 48, FE), lambda e: (0, e, 0, 0))


def experts_forward(x, att, small, routes, weights):
    args = (x, att, small, routes)
    return pl.pallas_call(
        experts_kernel,
        grid=(EXPERTS,),
        out_shape=jax.ShapeDtypeStruct((2, 4, 80, 384), bf16),
        in_specs=[fixed(a.shape) for a in args] + [EXPERT_BLOCK],
        out_specs=fixed((2, 4, 80, 384)),
        scratch_shapes=[
            pltpu.VMEM((PAIR, D), bf16),
            pltpu.VMEM((PAIR, EXPERTS), f32),
            pltpu.VMEM((PAIR, D), f32),
        ],
        compiler_params=compute_params(),
        name="experts_forward",
    )(*args, weights)


def experts_backward(x, att, small, routes, grad, weights, with_moe):
    args = (x, att, small, routes, grad)
    rows = 176 if with_moe else 96
    return pl.pallas_call(
        functools.partial(experts_back_kernel, with_moe),
        grid=(EXPERTS,),
        out_shape=[
            jax.ShapeDtypeStruct((2, 4, rows, 384), bf16),
            jax.ShapeDtypeStruct((16, 2 * EXPERTS, 48, FE), bf16),
        ],
        in_specs=[fixed(a.shape) for a in args] + [EXPERT_BLOCK],
        out_specs=[fixed((2, 4, rows, 384)), EXPERT_BLOCK],
        scratch_shapes=[
            pltpu.VMEM((PAIR, D), bf16),
            pltpu.VMEM((PAIR, EXPERTS), f32),
            pltpu.VMEM((PAIR, D), f32),
            pltpu.VMEM((PAIR, D), f32),
            pltpu.VMEM((EXPERTS, 8, PAIR), f32),
        ],
        compiler_params=compute_params(),
        name="experts_backward",
    )(*args, weights)


def attend_back_kernel(
    core, x, att, small, routes_t, grad, back, q, kv, mixed, dead, w_out_t,
    grad_h, grad_q, grad_kv, grad_w_out, grad_small,
):
    unit, scale = norm_parts(x[...].astype(f32) + pair_rows(att))
    b = (unit * small[1:2] + small[3:4]).astype(bf16)
    router = small[4:8]
    probs = softmax(dot(router.astype(bf16), b, NT), 0)
    ids = lax.broadcasted_iota(jnp.int32, (EXPERTS, PAIR), 0).astype(f32)
    named = (routes_t[0:1] == ids) | (routes_t[1:2] == ids)
    tables = [back[block, 0, 80:96, 0:ROWS].astype(f32)[0:EXPERTS] for block in range(2)]
    gate_grads = jnp.where(named, jnp.concatenate(tables, axis=1), 0.0)
    grad_logits = probs * (gate_grads - jnp.sum(probs * gate_grads, axis=0, keepdims=True))
    grad_b = pair_rows(back) + dot_exact(grad_logits, router, TN)
    grad_h[...] = grad[...].astype(f32) + norm_back(grad_b, unit, scale, small[1:2])
    first = core[0] == 0
    lanes = lax.broadcasted_iota(jnp.int32, (EXPERTS, PAIR), 1)
    own_t = (lanes < ROWS) == first
    lines = lax.broadcasted_iota(jnp.int32, (PAIR, 1), 0)
    own = (lines < ROWS) == first
    kept = jnp.where(own, grad_b, 0.0)
    grad_small[0:1] = jnp.sum(kept * unit, axis=0, keepdims=True)
    grad_small[1:2] = jnp.sum(kept, axis=0, keepdims=True)
    grad_small[2:4] = jnp.zeros((2, D), f32)
    grad_small[4:8] = dot_exact(jnp.where(own_t, grad_logits, 0.0), b.astype(f32), NN)
    at = pl.ds(pl.multiple_of(core[0] * ROWS, ROWS), ROWS)
    grad_att = grad_h[at].astype(bf16)
    grad_w_out[...] = dot(grad_att, mixed[...], TN).astype(bf16)
    grad_mixed = dot(grad_att, w_out_t[...], NN).astype(bf16)
    width = HEADS * HD
    keys = kv[...].reshape(KEYS, 2 * width)
    queries = q[...]
    q_parts, k_parts, v_parts = [], [], []
    for h in range(HEADS):
        q_h, k_h, v_h, g_h = head(queries, h), head(keys, h), head(keys, HEADS + h), head(grad_mixed, h)
        weights = softmax(HD**-0.5 * dot(q_h, k_h, NT) + dead[...], -1)
        v_parts.append(dot(weights.astype(bf16), g_h, TN))
        grad_weights = dot(g_h, v_h, NT)
        grad_scores = weights * (
            grad_weights - jnp.sum(weights * grad_weights, axis=-1, keepdims=True)
        )
        grad_scores = grad_scores.astype(bf16)
        q_parts.append(HD**-0.5 * dot(grad_scores, k_h, NN))
        k_parts.append(HD**-0.5 * dot(grad_scores, q_h, TN))
    grad_q[...] = jnp.concatenate(q_parts, axis=1).astype(bf16)
    total = jnp.concatenate(k_parts + v_parts, axis=1).astype(bf16)
    grad_kv[...] = total.reshape(4, ROWS, 2 * width)


def project_back_kernel(core, x, small, grad_q, grad_kv, w_qkv, part, grad_w):
    rows = x[pl.ds(pl.multiple_of(core[0] * ROWS, ROWS), ROWS)].astype(f32)
    unit, _ = norm_parts(rows)
    normed = (unit * small[0:1] + small[2:3]).astype(bf16)
    grads = jnp.concatenate([grad_q[...], grad_kv[...]], axis=1)
    grad_w[...] = dot(normed, grads, TN).astype(bf16)
    value = dot(grads, w_qkv[...], NT).astype(bf16)
    for j, chunk in enumerate(chunks(value)):
        part[0, j] = chunk


def tokens_back_kernel(core, x, small, grad_h, back, grad_x, grad_small):
    unit, scale = norm_parts(x[...].astype(f32))
    grad_a = pair_rows(back)
    grad_x[...] = (grad_h[...] + norm_back(grad_a, unit, scale, small[0:1])).astype(bf16)
    lines = lax.broadcasted_iota(jnp.int32, (PAIR, 1), 0)
    own = (lines < ROWS) == (core[0] == 0)
    kept = jnp.where(own, grad_a, 0.0)
    grad_small[0:1] = jnp.sum(kept * unit, axis=0, keepdims=True)
    grad_small[1:2] = jnp.sum(kept, axis=0, keepdims=True)
    grad_small[2:8] = jnp.zeros((6, D), f32)


def layer_back(core, x, att, small, routes, grad, saved, dead, w_qkv, w_out_t, weights, with_moe, cid):
    q, kv, mixed = saved
    part, grad_experts = experts_backward(x, att, small, routes, grad, weights, with_moe)
    back = reduce_rows(part, cid)
    grad_h, grad_q, grad_kv, grad_w_out, small_two = call(
        attend_back_kernel,
        [
            ((PAIR, D), f32),
            ((ROWS, 192), bf16),
            ((4, ROWS, 384), bf16),
            ((D, 192), bf16),
            ((8, D), f32),
        ],
        core, x, att, small, routes.T, grad, back, q, kv, mixed, dead, w_out_t,
        name="attend_back",
    )
    grad_kv = scatter_kv(grad_kv)
    part, grad_w_qkv = call(
        project_back_kernel,
        [((1, 4, 80, 384), bf16), ((D, 576), bf16)],
        core, x, small, grad_q, grad_kv, w_qkv,
        name="project_back",
    )
    back_one = reduce_rows(part, 2)
    grad_x, small_one = call(
        tokens_back_kernel,
        [((PAIR, D), bf16), ((8, D), f32)],
        core, x, small, grad_h, back_one,
        name="tokens_back",
    )
    grad_small = jnp.stack(
        [small_one[0], small_two[0], small_one[1], small_two[1]], axis=0
    )
    grad_small = jnp.concatenate([grad_small, small_two[4:8]], axis=0)
    grad_attn = jnp.concatenate([grad_w_qkv, grad_w_out], axis=1).reshape(32, 24, D)
    grad_small = grad_small.reshape(8, 32, 24).transpose(1, 0, 2).astype(bf16)
    grad_small = jnp.pad(grad_small, ((0, 0), (0, 0), (0, D - 24)))
    grad_pack = jnp.concatenate([grad_attn, grad_small], axis=1)
    return grad_x, grad_experts, grad_pack, back


def shards(boundary, routes, lengths, ln_gains, ln_biases, w_qkv, w_out, w_router, w_in, w_exp_out):
    core = lax.axis_index("core")
    high = lax.axis_index("x") // 2
    core_ref = core.astype(jnp.int32).reshape(1)

    turned = jnp.pad(
        routes[0].astype(bf16).transpose(0, 2, 1), ((0, 0), (0, 14), (0, D - ROWS))
    )
    images = jnp.concatenate([boundary[0], turned], axis=1)
    stacked = jnp.stack([w_in, w_exp_out.transpose(0, 1, 3, 2)], axis=2).reshape(384, 2, FE)
    own_half = lax.dynamic_index_in_dim(stacked, core, 1, keepdims=False)
    other_half = lax.dynamic_index_in_dim(stacked, 1 - core, 1, keepdims=False)
    got_images, got_half = start_exchange(images, other_half)
    low_half = jnp.where(core == 0, own_half, got_half).reshape(2, 8, 24, FE)
    high_half = jnp.where(core == 0, got_half, own_half).reshape(2, 8, 24, FE)
    chip_shard = jnp.concatenate([low_half, high_half], axis=2).reshape(2, 384, FE)
    experts = [
        lax.all_gather(chip_shard[layer], CHIPS, axis=0).reshape(16, 8, 48, FE)
        for layer in range(2)
    ]

    attn = jnp.concatenate([w_qkv.reshape(2, 24, 576), w_out.transpose(0, 2, 1)], axis=2)
    tiny = jnp.concatenate([ln_gains, ln_biases, w_router.transpose(0, 2, 1)], axis=1)
    tiny = jnp.pad(tiny, ((0, 0), (0, 0), (0, D - 24)))
    pack = jnp.concatenate([attn, tiny], axis=1).reshape(64, D)
    packs = gather_small(pack).reshape(32, 2, 32, D)
    w_qkvs, w_outs, smalls = [], [], []
    for layer in range(2):
        both = packs[:, layer, 0:24].reshape(D, D)
        w_qkvs.append(both[:, :576])
        w_outs.append(both[:, 576:])
        smalls.append(
            packs[:, layer, 24:32, 0:24].transpose(1, 0, 2).reshape(8, D).astype(f32)
        )

    live = jnp.arange(ROWS, dtype=jnp.int32)[None, :] < lengths[:, None]
    dead = jnp.where(live.reshape(1, KEYS), 0.0, -1e30).astype(f32)
    chip_live = lax.dynamic_slice_in_dim(live, 2 * lax.axis_index("zl"), 2, 0)
    own_live = lax.dynamic_index_in_dim(chip_live, core, 0, keepdims=False)

    x0 = got_images[:, 0, 0:ROWS].reshape(PAIR, D)
    cotangent = jnp.where(chip_live[:, :, None], got_images[:, 1, 0:ROWS], 0).reshape(PAIR, D)
    route_cols = [
        got_images[:, kind, ROWS : ROWS + 2, 0:ROWS].transpose(0, 2, 1).reshape(PAIR, 2).astype(f32)
        for kind in range(2)
    ]

    q0, kv0 = call(
        first_kernel, [((ROWS, 192), bf16), ((ROWS, 384), bf16)],
        core_ref, x0, smalls[0], w_qkvs[0], name="first_project",
    )
    kv0 = gather_kv(kv0)
    part, mixed0 = call(
        attend_kernel, [((1, 4, 80, 384), bf16), ((ROWS, 192), bf16)],
        q0, kv0, dead, w_outs[0], name="attend",
    )
    att0 = reduce_rows(part, 2)
    part = experts_forward(x0, att0, smalls[0], route_cols[0], experts[0])
    moe0 = reduce_rows(part, 3)

    q1, kv1, x1 = call(
        next_kernel, [((ROWS, 192), bf16), ((ROWS, 384), bf16), ((PAIR, D), bf16)],
        core_ref, x0, att0, moe0, smalls[1], w_qkvs[1], name="next_project",
    )
    kv1 = gather_kv(kv1)
    part, mixed1 = call(
        attend_kernel, [((1, 4, 80, 384), bf16), ((ROWS, 192), bf16)],
        q1, kv1, dead, w_outs[1], name="attend",
    )
    att1 = reduce_rows(part, 2)

    grad_x1, grad_experts1, grad_pack1, back1 = layer_back(
        core_ref, x1, att1, smalls[1], route_cols[1], cotangent, (q1, kv1, mixed1), dead,
        w_qkvs[1], w_outs[1], experts[1], True, 4,
    )
    grad_x0, grad_experts0, grad_pack0, _ = layer_back(
        core_ref, x0, att0, smalls[0], route_cols[0], grad_x1, (q0, kv0, mixed0), dead,
        w_qkvs[0], w_outs[0], experts[0], False, 8,
    )

    def own_block(value):
        return lax.dynamic_index_in_dim(value, core, 0, keepdims=False)

    def unchunk(value):
        return value.reshape(2, 2, 80, 384).transpose(0, 2, 1, 3).reshape(ROWS, D).astype(f32)

    y1 = (
        own_block(x1.reshape(2, ROWS, D)).astype(f32)
        + unchunk(own_block(att1))
        + unchunk(own_block(back1)[:, 96:176])
    )
    mine = jnp.stack([own_block(grad_x0.reshape(2, ROWS, D)).astype(f32), y1])
    mine = jnp.where(own_live[None, :, None], mine, 0.0)
    kept = lax.dynamic_index_in_dim(mine, high, 0, keepdims=False)
    sent = lax.dynamic_index_in_dim(mine, 1 - high, 0, keepdims=False).astype(bf16)
    landed = lax.ppermute(sent, "x", [(i, (i + 2) % 4) for i in range(4)]).astype(f32)
    ends = jnp.where(high == 0, jnp.stack([kept, landed]), jnp.stack([landed, kept]))

    sums = [
        lax.psum_scatter(g.reshape(16, 384, FE), CHIPS, scatter_dimension=0)
        for g in (grad_experts0, grad_experts1)
    ]
    sums = jnp.stack(sums).reshape(16, 2, 24, FE)
    own_sum = lax.dynamic_index_in_dim(sums, core, 1, keepdims=False)
    other_sum = lax.dynamic_index_in_dim(sums, 1 - core, 1, keepdims=False).reshape(384, FE)
    got_sum = lax.ppermute(other_sum, "core", [(0, 1), (1, 0)]).reshape(16, 24, FE)
    first = jnp.where(core == 0, own_sum, got_sum)
    second = jnp.where(core == 0, got_sum, own_sum)
    full = jnp.concatenate([first, second], axis=2).reshape(2, EXPERTS, 2, 24, D).astype(f32)
    grad_w_in = full[:, :, 0]
    grad_w_exp_out = full[:, :, 1].transpose(0, 1, 3, 2)

    packs = jnp.stack([grad_pack0, grad_pack1], axis=1).reshape(16, 2, 64, D)
    own = scatter_small(packs.transpose(1, 0, 2, 3)).reshape(2, 32, D)
    grad_w_qkv = own[:, 0:24, :576].reshape(2, 24, 3, 192)
    grad_w_out = own[:, 0:24, 576:].transpose(0, 2, 1)
    tiny = own[:, 24:32, 0:24]
    return (
        ends[None],
        tiny[:, 0:2],
        tiny[:, 2:4],
        grad_w_qkv,
        grad_w_out,
        tiny[:, 4:8].transpose(0, 2, 1),
        grad_w_in,
        grad_w_exp_out,
    )


def solution(mesh):
    fine = Mesh(mesh.devices.reshape(4, 2, 2, 2, 4), CHIPS + ("core", "tp"))
    section, ctx = ("x", "zh"), ("zl", "core")
    every = section + ctx
    return jax.shard_map(
        shards,
        mesh=fine,
        in_specs=(
            P(ctx, section, None, None),
            P(ctx, section, None, None),
            P(),
            P(None, None, every),
            P(None, None, every),
            P(None, every, None, "tp"),
            P(None, "tp", every),
            P(None, every, None),
            P(None, None, every, "tp"),
            P(None, None, "tp", every),
        ),
        out_specs=(
            P(ctx, section, None, None),
            P(None, None, every),
            P(None, None, every),
            P(None, every, None, "tp"),
            P(None, "tp", every),
            P(None, every, None),
            P(None, None, every, "tp"),
            P(None, None, "tp", every),
        ),
        check_vma=False,
    )
```

time: 1470 us -> 451 us (0.31)
  waiting for transfers between devices: 645 us -> 58.8 us
  blocking collectives: 349 us -> 0 us
  Pallas kernels: 0 us -> 321 us
  matrix products: 175 us -> 0 us
  local copies, waits for them, and re-layouts: 166 us -> 37.4 us
  other arithmetic: 88.9 us -> 7.77 us
    psum x12 -> x0, waiting for transfers between devices: 368 us -> none  [the longest x6 190 us: layer_forward(): lax.psum(jnp.dot(mixed_heads, w_out, preferred_element_type=jnp.float32)....]
    pallas_call x0 -> x27, Pallas kernels: none -> 321 us  [the longest x7 114 us: reduce_rows(): pl.pallas_call(functools.partial(reduce_kernel, both), out_shape=jax.Shap...]
    all_gather x16 -> x0, blocking collectives: 186 us -> none  [the longest x6 49.5 us: layer_forward(): lax.all_gather(projected[:, :, 1], 'ctx', axis=1, tiled=True)]
    dot_general x85 -> x0, matrix products: 168 us -> none  [the longest x6 26 us: layer_forward(): jnp.einsum('ecf,efd->ecd', active, w_exp_out, preferred_element_type=jnp....]
    unnamed x1 -> x0, blocking collectives: 124 us -> none
    all_gather x3 -> x2, waiting for transfers between devices: 109 us -> 0.01 us  [shards(): lax.all_gather(chip_shard[layer], CHIPS, axis=0).reshape(16, 8, 48, FE)]
    reduce_scatter x6 -> x0, waiting for transfers between devices: 94.8 us -> none  [the longest x3 63.4 us: layer_backward(): lax.psum_scatter(grad_keys_part.reshape(images, -1, head_count * HD).asty...]
    reduce_sum x51 -> x0, other arithmetic: 43.5 us -> none  [the longest x3 7.98 us: layer_forward(): expert_local = jnp.sum(gate_values[:, :, None] * picked, axis=1)]
  transfers between devices with their start and end apart: 27 -> 6, of which waited for: 22 -> 2; matrix products, arithmetic and copies ran while one was open for 15% -> 4% of each run, Pallas kernels for 0% -> 49%
where the time goes in v1:
time: 451 us; the launch traced here: 447 us
  Pallas kernels  321 us (71%)
  waiting for transfers between devices  58.8 us (13%)
  local copies, waits for them, and re-layouts  37.4 us (8%)
  between operations  15 us (3%)
  other arithmetic  7.77 us (2%)
  starting transfers between devices  7.52 us (2%)
    pallas_call x7, Pallas kernels, reduce_rows(): pl.pallas_call(functools.partial(reduce_kernel, both), out_shape=jax.Shap...  114 us
    unnamed x6, waiting for transfers between devices  58.6 us
    pallas_call x10, Pallas kernels, call(): pl.pallas_call(kernel, out_shape=[jax.ShapeDtypeStruct(s, t) for s, t in...  41.8 us
    pallas_call x1, Pallas kernels, gather_small(): pl.pallas_call(gather_kernel, out_shape=jax.ShapeDtypeStruct((16, 2) + ow...  35.8 us
    pallas_call x1, Pallas kernels, scatter_small(): pl.pallas_call(scatter_kernel, out_shape=jax.ShapeDtypeStruct(shape, f32)...  33.7 us
    pallas_call x2, Pallas kernels, experts_backward(): pl.pallas_call(functools.partial(experts_back_kernel, with_moe), grid=(EX...  27.8 us
    pallas_call x2, Pallas kernels, gather_kv(): pl.pallas_call(kv_kernel, out_shape=jax.ShapeDtypeStruct((4, ROWS, 2 * HE...  27.6 us
    unnamed x91, local copies, waits for them, and re-layouts  21.5 us
  transfers between devices with their start and end apart: 6, of which 2 were waited for; matrix products, arithmetic and copies ran while one was open for 4% of the time, Pallas kernels for 49%

profile of v1, /device:TPU:1, one launch (start us, length us, event | category | flops | bytes accessed | tf_op | source)
XLA Modules:
  0.0 447.5 jit_solution(10768726606217990949)
XLA Ops:
  9.9 12.9 %start_exchange.1 = (bf16[2,2,176,768]{3,2,1,0:T(8,128)(2,1)S(1)}, bf16[384,384]{1,0:T(8,128)(2,1)S(1)}) custom-call(bf16[2,176,768]{2,1,0:T(8,128)(2,1)S(1)} %fusion.7.images, bf16[384,384]{1,0:T(8,128)(2,1)S(1)} %bitcast.119), custom_call_target="tpu_custom_call" | custom-call | tf_op jit(solution)/shard_map/start_exchange/pallas_call | solution.py:210
  25.1 35.8 %gather_small.1 = bf16[16,2,64,768]{3,2,1,0:T(8,128)(2,1)S(1)} custom-call(bf16[64,768]{1,0:T(8,128)(2,1)S(1)} %bitcast.124), custom_call_target="tpu_custom_call" | custom-call | tf_op jit(solution)/shard_map/gather_small/pallas_call | solution.py:269
  70.2 13.8 %gather_kv.2.kv = bf16[4,160,384]{2,1,0:T(8,128)(2,1)S(1)} custom-call(bf16[160,384]{1,0:T(8,128)(2,1)S(1)} %copy-done.23), custom_call_target="tpu_custom_call" | custom-call | tf_op jit(solution)/shard_map/gather_kv/pallas_call | solution.py:139
  85.5 3.6 attend.2
  90.1 15.0 %reduce_rows.7.att = bf16[2,4,80,384]{3,2,1,0:T(8,128)(2,1)S(1)} custom-call(bf16[1,4,80,384]{3,2,1,0:T(8,128)(2,1)S(1)} %copy-done.20), custom_call_target="tpu_custom_call" | custom-call | tf_op jit(solution)/shard_map/reduce_rows/pallas_call | solution.py:104
  109.6 7.0 %experts_forward.1.part = bf16[2,4,80,384]{3,2,1,0:T(8,128)(2,1)} custom-call(bf16[320,768]{1,0:T(8,128)(2,1)} %bitcast.126, bf16[2,4,80,384]{3,2,1,0:T(8,128)(2,1)} %copy-done, f32[8,768]{1,0:T(8,128)} %reshape.265.small, f32[320,2]{1,0:T(8,128)} %copy.68.routes, bf16[16,8,48,384]{3,2,1,0:T(8,128)(2,1)} %bitcast.132), custom_call_target="tpu_custom_call" | custom-call | tf_op jit(solution)/shard_map/experts_forward/pallas_call | solution.py:528
  117.7 15.7 %reduce_rows.8.moe = bf16[2,4,80,384]{3,2,1,0:T(8,128)(2,1)S(1)} custom-call(bf16[2,4,80,384]{3,2,1,0:T(8,128)(2,1)S(1)} %copy-done.11), custom_call_target="tpu_custom_call" | custom-call | tf_op jit(solution)/shard_map/reduce_rows/pallas_call | solution.py:104
  134.1 3.4 next_project.1
  138.4 13.8 %gather_kv.3.kv = bf16[4,160,384]{2,1,0:T(8,128)(2,1)S(1)} custom-call(bf16[160,384]{1,0:T(8,128)(2,1)S(1)} %copy-done.22), custom_call_target="tpu_custom_call" | custom-call | tf_op jit(solution)/shard_map/gather_kv/pallas_call | solution.py:139
  153.0 3.6 attend.3
  157.6 13.9 %reduce_rows.9.att = bf16[2,4,80,384]{3,2,1,0:T(8,128)(2,1)S(1)} custom-call(bf16[1,4,80,384]{3,2,1,0:T(8,128)(2,1)S(1)} %copy-done.21), custom_call_target="tpu_custom_call" | custom-call | tf_op jit(solution)/shard_map/reduce_rows/pallas_call | solution.py:104
  172.3 15.0 %experts_backward.2 = (bf16[2,4,176,384]{3,2,1,0:T(8,128)(2,1)}, bf16[16,8,48,384]{3,2,1,0:T(8,128)(2,1)}) custom-call(bf16[320,768]{1,0:T(8,128)(2,1)} %get-tuple-element.46.x, bf16[2,4,80,384]{3,2,1,0:T(8,128)(2,1)} %copy-done.3, f32[8,768]{1,0:T(8,128)} %reshape.267.small, f32[320,2]{1,0:T(8,128)} %copy.72.routes, ...), custom_call_target="tpu_custom_call" | custom-call | tf_op jit(solution)/shard_map/experts_backward/pallas_call | solution.py:547
  188.5 25.4 %reduce_rows.10.back = bf16[2,4,176,384]{3,2,1,0:T(8,128)(2,1)S(1)} custom-call(bf16[2,4,176,384]{3,2,1,0:T(8,128)(2,1)S(1)} %copy-done.12), custom_call_target="tpu_custom_call" | custom-call | tf_op jit(solution)/shard_map/reduce_rows/pallas_call | solution.py:104
  215.0 7.9 %attend_back.2 = (f32[320,768]{1,0:T(8,128)}, bf16[160,192]{1,0:T(8,128)(2,1)}, bf16[4,160,384]{2,1,0:T(8,128)(2,1)}, bf16[768,192]{1,0:T(8,128)(2,1)}, f32[8,768]{1,0:T(8,128)}) custom-call(s32[1]{0:T(128)} %bitcast.core, bf16[320,768]{1,0:T(8,128)(2,1)} %get-tuple-element.46.x, bf16[2,4,80,384]{3,2,1,0:T(8,128)(2,1)} %copy-done.3, ...), custom_call_target="tpu_custom_call" | custom-call | tf_op jit(solution)/shard_map/attend_back/pallas_call | solution.py:391
  223.9 7.8 %scatter_kv.2.grad_kv = bf16[160,384]{1,0:T(8,128)(2,1)S(1)} custom-call(bf16[4,160,384]{2,1,0:T(8,128)(2,1)S(1)} %copy-done.17), custom_call_target="tpu_custom_call" | custom-call | tf_op jit(solution)/shard_map/scatter_kv/pallas_call | solution.py:169
  236.7 13.5 %reduce_rows.11.back = bf16[2,4,80,384]{3,2,1,0:T(8,128)(2,1)S(1)} custom-call(bf16[1,4,80,384]{3,2,1,0:T(8,128)(2,1)S(1)} %copy-done.18), custom_call_target="tpu_custom_call" | custom-call | tf_op jit(solution)/shard_map/reduce_rows/pallas_call | solution.py:104
  254.0 12.8 %experts_backward.3 = (bf16[2,4,96,384]{3,2,1,0:T(8,128)(2,1)}, bf16[16,8,48,384]{3,2,1,0:T(8,128)(2,1)}) custom-call(bf16[320,768]{1,0:T(8,128)(2,1)} %bitcast.128, bf16[2,4,80,384]{3,2,1,0:T(8,128)(2,1)} %copy-done, f32[8,768]{1,0:T(8,128)} %reshape.265.small, f32[320,2]{1,0:T(8,128)} %copy.68.routes, bf16[320,768]{1,0:T(8,128)(2,1)} %get-tuple-element.56.grad, ...), custom_call_target="tpu_custom_call" | custom-call | tf_op jit(solution)/shard_map/experts_backward/pallas_call | solution.py:547
  268.2 17.6 %reduce_rows.12.back = bf16[2,4,96,384]{3,2,1,0:T(8,128)(2,1)S(1)} custom-call(bf16[2,4,96,384]{3,2,1,0:T(8,128)(2,1)S(1)} %copy-done.13), custom_call_target="tpu_custom_call" | custom-call | tf_op jit(solution)/shard_map/reduce_rows/pallas_call | solution.py:104
  286.7 7.8 %attend_back.3 = (f32[320,768]{1,0:T(8,128)}, bf16[160,192]{1,0:T(8,128)(2,1)}, bf16[4,160,384]{2,1,0:T(8,128)(2,1)}, bf16[768,192]{1,0:T(8,128)(2,1)}, f32[8,768]{1,0:T(8,128)}) custom-call(s32[1]{0:T(128)} %bitcast.core, bf16[320,768]{1,0:T(8,128)(2,1)} %bitcast.129, bf16[2,4,80,384]{3,2,1,0:T(8,128)(2,1)} %copy-done, f32[8,768]{1,0:T(8,128)} %reshape.265.small, ...), custom_call_target="tpu_custom_call" | custom-call | tf_op jit(solution)/shard_map/attend_back/pallas_call | solution.py:391
  295.5 12.4 %scatter_kv.3.grad_kv = bf16[160,384]{1,0:T(8,128)(2,1)S(1)} custom-call(bf16[4,160,384]{2,1,0:T(8,128)(2,1)S(1)} %copy-done.16), custom_call_target="tpu_custom_call" | custom-call | tf_op jit(solution)/shard_map/scatter_kv/pallas_call | solution.py:169
  312.9 13.1 %reduce_rows.13.back = bf16[2,4,80,384]{3,2,1,0:T(8,128)(2,1)S(1)} custom-call(bf16[1,4,80,384]{3,2,1,0:T(8,128)(2,1)S(1)} %copy-done.19), custom_call_target="tpu_custom_call" | custom-call | tf_op jit(solution)/shard_map/reduce_rows/pallas_call | solution.py:104
  333.2 33.7 %scatter_small.1 = f32[64,768]{1,0:T(8,128)S(1)} custom-call(bf16[2,16,64,768]{3,2,1,0:T(8,128)(2,1)S(1)} %bitcast.116), custom_call_target="tpu_custom_call" | custom-call | tf_op jit(solution)/shard_map/scatter_small/pallas_call | solution.py:316
  370.3 4.6 %collective-permute-start = (bf16[160,768]{1,0:T(8,128)(2,1)S(1)}, bf16[160,768]{1,0:T(8,128)(2,1)S(1)}, u32[]{:S(2)}, u32[]{:S(2)}) collective-permute-start(bf16[160,768]{1,0:T(8,128)(2,1)S(1)} %fusion.9), channel_id=1, source_target_pairs={{0,64},{32,96},{64,0},{96,32},{1,65},{33,97},{65,1},{97,33},{2,66}... | collective-permute-start | bytes 737288 | tf_op jit(solution)/shard_map/ppermute | solution.py:776
  376.8 57.6 %reduce-scatter.9.cloned.1.call-done = bf16[1,384,384]{2,1,0:T(8,128)(2,1)} async-done(((bf16[16,384,384]{2,1,0:T(8,128)(2,1)}), bf16[1,384,384]{2,1,0:T(8,128)(2,1)}) %reduce-scatter.9.cloned.1.call-update) | async-done | bytes 294928
  (190 shorter events, 64.7 us)
Async XLA Ops:
  7.2 102.4 %all-gather.3.cloned.1.call-start = ((), (), s32[]{:S(2)}) async-start(), calls=%async_computation.2 | async-start | bytes 5013504 | tf_op jit(solution)/shard_map/all_gather | solution.py:698
  8.5 1.3 copy-start.38
  8.5 1.3 copy-start.27
  22.8 2.0 copy-start.31
  22.8 2.2 copy-start.39
  22.8 2.2 copy-start.40
  22.8 2.2 copy-start.41
  22.9 2.2 copy-start.34
  23.9 148.5 %all-gather.5.cloned.1.call-start = ((), (), s32[]{:S(2)}) async-start(), calls=%async_computation.3 | async-start | bytes 5013504 | tf_op jit(solution)/shard_map/all_gather | solution.py:698
  24.6 352.2 %reduce-scatter.7.cloned.1.call-start = ((), (), s32[]{:S(2)}) async-start(), calls=%async_computation.4 | async-start | bytes 5013504
  65.8 19.0 %copy-start.42 = (s32[4]{0:T(128)S(1)}, s32[4]{0:T(128)}, u32[]{:S(2)}) copy-start(s32[4]{0:T(128)} %param.12) | copy-start | bytes 52
  106.0 10.6 %copy-start.33 = (f32[320,2]{0,1:T(2,128)}, f32[320,2]{0,1:T(2,128)S(1)}, u32[]{:S(2)}) copy-start(f32[320,2]{0,1:T(2,128)S(1)} %reshape.266) | copy-start | bytes 7684
  107.9 8.8 %copy-start.32 = (f32[320,2]{0,1:T(2,128)}, f32[320,2]{0,1:T(2,128)S(1)}, u32[]{:S(2)}) copy-start(f32[320,2]{0,1:T(2,128)S(1)} %reshape.268) | copy-start | bytes 7684
  187.3 1.2 copy-start.12
  266.8 167.6 %reduce-scatter.9.cloned.1.call-start = ((), (), s32[]{:S(2)}) async-start(), calls=%async_computation.5 | async-start | bytes 5013504
  312.9 17.7 %copy-start.37 = (f32[8,768]{1,0:T(8,128)S(1)}, f32[8,768]{1,0:T(8,128)}, u32[]{:S(2)}) copy-start(f32[8,768]{1,0:T(8,128)} %get-tuple-element.67) | copy-start | bytes 73732
  312.9 18.0 %copy-start.36 = (f32[8,768]{1,0:T(8,128)S(1)}, f32[8,768]{1,0:T(8,128)}, u32[]{:S(2)}) copy-start(f32[8,768]{1,0:T(8,128)} %get-tuple-element.70) | copy-start | bytes 73732
  312.9 18.0 %copy-start.35 = (f32[8,768]{1,0:T(8,128)S(1)}, f32[8,768]{1,0:T(8,128)}, u32[]{:S(2)}) copy-start(f32[8,768]{1,0:T(8,128)} %get-tuple-element.71) | copy-start | bytes 73732
  312.9 18.3 %copy-start.26 = (bf16[768,576]{1,0:T(8,128)(2,1)S(1)}, bf16[768,576]{1,0:T(8,128)(2,1)}, u32[]{:S(2)}) copy-start(bf16[768,576]{1,0:T(8,128)(2,1)} %get-tuple-element.64) | copy-start | bytes 2654212
  312.9 18.3 %copy-start.29 = (bf16[768,192]{1,0:T(8,128)(2,1)S(1)}, bf16[768,192]{1,0:T(8,128)(2,1)}, u32[]{:S(2)}) copy-start(bf16[768,192]{1,0:T(8,128)(2,1)} %get-tuple-element.65) | copy-start | bytes 884740
  330.7 1.3 copy-start.28
  333.2 34.5 %copy-start.2 = (bf16[2,4,176,384]{3,2,1,0:T(8,128)(2,1)S(1)}, bf16[2,4,176,384]{3,2,1,0:T(8,128)(2,1)}, u32[]{:S(2)}) copy-start(bf16[2,4,176,384]{3,2,1,0:T(8,128)(2,1)} %copy-done.1) | copy-start | bytes 3244036
  370.3 67.7 %collective-permute-start = (bf16[160,768]{1,0:T(8,128)(2,1)S(1)}, bf16[160,768]{1,0:T(8,128)(2,1)S(1)}, u32[]{:S(2)}, u32[]{:S(2)}) collective-permute-start(bf16[160,768]{1,0:T(8,128)(2,1)S(1)} %fusion.9), channel_id=1, source_target_pairs={{0,64},{32,96},{64,0},{96,32},{1,65},{33,97},{65,1},{97,33},{2,66}... | collective-permute-start | bytes 737288 | tf_op jit(solution)/shard_map/ppermute | solution.py:776
  435.6 3.6 collective-permute-start.1
  (25 other events, 22.9 us)
Sparse Core Ops, SparseCore 0:
  24.0 71.8 all-gather.2
  98.1 58.5 all-gather.4
  267.0 73.5 reduce-scatter.6
  343.7 90.6 reduce-scatter.8

commit v2 on v1

v2 whole, which is shorter than its diff:
```python
import functools

import jax
import jax.numpy as jnp
from jax import lax
from jax.experimental import pallas as pl
from jax.experimental.pallas import tpu as pltpu
from jax.sharding import Mesh
from jax.sharding import PartitionSpec as P

D = 768
HD = 64
HEADS = 3
ROWS = 160
PAIR = 320
KEYS = 640
FE = 384
EXPERTS = 4
EPS = 1e-06
WIDTH = HEADS * HD
MESH = pl.DeviceIdType.MESH
CHIPS = ("x", "zh", "zl")
f32, bf16 = jnp.float32, jnp.bfloat16
VMEM = pl.BlockSpec(memory_space=pltpu.VMEM)
SMEM = pl.BlockSpec(memory_space=pltpu.SMEM)
NN = (((1,), (0,)), ((), ()))
NT = (((1,), (1,)), ((), ()))
TN = (((0,), (0,)), ((), ()))


def dot(a, b, dims):
    return lax.dot_general(a, b, dims, preferred_element_type=f32)


def dot_exact(a, b, dims):
    return lax.dot_general(
        a, b, dims, preferred_element_type=f32, precision=lax.Precision.HIGHEST
    )


def params(cid, mib):
    return pltpu.CompilerParams(
        collective_id=cid, has_side_effects=True, vmem_limit_bytes=mib * 2**20
    )


def arrive(peers):
    barrier = pltpu.get_barrier_semaphore()
    for peer in peers:
        pl.semaphore_signal(barrier, inc=1, device_id=peer, device_id_type=MESH)


def all_here(count):
    pl.semaphore_wait(pltpu.get_barrier_semaphore(), count)


def dma_sems(*counts):
    return [pltpu.SemaphoreType.DMA((count,)) for count in counts for _ in range(2)]


def remote(src, dst, send, recv, peer):
    return pltpu.make_async_remote_copy(
        src_ref=src, dst_ref=dst, send_sem=send, recv_sem=recv, device_id=peer, device_id_type=MESH
    )


def sum_peers(both):
    core, tp = lax.axis_index("core"), lax.axis_index("tp")
    offsets = [(k // 4, k % 4) for k in range(1, 8 if both else 4)]
    return [{"core": (core + dc) % 2, "tp": (tp + dt) % 4} for dc, dt in offsets]


def sum_terms(both, part, landed, send, recv):
    return [
        remote(part.at[peer["core"] if both else 0, peer["tp"]], landed.at[k], send.at[k], recv.at[k], peer)
        for k, peer in enumerate(sum_peers(both))
    ]


def sum_results(out, send, recv):
    core, tp = lax.axis_index("core"), lax.axis_index("tp")
    return [
        remote(out.at[core, tp], out.at[core, tp], send.at[k], recv.at[k], {"tp": (tp + k + 1) % 4})
        for k in range(3)
    ]


def sum_cross(out, send, recv):
    core, tp = lax.axis_index("core"), lax.axis_index("tp")
    return [
        remote(out.at[core, at], out.at[core, at], send.at[k], recv.at[k], {"core": 1 - core})
        for k, at in enumerate([(tp + 4 - k) % 4 for k in range(4)])
    ]


def sum_start(both, part, out, landed, rs, rr, gs, gr, cs, cr):
    for copy in sum_terms(both, part, landed, rs, rr):
        copy.start()


def sum_middle(both, part, out, landed, rs, rr, gs, gr, cs, cr):
    core, tp = lax.axis_index("core"), lax.axis_index("tp")
    total = part[core if both else 0, tp].astype(f32)
    for k, copy in enumerate(sum_terms(both, part, landed, rs, rr)):
        copy.wait_recv()
        total = total + landed[k].astype(f32)
    out[core, tp] = total.astype(bf16)
    for copy in sum_results(out, gs, gr):
        copy.start()


def sum_end(both, part, out, landed, rs, rr, gs, gr, cs, cr):
    gathers, crosses = sum_results(out, gs, gr), sum_cross(out, cs, cr)
    for k in range(4):
        if k > 0:
            gathers[k - 1].wait_recv()
        crosses[k].start()
    for copy in crosses:
        copy.wait()
    for copy in sum_terms(both, part, landed, rs, rr) + gathers:
        copy.wait_send()


def sum_scratch(both, rows):
    count = 7 if both else 3
    return [
        pltpu.VMEM((2 if both else 1, 4, rows, 384), bf16),
        pltpu.VMEM((count, rows, 384), bf16),
    ] + dma_sems(count, 3, 4)


def ctx_peers():
    core, zl = lax.axis_index("core"), lax.axis_index("zl")
    return [
        {"zl": (zl + k // 2) % 2, "core": (core + k % 2) % 2} for k in range(1, 4)
    ], zl * 2 + core


def chip_peer(k):
    x, zh, zl = (lax.axis_index(a) for a in CHIPS)
    dx, dh, dl = k // 4, (k // 2) % 2, k % 2
    ahead = ((x + dx) % 4, (zh + dh) % 2, (zl + dl) % 2)
    back = ((x + 4 - dx) % 4, (zh + 2 - dh) % 2, (zl + 2 - dl) % 2)
    return dict(zip(CHIPS, ahead)), *(c[0] * 4 + c[1] * 2 + c[2] for c in (ahead, back))


def cross_kernel(own, out, send, recv):
    other = {"core": 1 - lax.axis_index("core")}
    arrive([other])
    all_here(1)
    copy = remote(own, out, send.at[0], recv.at[0], other)
    copy.start()
    copy.wait()


def cross(own, cid):
    return pl.pallas_call(
        cross_kernel,
        out_shape=jax.ShapeDtypeStruct(own.shape, own.dtype),
        in_specs=[VMEM],
        out_specs=VMEM,
        scratch_shapes=dma_sems(1),
        compiler_params=params(cid, 8),
        name="cross",
    )(own)


def start_kernel(images, own, out_images, out, im_send, im_recv, send, recv, cx_send, cx_recv):
    core, x = lax.axis_index("core"), lax.axis_index("x")
    high = x // 2
    other = {"core": 1 - core}
    _, me, _ = chip_peer(0)
    arrive([chip_peer(k)[0] for k in range(1, 16)] + [other])
    out[me, core] = own[...]
    out_images[core, high] = images[high]
    all_here(16)

    def push(k):
        peer, _, _ = chip_peer(k)
        return remote(own, out.at[me, core], send.at[k], recv.at[k], peer)

    def pass_on(k):
        _, _, at = chip_peer(k)
        return remote(out.at[at, core], out.at[at, core], cx_send.at[k], cx_recv.at[k], other)

    swap = remote(
        images.at[1 - high], out_images.at[core, high], im_send.at[0], im_recv.at[0], {"x": (x + 2) % 4}
    )
    kept = remote(images.at[high], out_images.at[core, high], im_send.at[1], im_recv.at[1], other)
    swap.start()

    def first(k, carry):
        push(k).start()
        return carry

    def onward(k, carry):
        push(k).wait_recv()
        pass_on(k).start()
        return carry

    def last(k, carry):
        push(k).wait_send()
        pass_on(k).wait()
        return carry

    lax.fori_loop(1, 16, first, 0)
    kept.start()
    pass_on(0).start()
    swap.wait_recv()
    passed = remote(
        out_images.at[core, 1 - high], out_images.at[core, 1 - high], im_send.at[2], im_recv.at[2], other
    )
    passed.start()
    lax.fori_loop(1, 16, onward, 0)
    pass_on(0).wait()
    lax.fori_loop(1, 16, last, 0)
    for copy in (kept, passed):
        copy.wait()
    swap.wait_send()


def start_exchange(images, own):
    return pl.pallas_call(
        start_kernel,
        out_shape=(
            jax.ShapeDtypeStruct((2,) + images.shape, bf16),
            jax.ShapeDtypeStruct((16, 2) + own.shape, bf16),
        ),
        in_specs=[VMEM, VMEM],
        out_specs=(VMEM, VMEM),
        scratch_shapes=dma_sems(3, 16, 16),
        compiler_params=params(1, 56),
        name="start_exchange",
    )(images, own)


def end_kernel(
    part, image, half, out, out_image, out_half, landed, sums, pieces, cx_s, cx_r, send, recv
):
    core, x = lax.axis_index("core"), lax.axis_index("x")
    other = {"core": 1 - core}
    _, me, _ = chip_peer(0)
    arrive([chip_peer(k)[0] for k in range(1, 16)] + [other])
    all_here(16)
    crossing = remote(part.at[1 - core], landed, cx_s.at[0], cx_r.at[0], other)
    crossing.start()
    swap = remote(image, out_image, cx_s.at[1], cx_r.at[1], {"x": (x + 2) % 4})
    swap.start()
    halves = remote(half, out_half, cx_s.at[2], cx_r.at[2], other)
    halves.start()
    crossing.wait()

    def push(k):
        peer, at, _ = chip_peer(k)
        return remote(sums.at[at], pieces.at[k], send.at[k], recv.at[k], peer)

    def add(k, carry):
        _, at, _ = chip_peer(k)
        sums[at] = (part[core, at].astype(f32) + landed[at].astype(f32)).astype(bf16)
        push(k).start()
        return carry

    def collect(k, carry):
        push(k).wait_recv()
        out[...] += pieces[k].astype(f32)
        return carry

    def last(k, carry):
        push(k).wait_send()
        return carry

    lax.fori_loop(1, 16, add, 0)
    out[...] = part[core, me].astype(f32) + landed[me].astype(f32)
    lax.fori_loop(1, 16, collect, 0)
    lax.fori_loop(1, 16, last, 0)
    swap.wait()
    halves.wait()


def end_exchange(part, image, half):
    shape = part.shape[2:]
    return pl.pallas_call(
        end_kernel,
        out_shape=(
            jax.ShapeDtypeStruct(shape, f32),
            jax.ShapeDtypeStruct(image.shape, bf16),
            jax.ShapeDtypeStruct(half.shape, bf16),
        ),
        in_specs=[VMEM] * 3,
        out_specs=(VMEM,) * 3,
        scratch_shapes=[pltpu.VMEM((16,) + shape, bf16)] * 3 + dma_sems(3, 16),
        compiler_params=params(2, 56),
        name="end_exchange",
    )(part, image, half)


def block_rows(ref, block):
    top = jnp.concatenate([ref[block, 0, 0:80], ref[block, 1, 0:80]], axis=1)
    low = jnp.concatenate([ref[block, 2, 0:80], ref[block, 3, 0:80]], axis=1)
    return jnp.concatenate([top, low], axis=0).astype(f32)


def pair_rows(ref):
    return jnp.concatenate([block_rows(ref, 0), block_rows(ref, 1)], axis=0)


def put_chunks(ref, block, value, first=0):
    for j in range(4):
        r, c = 80 * (j // 2), 384 * (j % 2)
        ref[block, j, first : first + 80] = value[r : r + 80, c : c + 384]


def norm_parts(rows):
    centered = rows - jnp.mean(rows, axis=-1, keepdims=True)
    scale = lax.rsqrt(jnp.mean(centered * centered, axis=-1, keepdims=True) + EPS)
    return centered * scale, scale


def norm_back(grad, unit, scale, gain):
    inner = grad * gain
    return scale * (
        inner
        - jnp.mean(inner, axis=-1, keepdims=True)
        - unit * jnp.mean(inner * unit, axis=-1, keepdims=True)
    )


def softmax(logits, axis):
    top = jnp.max(logits, axis=axis, keepdims=True)
    powers = jnp.exp(logits - top)
    return powers / jnp.sum(powers, axis=axis, keepdims=True)


def own_rows(core):
    return pl.ds(pl.multiple_of(core * ROWS, ROWS), ROWS)


def head(value, h):
    return value[:, HD * h : HD * h + HD]


def gelu_parts(u):
    c = 0.7978845608028654
    t = jnp.tanh(c * (u + 0.044715 * u * u * u))
    return 0.5 * u * (1.0 + t), t


def gelu_slope(u, t):
    c = 0.7978845608028654
    return 0.5 * (1.0 + t) + 0.5 * u * (1.0 - t * t) * (c * (1.0 + 3 * 0.044715 * u * u))


def attend_forward_kernel(follows, *refs):
    if follows:
        x, att_before, moe_before, small, w_kv, w_qo, dead, q, kv, mixed, att, x_next, *scratch = refs
    else:
        x, small, w_kv, w_qo, dead, q, kv, mixed, att, *scratch = refs
    part, landed, *sems, kv_send, kv_recv = scratch
    sums = (False, part, att, landed, *sems)
    core = lax.axis_index("core")
    peers, me = ctx_peers()
    arrive(peers + sum_peers(False))
    if follows:
        x_next[...] = (x[...].astype(f32) + pair_rows(att_before) + pair_rows(moe_before)).astype(bf16)
        x = x_next
    unit, _ = norm_parts(x[own_rows(core)].astype(f32))
    normed = (unit * small[0:1] + small[2:3]).astype(bf16)
    kv[me] = dot(normed, w_kv[...], NN).astype(bf16)
    all_here(6)
    copies = [
        remote(kv.at[me], kv.at[me], kv_send.at[k], kv_recv.at[k], peer)
        for k, peer in enumerate(peers)
    ]
    for copy in copies:
        copy.start()
    queries = dot(normed, w_qo[:, :WIDTH], NN).astype(bf16)
    q[...] = queries
    for copy in copies:
        copy.wait_recv()
    keys = kv[...].reshape(KEYS, 2 * WIDTH)
    outs = []
    for h in range(HEADS):
        scores = HD**-0.5 * dot(head(queries, h), head(keys, h), NT) + dead[...]
        probs = softmax(scores, -1).astype(bf16)
        outs.append(dot(probs, head(keys, HEADS + h), NN))
    heads = jnp.concatenate(outs, axis=1).astype(bf16)
    mixed[...] = heads
    put_chunks(part, 0, dot(heads, w_qo[:, WIDTH:], NT).astype(bf16))
    sum_start(*sums)
    sum_middle(*sums)
    sum_end(*sums)
    for copy in copies:
        copy.wait_send()


def attend_forward(x, before, small, w_kv, w_qo, dead, cid):
    args = (x, *before, small, w_kv, w_qo, dead)
    shapes = [(ROWS, WIDTH), (4, ROWS, 2 * WIDTH), (ROWS, WIDTH), (2, 4, 80, 384)]
    if before:
        shapes.append((PAIR, D))
    return pl.pallas_call(
        functools.partial(attend_forward_kernel, bool(before)),
        out_shape=[jax.ShapeDtypeStruct(s, bf16) for s in shapes],
        in_specs=[VMEM] * len(args),
        out_specs=[VMEM] * len(shapes),
        scratch_shapes=sum_scratch(False, 80) + dma_sems(3),
        compiler_params=params(cid, 56),
        name="attend_forward",
    )(*args)


def expert_weights(weights):
    block = weights[...]
    return block[:, 0:48].reshape(D, FE), block[:, 48:96].reshape(D, FE)


def experts_setup(x, att, small, routes, b, gates):
    unit, _ = norm_parts(x[...].astype(f32) + pair_rows(att))
    b[...] = (unit * small[1:2] + small[3:4]).astype(bf16)
    probs = softmax(dot(b[...], small[4:8].astype(bf16), NT), -1)
    ids = lax.broadcasted_iota(jnp.int32, (PAIR, EXPERTS), 1).astype(f32)
    named = (routes[:, 0:1] == ids) | (routes[:, 1:2] == ids)
    gates[...] = jnp.where(named, probs, 0.0)


def gate_of(gates, expert):
    ids = lax.broadcasted_iota(jnp.int32, (PAIR, EXPERTS), 1)
    return jnp.sum(jnp.where(ids == expert, gates[...], 0.0), axis=1, keepdims=True)


def experts_forward_kernel(
    x, att, small, routes, weights, result, b, gates, total, out, part, landed, *sems
):
    expert = pl.program_id(0)
    sums = (True, part, out, landed, *sems)

    @pl.when(expert == 0)
    def _():
        arrive(sum_peers(True))
        experts_setup(x, att, small, routes, b, gates)
        total[...] = jnp.zeros_like(total)

    w_in, w_out_t = expert_weights(weights)
    u = dot(b[...], w_in, NN)
    active = gelu_parts(u)[0].astype(bf16).astype(f32)
    gated = (gate_of(gates, expert) * active).astype(bf16)
    total[...] += dot(gated, w_out_t, NT)

    @pl.when(expert == EXPERTS - 1)
    def _():
        for block in range(2):
            put_chunks(part, block, total[ROWS * block : ROWS * block + ROWS].astype(bf16))
        all_here(7)
        sum_start(*sums)
        sum_middle(*sums)
        sum_end(*sums)
        result[...] = out[...]


def fixed(shape):
    return pl.BlockSpec(shape, lambda e: (0,) * len(shape))


def experts_forward(x, att, small, routes, weights, cid):
    args = (x, att, small, routes)
    return pl.pallas_call(
        experts_forward_kernel,
        grid=(EXPERTS,),
        out_shape=jax.ShapeDtypeStruct((2, 4, 80, 384), bf16),
        in_specs=[fixed(a.shape) for a in args] + [pl.BlockSpec((16, 96, FE), lambda e: (0, e, 0))],
        out_specs=fixed((2, 4, 80, 384)),
        scratch_shapes=[
            pltpu.VMEM((PAIR, D), bf16),
            pltpu.VMEM((PAIR, EXPERTS), f32),
            pltpu.VMEM((PAIR, D), f32),
            pltpu.VMEM((2, 4, 80, 384), bf16),
        ]
        + sum_scratch(True, 80),
        compiler_params=params(cid, 56),
        name="experts_forward",
    )(*args, weights)


def experts_backward_kernel(
    steps, x, att, small, routes, grad, extra, weights, result, moe_part, grad_w,
    b, gates, total, moe, gate_t, gated_all, grad_u_all, out, part, landed, *sems,
):
    step = pl.program_id(0)
    sums = (True, part, out, landed, *sems)
    with_moe = moe_part is not None

    @pl.when(step == 0)
    def _():
        arrive(sum_peers(True))
        experts_setup(x, att, small, routes, b, gates)
        total[...] = jnp.zeros_like(total)
        if with_moe:
            moe[...] = jnp.zeros_like(moe)

    @pl.when(step < EXPERTS)
    def _():
        w_in, w_out_t = expert_weights(weights)
        u = dot(b[...], w_in, NN)
        act, t = gelu_parts(u)
        active = act.astype(bf16).astype(f32)
        gate = gate_of(gates, step)
        gated = (gate * active).astype(bf16)
        gated_all[step] = gated
        if with_moe:
            moe[...] += dot(gated, w_out_t, NT)
        back = dot(grad[...], w_out_t, NN)
        gate_t[step] = dot_exact(jnp.ones((8, FE), f32), back * active, NT)
        grad_u = (gate * back * gelu_slope(u, t)).astype(bf16)
        grad_u_all[step] = grad_u
        total[...] += dot(grad_u, w_in, NT)

    @pl.when(step == EXPERTS - 1)
    def _():
        part[...] = jnp.zeros_like(part)
        for block in range(2):
            lines = slice(ROWS * block, ROWS * block + ROWS)
            put_chunks(part, block, total[lines].astype(bf16))
            table = jnp.concatenate(
                [gate_t[e, 0:1, lines] for e in range(EXPERTS)] + [jnp.zeros((12, ROWS), f32)], axis=0
            )
            part[block, 0, 80:96, 0:ROWS] = table.astype(bf16)
            if with_moe:
                put_chunks(moe_part, block, moe[lines].astype(bf16))
        all_here(7)
        sum_start(*sums)

    @pl.when((step >= EXPERTS) & (step < 2 * EXPERTS))
    def _():
        at = step - EXPERTS
        grad_w[:, 0:48] = dot(b[...], grad_u_all[at], TN).astype(bf16).reshape(16, 48, FE)
        grad_w[:, 48:96] = dot(grad[...], gated_all[at], TN).astype(bf16).reshape(16, 48, FE)

    @pl.when(step == EXPERTS + 1)
    def _():
        sum_middle(*sums)

    if steps > 2 * EXPERTS:

        @pl.when(step == 2 * EXPERTS)
        def _():
            grad_w[:, 0:48] = extra[0].reshape(16, 48, FE)
            grad_w[:, 48:96] = extra[1].reshape(16, 48, FE)

    @pl.when(step == steps - 1)
    def _():
        sum_end(*sums)
        result[...] = out[...]


def experts_backward(x, att, small, routes, grad, extra, weights, first, cid):
    args = (x, att, small, routes, grad)
    steps = 2 * EXPERTS
    shapes = [(2, 4, 96, 384)]
    blocks = [fixed((2, 4, 96, 384))]
    if extra is None:
        shapes.append((2, 4, 80, 384))
        blocks.append(fixed((2, 4, 80, 384)))

        def kernel(*refs):
            experts_backward_kernel(steps, *refs[:5], None, *refs[5:])
    else:
        args, steps = args + (extra,), steps + 1

        def kernel(*refs):
            experts_backward_kernel(steps, *refs[:8], None, *refs[8:])

    grads = steps - EXPERTS
    return pl.pallas_call(
        kernel,
        grid=(steps,),
        out_shape=[jax.ShapeDtypeStruct(s, bf16) for s in shapes + [(16, 96 * grads, FE)]],
        in_specs=[fixed(a.shape) for a in args]
        + [pl.BlockSpec((16, 96, FE), lambda s: (0, first + jnp.minimum(s, EXPERTS - 1), 0))],
        out_specs=blocks + [pl.BlockSpec((16, 96, FE), lambda s: (0, jnp.maximum(s - EXPERTS, 0), 0))],
        scratch_shapes=[
            pltpu.VMEM((PAIR, D), bf16),
            pltpu.VMEM((PAIR, EXPERTS), f32),
            pltpu.VMEM((PAIR, D), f32),
            pltpu.VMEM((PAIR, D), f32),
            pltpu.VMEM((EXPERTS, 8, PAIR), f32),
            pltpu.VMEM((EXPERTS, PAIR, FE), bf16),
            pltpu.VMEM((EXPERTS, PAIR, FE), bf16),
            pltpu.VMEM((2, 4, 96, 384), bf16),
        ]
        + sum_scratch(True, 96),
        compiler_params=params(cid, 56),
        name="experts_backward",
    )(*args, weights)


def attend_backward_kernel(with_moe, *refs):
    x, att, small, routes_t, grad, back, q, kv, mixed, dead, w_kv, w_qo, *refs = refs
    if with_moe:
        moe_part, *refs = refs
    grad_x, grad_small, grad_w, *refs = refs
    if with_moe:
        moe, *refs = refs
    grad_h, both_units, parts, kv_landed, back_one, part, landed, *sems = refs
    if with_moe:
        *sems, moe_landed, ms, mr, ns, nr = sems
    *sems, kv_send, kv_recv = sems
    sums = (False, part, back_one, landed, *sems)
    core, tp = lax.axis_index("core"), lax.axis_index("tp")
    peers, me = ctx_peers()
    arrive(peers + sum_peers(False) + (sum_peers(True)[4:] if with_moe else []))
    unit, scale = norm_parts(x[...].astype(f32) + pair_rows(att))
    b = (unit * small[1:2] + small[3:4]).astype(bf16)
    router = small[4:8]
    probs = softmax(dot(router.astype(bf16), b, NT), 0)
    ids = lax.broadcasted_iota(jnp.int32, (EXPERTS, PAIR), 0).astype(f32)
    named = (routes_t[0:1] == ids) | (routes_t[1:2] == ids)
    tables = [back[block, 0, 80:96, 0:ROWS].astype(f32)[0:EXPERTS] for block in range(2)]
    gate_grads = jnp.where(named, jnp.concatenate(tables, axis=1), 0.0)
    grad_logits = probs * (gate_grads - jnp.sum(probs * gate_grads, axis=0, keepdims=True))
    grad_b = pair_rows(back) + dot_exact(grad_logits, router, TN)
    grad_h[...] = grad[...].astype(f32) + norm_back(grad_b, unit, scale, small[1:2])
    grad_att = grad_h[own_rows(core)].astype(bf16)
    grad_mixed = dot(grad_att, w_qo[:, WIDTH:], NN).astype(bf16)
    keys = kv[...].reshape(KEYS, 2 * WIDTH)
    queries = q[...]
    q_parts, k_parts, v_parts = [], [], []
    for h in range(HEADS):
        q_h, g_h = head(queries, h), head(grad_mixed, h)
        k_h, v_h = head(keys, h), head(keys, HEADS + h)
        weights = softmax(HD**-0.5 * dot(q_h, k_h, NT) + dead[...], -1)
        v_parts.append(dot(weights.astype(bf16), g_h, TN))
        grad_weights = dot(g_h, v_h, NT)
        grad_scores = weights * (
            grad_weights - jnp.sum(weights * grad_weights, axis=-1, keepdims=True)
        )
        grad_scores = grad_scores.astype(bf16)
        q_parts.append(HD**-0.5 * dot(grad_scores, k_h, NN))
        k_parts.append(HD**-0.5 * dot(grad_scores, q_h, TN))
    total = jnp.concatenate(k_parts + v_parts, axis=1).astype(bf16)
    parts[...] = total.reshape(4, ROWS, 2 * WIDTH)
    all_here(9 if with_moe else 6)
    copies = [
        remote(parts.at[peer["zl"] * 2 + peer["core"]], kv_landed.at[k], kv_send.at[k], kv_recv.at[k], peer)
        for k, peer in enumerate(peers)
    ]
    for copy in copies:
        copy.start()
    if with_moe:
        moe_terms = sum_terms(True, moe_part, moe_landed, ms, mr)
        for copy in moe_terms:
            copy.start()
    grad_q = jnp.concatenate(q_parts, axis=1).astype(bf16)
    grad_w[1, :, WIDTH:] = dot(grad_att, mixed[...], TN).astype(bf16)
    lanes = lax.broadcasted_iota(jnp.int32, (EXPERTS, PAIR), 1)
    own_lanes = (lanes < ROWS) == (core == 0)
    own = (lax.broadcasted_iota(jnp.int32, (PAIR, 1), 0) < ROWS) == (core == 0)
    kept = jnp.where(own, grad_b, 0.0)
    grad_small[1:2] = jnp.sum(kept * unit, axis=0, keepdims=True)
    grad_small[3:4] = jnp.sum(kept, axis=0, keepdims=True)
    grad_small[4:8] = dot_exact(jnp.where(own_lanes, grad_logits, 0.0), b.astype(f32), NN)
    unit_one, scale_one = norm_parts(x[...].astype(f32))
    both_units[...] = unit_one
    normed = (both_units[own_rows(core)] * small[0:1] + small[2:3]).astype(bf16)
    grad_kv = parts[me].astype(f32)
    for k, copy in enumerate(copies):
        copy.wait_recv()
        grad_kv = grad_kv + kv_landed[k].astype(f32)
    grad_kv = grad_kv.astype(bf16)
    value = dot(grad_kv, w_kv[...], NT) + dot(grad_q, w_qo[:, :WIDTH], NT)
    put_chunks(part, 0, value.astype(bf16))
    sum_start(*sums)
    grad_w[0] = dot(normed, grad_kv, TN).astype(bf16)
    grad_w[1, :, :WIDTH] = dot(normed, grad_q, TN).astype(bf16)
    sum_middle(*sums)
    if with_moe:
        total = moe_part[core, tp].astype(f32)
        for k, copy in enumerate(moe_terms):
            copy.wait_recv()
            total = total + moe_landed[k].astype(f32)
        moe[tp] = total.astype(bf16)
        moe_results = [
            remote(moe.at[tp], moe.at[tp], ns.at[k], nr.at[k], {"tp": (tp + k + 1) % 4}) for k in range(3)
        ]
        for copy in moe_results:
            copy.start()
    sum_end(*sums)
    grad_a = pair_rows(back_one)
    grad_x[...] = (grad_h[...] + norm_back(grad_a, unit_one, scale_one, small[0:1])).astype(bf16)
    kept = jnp.where(own, grad_a, 0.0)
    grad_small[0:1] = jnp.sum(kept * unit_one, axis=0, keepdims=True)
    grad_small[2:3] = jnp.sum(kept, axis=0, keepdims=True)
    for copy in copies:
        copy.wait_send()
    if with_moe:
        for copy in moe_terms:
            copy.wait_send()
        for copy in moe_results:
            copy.wait()


def attend_backward(args, moe_part, cid):
    with_moe = moe_part is not None
    shapes = [((PAIR, D), bf16), ((8, D), f32), ((2, D, 2 * WIDTH), bf16)]
    scratch = [
        pltpu.VMEM((PAIR, D), f32),
        pltpu.VMEM((PAIR, D), f32),
        pltpu.VMEM((4, ROWS, 2 * WIDTH), bf16),
        pltpu.VMEM((3, ROWS, 2 * WIDTH), bf16),
        pltpu.VMEM((2, 4, 80, 384), bf16),
    ]
    scratch += sum_scratch(False, 80) + dma_sems(3)
    if with_moe:
        args = args + (moe_part,)
        shapes.append(((4, 80, 384), bf16))
        scratch += [pltpu.VMEM((7, 80, 384), bf16)] + dma_sems(7, 3)
    return pl.pallas_call(
        functools.partial(attend_backward_kernel, with_moe),
        out_shape=[jax.ShapeDtypeStruct(*s) for s in shapes],
        in_specs=[VMEM] * len(args),
        out_specs=[VMEM] * len(shapes),
        scratch_shapes=scratch,
        compiler_params=params(cid, 56),
        name="attend_backward",
    )(*args)


def shards(boundary, routes, lengths, ln_gains, ln_biases, w_qkv, w_out, w_router, w_in, w_exp_out):
    core = lax.axis_index("core")
    high = lax.axis_index("x") // 2

    def pick(value, at, axis):
        return lax.dynamic_index_in_dim(value, at, axis, keepdims=False)

    halves = jnp.stack(
        [
            w_qkv[:, :, 1:].reshape(2, 24, 384),
            jnp.concatenate([w_qkv[:, :, 0], w_out.transpose(0, 2, 1)], axis=2),
        ],
        axis=1,
    )

    stacked = jnp.stack([w_in, w_exp_out.transpose(0, 1, 3, 2)], axis=2).reshape(384, 2, FE)
    attn_one = halves[1].reshape(48, 384)
    own_half = jnp.concatenate([pick(stacked, core, 1), attn_one])
    got_half = cross(jnp.concatenate([pick(stacked, 1 - core, 1), attn_one]), 0)
    low_half = jnp.where(core == 0, own_half, got_half).reshape(18, 24, FE)
    high_half = jnp.where(core == 0, got_half, own_half).reshape(18, 24, FE)
    chip = jnp.concatenate([low_half, high_half], axis=1).reshape(864, FE)
    every = lax.all_gather(chip, CHIPS, axis=0)
    experts = [every, every]

    turned = jnp.pad(
        routes[0].astype(bf16).transpose(0, 2, 1), ((0, 0), (0, 14), (0, D - ROWS))
    )
    images = jnp.concatenate([boundary[0], turned], axis=1)
    tiny = jnp.concatenate([ln_gains, ln_biases, w_router.transpose(0, 2, 1)], axis=1)
    tiny = jnp.pad(tiny.transpose(1, 0, 2).reshape(8, 48), ((0, 0), (0, D - 48)))
    pack = jnp.concatenate([jnp.concatenate([halves[0, 0], halves[0, 1]], axis=1), tiny])
    got_images, packs = start_exchange(images, pack)
    packs = packs.reshape(32, 32, D)
    w_kvs, w_qos = [packs[:, 0:24, 0:384].reshape(D, 384)], [packs[:, 0:24, 384:].reshape(D, 384)]
    w_kvs.append(every[:, 768:816].reshape(D, 384))
    w_qos.append(every[:, 816:864].reshape(D, 384))
    tiny = packs[:, 24:32, 0:48].reshape(32, 8, 2, 24).transpose(2, 1, 0, 3).reshape(2, 8, D)
    smalls = [tiny[0].astype(f32), tiny[1].astype(f32)]

    live = jnp.arange(ROWS, dtype=jnp.int32)[None, :] < lengths[:, None]
    dead = jnp.where(live.reshape(1, KEYS), 0.0, -1e30).astype(f32)
    chip_live = lax.dynamic_slice_in_dim(live, 2 * lax.axis_index("zl"), 2, 0)
    own_live = pick(chip_live, core, 0)

    x0 = got_images[:, 0, 0:ROWS].reshape(PAIR, D)
    cotangent = jnp.where(chip_live[:, :, None], got_images[:, 1, 0:ROWS], 0).reshape(PAIR, D)
    route_rows = [
        got_images[:, kind, ROWS : ROWS + 2, 0:ROWS].transpose(1, 0, 2).reshape(2, PAIR).astype(f32)
        for kind in range(2)
    ]
    route_cols = [rows.T for rows in route_rows]

    q0, kv0, mixed0, att0 = attend_forward(x0, (), smalls[0], w_kvs[0], w_qos[0], dead, 3)
    moe0 = experts_forward(x0, att0, smalls[0], route_cols[0], experts[0], 4)
    q1, kv1, mixed1, att1, x1 = attend_forward(
        x0, (att0, moe0), smalls[1], w_kvs[1], w_qos[1], dead, 5
    )
    back, moe_part, grad_experts1 = experts_backward(
        x1, att1, smalls[1], route_cols[1], cotangent, None, experts[1], EXPERTS, 6
    )
    sums1 = lax.psum_scatter(grad_experts1, CHIPS, scatter_dimension=0).reshape(8, 48, FE)
    grad_x1, grad_small1, grad_attn1, moe1 = attend_backward(
        (x1, att1, smalls[1], route_rows[1], cotangent, back, q1, kv1, mixed1, dead, w_kvs[1], w_qos[1]),
        moe_part,
        7,
    )
    back, grad_experts0 = experts_backward(
        x0, att0, smalls[0], route_cols[0], grad_x1, grad_attn1, experts[0], 0, 8
    )
    sums0 = lax.psum_scatter(grad_experts0, CHIPS, scatter_dimension=0).reshape(10, 48, FE)
    grad_x0, grad_small0, grad_attn0 = attend_backward(
        (x0, att0, smalls[0], route_rows[0], grad_x1, back, q0, kv0, mixed0, dead, w_kvs[0], w_qos[0]),
        None,
        9,
    )

    def own_block(value):
        return pick(value, core, 0)

    def unchunk(value):
        return value.reshape(2, 2, 80, 384).transpose(0, 2, 1, 3).reshape(ROWS, D).astype(f32)

    y1 = own_block(x1.reshape(2, ROWS, D)).astype(f32) + unchunk(own_block(att1)) + unchunk(moe1)
    mine = jnp.stack([own_block(grad_x0.reshape(2, ROWS, D)).astype(f32), y1])
    mine = jnp.where(own_live[None, :, None], mine, 0.0)
    kept, sent = pick(mine, high, 0), pick(mine, 1 - high, 0).astype(bf16)

    tiny = jnp.stack([grad_small0, grad_small1], axis=1).astype(bf16).reshape(8, 2, 16, 2, 24)
    tiny = tiny.transpose(3, 2, 0, 1, 4).reshape(2, 16, 8, 48)
    tiny = jnp.pad(tiny, ((0, 0), (0, 0), (0, 0), (0, D - 48)))
    packs = grad_attn0.reshape(2, 16, 2, 24, 384).transpose(2, 1, 3, 0, 4).reshape(2, 16, 24, D)
    packs = jnp.concatenate([packs, tiny], axis=2)

    def by_core(sums, at):
        return lax.dynamic_slice_in_dim(sums, 24 * at, 24, 1)

    own, landed, got1 = end_exchange(packs, sent, by_core(sums1, 1 - core).reshape(192, FE))
    landed = landed.astype(f32)
    ends = jnp.where(high == 0, jnp.stack([kept, landed]), jnp.stack([landed, kept]))
    got0 = cross(by_core(sums0, 1 - core).reshape(240, FE), 10).reshape(10, 24, FE)
    own0 = by_core(sums0, core)
    attn1 = own0[8:10].astype(f32) + got0[8:10].astype(f32)

    def both_halves(own_sum, got_sum):
        first = jnp.where(core == 0, own_sum, got_sum)
        second = jnp.where(core == 0, got_sum, own_sum)
        return jnp.concatenate([first, second], axis=2).reshape(EXPERTS, 2, 24, D).astype(f32)

    full = jnp.stack(
        [both_halves(own0[0:8], got0[0:8]), both_halves(by_core(sums1, core), got1.reshape(8, 24, FE))]
    )
    attn0 = own[0:24].reshape(24, 2, 384).transpose(1, 0, 2)
    attn = jnp.stack([attn0, attn1])
    grad_w_qkv = jnp.concatenate([attn[:, 1, :, None, :WIDTH], attn[:, 0].reshape(2, 24, 2, WIDTH)], axis=2)
    grad_w_out = attn[:, 1, :, WIDTH:].transpose(0, 2, 1)
    tiny = own[24:32, 0:48].reshape(8, 2, 24).transpose(1, 0, 2)
    return (
        ends[None],
        tiny[:, 0:2],
        tiny[:, 2:4],
        grad_w_qkv,
        grad_w_out,
        tiny[:, 4:8].transpose(0, 2, 1),
        full[:, :, 0],
        full[:, :, 1].transpose(0, 1, 3, 2),
    )


def solution(mesh):
    fine = Mesh(mesh.devices.reshape(4, 2, 2, 2, 4), CHIPS + ("core", "tp"))
    section, ctx = ("x", "zh"), ("zl", "core")
    every = section + ctx
    return jax.shard_map(
        shards,
        mesh=fine,
        in_specs=(
            P(ctx, section, None, None),
            P(ctx, section, None, None),
            P(),
            P(None, None, every),
            P(None, None, every),
            P(None, every, None, "tp"),
            P(None, "tp", every),
            P(None, every, None),
            P(None, None, every, "tp"),
            P(None, None, "tp", every),
        ),
        out_specs=(
            P(ctx, section, None, None),
            P(None, None, every),
            P(None, None, every),
            P(None, every, None, "tp"),
            P(None, "tp", every),
            P(None, every, None),
            P(None, None, every, "tp"),
            P(None, None, "tp", every),
        ),
        check_vma=False,
    )
```

time: 451 us -> 381 us (0.84)
  Pallas kernels: 321 us -> 271 us
  local copies, waits for them, and re-layouts: 37.4 us -> 26.9 us
  waiting for transfers between devices: 58.8 us -> 50.1 us
  starting transfers between devices: 7.52 us -> 0.51 us
  other arithmetic: 7.77 us -> 13.8 us
    pallas_call x26 -> x10, Pallas kernels: 308 us -> 237 us  [the longest x2 63.7 us: attend_backward(): pl.pallas_call(functools.partial(attend_backward_kernel, with_moe), out_s...]
    unnamed x6 -> x5, waiting for transfers between devices: 58.6 us -> 34.5 us
    pallas_call x1, Pallas kernels: 12.9 us -> 34.8 us  [start_exchange(): pl.pallas_call(start_kernel, out_shape=(jax.ShapeDtypeStruct((2,) + image...]
    unnamed x91 -> x40, local copies, waits for them, and re-layouts: 21.5 us -> 1.77 us
    all_gather x2 -> x1, waiting for transfers between devices: 0.01 us -> 15.6 us  [shards(): every = lax.all_gather(chip, CHIPS, axis=0)]
    ppermute x2 -> x0, starting transfers between devices: 6.94 us -> none  [the longest x1 4.59 us: shards(): lax.ppermute(sent, 'x', [(i, (i + 2) % 4) for i in range(4)]).astype(f32)]
  transfers between devices with their start and end apart: 6 -> 3, of which waited for: 2 -> 2; matrix products, arithmetic and copies ran while one was open for 4% -> 7% of each run, Pallas kernels for 49% -> 50%
where the time goes in v2:
time: 381 us; the launch traced here: 377 us
  Pallas kernels  271 us (71%)
  waiting for transfers between devices  50.1 us (13%)
  local copies, waits for them, and re-layouts  26.9 us (7%)
  between operations  14.8 us (4%)
  other arithmetic  13.8 us (4%)
    pallas_call x2, Pallas kernels, attend_backward(): pl.pallas_call(functools.partial(attend_backward_kernel, with_moe), out_s...  63.7 us
    pallas_call x2, Pallas kernels, attend_forward(): pl.pallas_call(functools.partial(attend_forward_kernel, bool(before)), ou...  58.2 us
    pallas_call x2, Pallas kernels, experts_backward(): pl.pallas_call(kernel, grid=(steps,), out_shape=[jax.ShapeDtypeStruct(s,...  56.2 us
    pallas_call x1, Pallas kernels, start_exchange(): pl.pallas_call(start_kernel, out_shape=(jax.ShapeDtypeStruct((2,) + image...  34.8 us
    unnamed x5, waiting for transfers between devices  34.5 us
    pallas_call x1, Pallas kernels, end_exchange(): pl.pallas_call(end_kernel, out_shape=(jax.ShapeDtypeStruct(shape, f32), j...  30.3 us
    pallas_call x1, Pallas kernels, experts_forward(): pl.pallas_call(experts_forward_kernel, grid=(EXPERTS,), out_shape=jax.Sha...  22.4 us
    all_gather x1, waiting for transfers between devices, shards(): every = lax.all_gather(chip, CHIPS, axis=0)  15.6 us
  transfers between devices with their start and end apart: 3, of which 2 were waited for; matrix products, arithmetic and copies ran while one was open for 7% of the time, Pallas kernels for 50%

profile of v2, /device:TPU:1, one launch (start us, length us, event | category | flops | bytes accessed | tf_op | source)
XLA Modules:
  0.0 377.5 jit_solution(3064522584372072196)
XLA Ops:
  8.0 1.1 pad_maximum_fusion.1
  10.0 1.2 constant_dynamic-slice_fusion.5
  12.1 2.8 cross.2
  18.1 34.8 %start_exchange.1 = (bf16[2,2,176,768]{3,2,1,0:T(8,128)(2,1)}, bf16[16,2,32,768]{3,2,1,0:T(8,128)(2,1)}) custom-call(bf16[2,176,768]{2,1,0:T(8,128)(2,1)} %fusion.3.images, bf16[32,768]{1,0:T(8,128)(2,1)} %fusion.8.own), custom_call_target="tpu_custom_call" | custom-call | tf_op jit(solution)/shard_map/start_exchange/pallas_call | solution.py:223
  60.0 1.1 fusion.16
  61.1 33.1 %attend_forward.2 = (bf16[160,192]{1,0:T(8,128)(2,1)}, bf16[4,160,384]{2,1,0:T(8,128)(2,1)}, bf16[160,192]{1,0:T(8,128)(2,1)}, bf16[2,4,80,384]{3,2,1,0:T(8,128)(2,1)}) custom-call(bf16[320,768]{1,0:T(8,128)(2,1)} %bitcast.127, f32[8,768]{1,0:T(8,128)} %reshape.287.refs_1_.small.refs_2_, bf16[768,384]{1,0:T(8,128)(2,1)} %bitcast.138, ...), custom_call_target="tpu_custom_call" | custom-call | tf_op jit(solution)/shard_map/attend_forward/pallas_call | solution.py:401
  95.1 15.6 %all-gather.2.cloned.1.call-done.weights.refs_5_.refs_6_ = bf16[16,864,384]{2,1,0:T(8,128)(2,1)} async-done(((bf16[1,864,384]{2,1,0:T(8,128)(2,1)}), bf16[16,864,384]{2,1,0:T(8,128)(2,1)}) %all-gather.2.cloned.1.call-update) | async-done | bytes 10616848 | tf_op jit(solution)/shard_map/all_gather | solution.py:749
  110.7 2.4 fusion.15
  113.0 22.4 %experts_forward.1.refs_2_ = bf16[2,4,80,384]{3,2,1,0:T(8,128)(2,1)} custom-call(bf16[320,768]{1,0:T(8,128)(2,1)} %bitcast.128, bf16[2,4,80,384]{3,2,1,0:T(8,128)(2,1)} %get-tuple-element.36.att.refs_1_, f32[8,768]{1,0:T(8,128)} %reshape.287.refs_1_.small.refs_2_, f32[320,2]{1,0:T(8,128)} %copy.89.routes.refs_3_, ...), custom_call_target="tpu_custom_call" | custom-call | tf_op jit(solution)/shard_map/experts_forward/pallas_call | solution.py:466
  135.4 25.1 %attend_forward.3 = (bf16[160,192]{1,0:T(8,128)(2,1)}, bf16[4,160,384]{2,1,0:T(8,128)(2,1)}, bf16[160,192]{1,0:T(8,128)(2,1)}, bf16[2,4,80,384]{3,2,1,0:T(8,128)(2,1)}, bf16[320,768]{1,0:T(8,128)(2,1)}) custom-call(bf16[320,768]{1,0:T(8,128)(2,1)} %bitcast.129, bf16[2,4,80,384]{3,2,1,0:T(8,128)(2,1)} %get-tuple-element.36.att.refs_1_, ...), custom_call_target="tpu_custom_call" | custom-call | tf_op jit(solution)/shard_map/attend_forward/pallas_call | solution.py:401
  160.6 28.6 %experts_backward.2 = (bf16[2,4,96,384]{3,2,1,0:T(8,128)(2,1)}, bf16[2,4,80,384]{3,2,1,0:T(8,128)(2,1)}, bf16[16,384,384]{2,1,0:T(8,128)(2,1)}) custom-call(bf16[320,768]{1,0:T(8,128)(2,1)} %get-tuple-element.37.refs_0_, bf16[2,4,80,384]{3,2,1,0:T(8,128)(2,1)} %get-tuple-element.38.refs_1_, f32[8,768]{1,0:T(8,128)} %reshape.289.refs_3_.refs_2_, ...), custom_call_target="tpu_custom_call" | custom-call | tf_op jit(solution)/shard_map/experts_backward/pallas_call | solution.py:573
  189.5 33.4 %attend_backward.2 = (bf16[320,768]{1,0:T(8,128)(2,1)}, f32[8,768]{1,0:T(8,128)}, bf16[2,768,384]{2,1,0:T(8,128)(2,1)}, bf16[4,80,384]{2,1,0:T(8,128)(2,1)}) custom-call(bf16[320,768]{1,0:T(8,128)(2,1)} %get-tuple-element.37.refs_0_, bf16[2,4,80,384]{3,2,1,0:T(8,128)(2,1)} %get-tuple-element.38.refs_1_, f32[8,768]{1,0:T(8,128)} %reshape.289.refs_3_.refs_2_, ...), custom_call_target="tpu_custom_call" | custom-call | tf_op jit(solution)/shard_map/attend_backward/pallas_call | solution.py:716
  222.9 27.5 %experts_backward.3 = (bf16[2,4,96,384]{3,2,1,0:T(8,128)(2,1)}, bf16[16,480,384]{2,1,0:T(8,128)(2,1)}) custom-call(bf16[320,768]{1,0:T(8,128)(2,1)} %bitcast.130, bf16[2,4,80,384]{3,2,1,0:T(8,128)(2,1)} %get-tuple-element.36.att.refs_1_, f32[8,768]{1,0:T(8,128)} %reshape.287.refs_1_.small.refs_2_, f32[320,2]{1,0:T(8,128)} %copy.89.routes.refs_3_, ...), custom_call_target="tpu_custom_call" | custom-call | tf_op jit(solution)/shard_map/experts_backward/pallas_call | solution.py:573
  252.6 30.4 %attend_backward.3 = (bf16[320,768]{1,0:T(8,128)(2,1)}, f32[8,768]{1,0:T(8,128)}, bf16[2,768,384]{2,1,0:T(8,128)(2,1)}) custom-call(bf16[320,768]{1,0:T(8,128)(2,1)} %bitcast.131, bf16[2,4,80,384]{3,2,1,0:T(8,128)(2,1)} %get-tuple-element.36.att.refs_1_, f32[8,768]{1,0:T(8,128)} %reshape.287.refs_1_.small.refs_2_, f32[2,320]{1,0:T(2,128)} %copy-done.10, ...), custom_call_target="tpu_custom_call" | custom-call | tf_op jit(solution)/shard_map/attend_backward/pallas_call | solution.py:716
  283.0 2.5 copy.115
  287.3 1.0 dynamic-slice_convert_fusion.1
  289.3 1.4 fusion.1.part
  290.7 1.7 constant_dynamic-slice_fusion.1
  292.3 30.3 %end_exchange.1 = (f32[32,768]{1,0:T(8,128)}, bf16[160,768]{1,0:T(8,128)(2,1)}, bf16[192,384]{1,0:T(8,128)(2,1)}) custom-call(bf16[2,16,32,768]{3,2,1,0:T(8,128)(2,1)} %fusion.1.part, bf16[160,768]{1,0:T(8,128)(2,1)} %fusion.4.image, bf16[192,384]{1,0:T(8,128)(2,1)} %bitcast.156), custom_call_target="tpu_custom_call" | custom-call | tf_op jit(solution)/shard_map/end_exchange/pallas_call | solution.py:282
  324.3 1.0 broadcast_select_fusion.3
  325.4 1.0 maximum_select_fusion.1
  327.6 34.5 %reduce-scatter.9.cloned.1.call-done = bf16[1,480,384]{2,1,0:T(8,128)(2,1)} async-done(((bf16[16,480,384]{2,1,0:T(8,128)(2,1)}), bf16[1,480,384]{2,1,0:T(8,128)(2,1)}) %reduce-scatter.9.cloned.1.call-update) | async-done | bytes 368656
  363.0 2.9 cross.3
  368.6 1.1 slice_bitcast_fusion
  (129 shorter events, 25.8 us)
Async XLA Ops:
  7.2 103.5 %all-gather.2.cloned.1.call-start = ((), (), s32[]{:S(2)}) async-start(), calls=%async_computation.2 | async-start | bytes 11280384 | tf_op jit(solution)/shard_map/all_gather | solution.py:749
  9.1 0.8 slice-start
  11.2 0.7 copy-start.9
  15.1 1.2 copy-start.8
  15.1 1.4 copy-start.15
  15.1 1.3 copy-start.16
  15.1 1.3 copy-start.17
  15.1 2.2 copy-start.14
  15.1 2.2 copy-start.4
  16.1 274.6 %reduce-scatter.7.cloned.1.call-start = ((), (), s32[]{:S(2)}) async-start(), calls=%async_computation.3 | async-start | bytes 5013504
  17.3 37.6 %copy-start.18 = (s32[4]{0:T(128)S(1)}, s32[4]{0:T(128)}, u32[]{:S(2)}) copy-start(s32[4]{0:T(128)} %param.12) | copy-start | bytes 52
  52.9 6.2 %copy-start.3 = (bf16[2,2,176,768]{3,2,1,0:T(8,128)(2,1)S(1)}, bf16[2,2,176,768]{3,2,1,0:T(8,128)(2,1)}, u32[]{:S(2)}) copy-start(bf16[2,2,176,768]{3,2,1,0:T(8,128)(2,1)} %get-tuple-element.34) | copy-start | bytes 3244036
  56.4 3.6 copy-start.10
  56.4 3.6 copy-start.2
  58.3 2.8 copy-start.11
  189.2 172.8 %reduce-scatter.9.cloned.1.call-start = ((), (), s32[]{:S(2)}) async-start(), calls=%async_computation.4 | async-start | bytes 6266880
  250.4 0.9 copy-start.6
  250.5 1.5 copy-start.1
  285.5 0.8 copy-start.13
  285.5 1.1 copy-start.12
  286.3 2.0 copy-start
  290.7 33.7 %copy-start.5 = (bf16[1,384,384]{2,1,0:T(8,128)(2,1)S(1)}, bf16[1,384,384]{2,1,0:T(8,128)(2,1)}, u32[]{:S(2)}) copy-start(bf16[1,384,384]{2,1,0:T(8,128)(2,1)} %reduce-scatter.7.cloned.1.call-done) | copy-start | bytes 884740
  322.6 2.7 copy-start.7
Sparse Core Ops, SparseCore 0:
  16.2 94.4 all-gather.1
  189.4 76.1 reduce-scatter.6
  268.9 93.0 reduce-scatter.8

commit v3 on v2

--- a/solution.py
+++ b/solution.py
@@ -64,24 +64,28 @@
     )
 
 
-def sum_peers(both):
-    core, tp = lax.axis_index("core"), lax.axis_index("tp")
-    offsets = [(k // 4, k % 4) for k in range(1, 8 if both else 4)]
-    return [{"core": (core + dc) % 2, "tp": (tp + dt) % 4} for dc, dt in offsets]
+def tp_peers():
+    return [{"tp": (lax.axis_index("tp") + k) % 4} for k in (1, 2, 3)]
+
+
+def sum_cores(part, crossed, send, recv):
+    core = lax.axis_index("core")
+    return remote(part.at[1 - core], crossed, send.at[0], recv.at[0], {"core": 1 - core})
 
 
 def sum_terms(both, part, landed, send, recv):
+    block = lax.axis_index("core") if both else 0
     return [
-        remote(part.at[peer["core"] if both else 0, peer["tp"]], landed.at[k], send.at[k], recv.at[k], peer)
-        for k, peer in enumerate(sum_peers(both))
+        remote(part.at[block, peer["tp"]], landed.at[k], send.at[k], recv.at[k], peer)
+        for k, peer in enumerate(tp_peers())
     ]
 
 
 def sum_results(out, send, recv):
     core, tp = lax.axis_index("core"), lax.axis_index("tp")
     return [
-        remote(out.at[core, tp], out.at[core, tp], send.at[k], recv.at[k], {"tp": (tp + k + 1) % 4})
-        for k in range(3)
+        remote(out.at[core, tp], out.at[core, tp], send.at[k], recv.at[k], peer)
+        for k, peer in enumerate(tp_peers())
     ]
 
 
@@ -93,12 +97,19 @@
     ]
 
 
-def sum_start(both, part, out, landed, rs, rr, gs, gr, cs, cr):
+def sum_start(both, out, part, landed, rs, rr, gs, gr, cs, cr, crossed=None, ps=None, pr=None):
+    if both:
+        core = lax.axis_index("core")
+        pre = sum_cores(part, crossed, ps, pr)
+        pre.start()
+        pre.wait_recv()
+        for j in range(4):
+            part[core, j] = (part[core, j].astype(f32) + crossed[j].astype(f32)).astype(bf16)
     for copy in sum_terms(both, part, landed, rs, rr):
         copy.start()
 
 
-def sum_middle(both, part, out, landed, rs, rr, gs, gr, cs, cr):
+def sum_middle(both, out, part, landed, rs, rr, gs, gr, cs, cr, *pre):
     core, tp = lax.axis_index("core"), lax.axis_index("tp")
     total = part[core if both else 0, tp].astype(f32)
     for k, copy in enumerate(sum_terms(both, part, landed, rs, rr)):
@@ -109,7 +120,7 @@
         copy.start()
 
 
-def sum_end(both, part, out, landed, rs, rr, gs, gr, cs, cr):
+def sum_end(both, out, part, landed, rs, rr, gs, gr, cs, cr, *pre):
     gathers, crosses = sum_results(out, gs, gr), sum_cross(out, cs, cr)
     for k in range(4):
         if k > 0:
@@ -119,21 +130,23 @@
         copy.wait()
     for copy in sum_terms(both, part, landed, rs, rr) + gathers:
         copy.wait_send()
+    if both:
+        sum_cores(part, *pre).wait_send()
 
 
 def sum_scratch(both, rows):
-    count = 7 if both else 3
-    return [
+    scratch = [
         pltpu.VMEM((2 if both else 1, 4, rows, 384), bf16),
-        pltpu.VMEM((count, rows, 384), bf16),
-    ] + dma_sems(count, 3, 4)
-
-
-def ctx_peers():
+        pltpu.VMEM((3, rows, 384), bf16),
+    ] + dma_sems(3, 3, 4)
+    if both:
+        scratch += [pltpu.VMEM((4, rows, 384), bf16)] + dma_sems(1)
+    return scratch
+
+
+def chip_peers():
     core, zl = lax.axis_index("core"), lax.axis_index("zl")
-    return [
-        {"zl": (zl + k // 2) % 2, "core": (core + k % 2) % 2} for k in range(1, 4)
-    ], zl * 2 + core
+    return {"core": 1 - core}, {"zl": 1 - zl}, zl * 2 + core
 
 
 def chip_peer(k):
@@ -165,77 +178,192 @@
     )(own)
 
 
-def start_kernel(images, own, out_images, out, im_send, im_recv, send, recv, cx_send, cx_recv):
-    core, x = lax.axis_index("core"), lax.axis_index("x")
-    high = x // 2
+def places():
+    return lax.axis_index("x"), lax.axis_index("zh") * 2 + lax.axis_index("zl")
+
+
+def axis_peer(along_x, k):
+    x, z = places()
+    if along_x:
+        return {"x": (x + k) % 4}, (x + k) % 4
+    to = (z + k) % 4
+    return {"zh": to // 2, "zl": to % 2}, to
+
+
+def half(rows, route):
+    return pl.ds(route * (rows // 2), rows // 2)
+
+
+def line(whole, route, second, rows):
+    return whole.at[:, second, rows] if route == 0 else whole.at[second, :, rows]
+
+
+def axis_peers(*ks):
+    return [axis_peer(along_x, k)[0] for along_x in (True, False) for k in ks]
+
+
+def start_kernel(
+    images, urgent, later, out_images, all_urgent, all_later, own_sem, im_s, im_r, u1_s, u1_r, u2_s, u2_r, l_s, l_r
+):
+    core = lax.axis_index("core")
+    at_x, at_z = places()
+    high = at_x // 2
     other = {"core": 1 - core}
-    _, me, _ = chip_peer(0)
-    arrive([chip_peer(k)[0] for k in range(1, 16)] + [other])
-    out[me, core] = own[...]
+    arrive(axis_peers(1, 2, 3) + [other])
+    all_urgent[at_x, at_z] = urgent[...]
     out_images[core, high] = images[high]
-    all_here(16)
-
-    def push(k):
-        peer, _, _ = chip_peer(k)
-        return remote(own, out.at[me, core], send.at[k], recv.at[k], peer)
-
-    def pass_on(k):
-        _, _, at = chip_peer(k)
-        return remote(out.at[at, core], out.at[at, core], cx_send.at[k], cx_recv.at[k], other)
-
-    swap = remote(
-        images.at[1 - high], out_images.at[core, high], im_send.at[0], im_recv.at[0], {"x": (x + 2) % 4}
-    )
-    kept = remote(images.at[high], out_images.at[core, high], im_send.at[1], im_recv.at[1], other)
-    swap.start()
-
-    def first(k, carry):
-        push(k).start()
-        return carry
-
-    def onward(k, carry):
-        push(k).wait_recv()
-        pass_on(k).start()
-        return carry
-
-    def last(k, carry):
-        push(k).wait_send()
-        pass_on(k).wait()
-        return carry
-
-    lax.fori_loop(1, 16, first, 0)
-    kept.start()
-    pass_on(0).start()
+    own = pltpu.make_async_copy(later, all_later.at[at_x, at_z], own_sem)
+    own.start()
+    all_here(7)
+    firsts, seconds, laters = [], [], []
+    for route in range(2):
+        b = (at_z, at_x)[route]
+        rows, late = half(urgent.shape[0], route), half(later.shape[0], route)
+        for k in range(1, 4):
+            peer, _ = axis_peer(route == 0, k)
+            n = 3 * route + k - 1
+            firsts.append(
+                remote(urgent.at[rows], all_urgent.at[at_x, at_z, rows], u1_s.at[n], u1_r.at[n], peer)
+            )
+            laters.append(
+                remote(later.at[late], all_later.at[at_x, at_z, late], l_s.at[n], l_r.at[n], peer)
+            )
+            slabs = line(all_urgent, route, b, rows)
+            seconds.append(remote(slabs, slabs, u2_s.at[n], u2_r.at[n], axis_peer(route == 1, k)[0]))
+    swap = remote(images.at[1 - high], out_images.at[core, high], im_s.at[0], im_r.at[0], {"x": (at_x + 2) % 4})
+    kept = remote(images.at[high], out_images.at[core, high], im_s.at[1], im_r.at[1], other)
+    passed = remote(
+        out_images.at[core, 1 - high], out_images.at[core, 1 - high], im_s.at[2], im_r.at[2], other
+    )
+    for copy in firsts + [swap, kept]:
+        copy.start()
+    for copy in firsts:
+        copy.wait_recv()
+    for copy in seconds + laters:
+        copy.start()
     swap.wait_recv()
-    passed = remote(
-        out_images.at[core, 1 - high], out_images.at[core, 1 - high], im_send.at[2], im_recv.at[2], other
-    )
     passed.start()
-    lax.fori_loop(1, 16, onward, 0)
-    pass_on(0).wait()
-    lax.fori_loop(1, 16, last, 0)
-    for copy in (kept, passed):
+    for copy in seconds + laters + [kept, passed]:
         copy.wait()
-    swap.wait_send()
-
-
-def start_exchange(images, own):
+    for copy in firsts + [swap]:
+        copy.wait_send()
+    own.wait()
+
+
+def start_exchange(images, urgent, later):
     return pl.pallas_call(
         start_kernel,
-        out_shape=(
-            jax.ShapeDtypeStruct((2,) + images.shape, bf16),
-            jax.ShapeDtypeStruct((16, 2) + own.shape, bf16),
-        ),
-        in_specs=[VMEM, VMEM],
-        out_specs=(VMEM, VMEM),
-        scratch_shapes=dma_sems(3, 16, 16),
+        out_shape=[
+            jax.ShapeDtypeStruct(s, bf16)
+            for s in ((2,) + images.shape, (4, 4) + urgent.shape, (4, 4) + later.shape)
+        ],
+        in_specs=[VMEM] * 3,
+        out_specs=[VMEM, VMEM, pl.BlockSpec(memory_space=pl.ANY)],
+        scratch_shapes=[pltpu.SemaphoreType.DMA] + dma_sems(3, 6, 6, 6),
         compiler_params=params(1, 56),
         name="start_exchange",
-    )(images, own)
+    )(images, urgent, later)
+
+
+def spread_near(whole, send, recv):
+    copies = []
+    for route in range(2):
+        slabs = line(whole, route, places()[1 - route], half(whole.shape[2], route))
+        for n, k in enumerate((1, 3)):
+            at, peer = 2 * route + n, axis_peer(route == 1, k)[0]
+            copies.append(remote(slabs, slabs, send.at[at], recv.at[at], peer))
+    return copies
+
+
+def spread_far(whole, send, recv):
+    copies = []
+    size = whole.shape[2] // 2
+    cut = size // 32 * 16 + size % 32
+    for route in range(2):
+        b = places()[1 - route]
+        for n, k in enumerate((1, 3)):
+            rows = pl.ds(route * size + n * cut, size - cut if n else cut)
+            slabs = line(whole, route, (b + 4 - k) % 4, rows)
+            at, peer = 4 + 2 * route + n, axis_peer(route == 1, k)[0]
+            copies.append(remote(slabs, slabs, send.at[at], recv.at[at], peer))
+    return copies
+
+
+def part_rows(rows, route, n):
+    size = rows // 2
+    cut = size // 32 * 16 + size % 32
+    return pl.ds(route * size + n * cut, size - cut if n else cut)
+
+
+def toward_far(whole, passing, route, send, recv):
+    copies, b = [], places()[1 - route]
+    for n, k in enumerate((1, 3)):
+        rows = part_rows(whole.shape[2], route, n)
+        target = passing.at[route, n, :, 0 : rows.size]
+        at, peer = 2 * route + n, axis_peer(route == 1, k)[0]
+        copies.append(remote(line(whole, route, (b + 2) % 4, rows), target, send.at[at], recv.at[at], peer))
+    return copies
+
+
+def toward_near(whole, passing, landed, route, send, recv):
+    copies, b = [], places()[1 - route]
+    for n, k in enumerate((1, 3)):
+        rows, others = (part_rows(whole.shape[2], route, m) for m in (n, 1 - n))
+        at, peer = 4 * route + 2 * n, axis_peer(route == 1, k)[0]
+        copies += [
+            remote(passing.at[route, n, :, 0 : rows.size], landed.at[n, :, rows], send.at[at], recv.at[at], peer),
+            remote(
+                line(whole, route, (b + k) % 4, others), landed.at[n, :, others],
+                send.at[at + 1], recv.at[at + 1], peer,
+            ),
+        ]
+    return copies
+
+
+def add_passing(whole, passing, route):
+    x, z = places()
+    b = (z, x)[route]
+    for n, k in enumerate((1, 3)):
+        rows, to = part_rows(whole.shape[2], route, n), (b + k) % 4
+
+        def add(j, carry, n=n, rows=rows, to=to):
+            own = whole[j, to, rows] if route == 0 else whole[to, j, rows]
+            total = passing[route, n, j, 0 : rows.size].astype(f32) + own.astype(f32)
+            passing[route, n, j, 0 : rows.size] = total.astype(bf16)
+            return carry
+
+        lax.fori_loop(0, 4, add, 0)
+
+
+def last_copies(some, slabs, send, recv):
+    copies = []
+    for route in range(2):
+        rows = half(some.shape[1], route)
+        for k in range(1, 4):
+            peer, at = axis_peer(route == 0, k)
+            n = 3 * route + k - 1
+            copies.append(remote(some.at[at, rows], slabs.at[k - 1, rows], send.at[n], recv.at[n], peer))
+    return copies
+
+
+def add_slabs(some, slabs, out):
+    x, z = places()
+    steps = out.shape[0] // 48
+
+    def add(i, carry):
+        rows, route = pl.ds(pl.multiple_of(i * 48, 48), 48), i // (steps // 2)
+        total = some[x * (1 - route) + z * route, rows].astype(f32)
+        for k in range(3):
+            total = total + slabs[k, rows].astype(f32)
+        out[rows] = total.astype(bf16)
+        return carry
+
+    lax.fori_loop(0, steps, add, 0)
 
 
 def end_kernel(
-    part, image, half, out, out_image, out_half, landed, sums, pieces, cx_s, cx_r, send, recv
+    part, image, half, some, out, out_image, out_half, own_sum, other_sum,
+    landed, sums, pieces, total, slabs, cx_s, cx_r, sl_s, sl_r, send, recv,
 ):
     core, x = lax.axis_index("core"), lax.axis_index("x")
     other = {"core": 1 - core}
@@ -244,10 +372,9 @@
     all_here(16)
     crossing = remote(part.at[1 - core], landed, cx_s.at[0], cx_r.at[0], other)
     crossing.start()
-    swap = remote(image, out_image, cx_s.at[1], cx_r.at[1], {"x": (x + 2) % 4})
-    swap.start()
-    halves = remote(half, out_half, cx_s.at[2], cx_r.at[2], other)
-    halves.start()
+    lasts = last_copies(some, slabs, sl_s, sl_r)
+    for copy in lasts:
+        copy.start()
     crossing.wait()
 
     def push(k):
@@ -262,7 +389,7 @@
 
     def collect(k, carry):
         push(k).wait_recv()
-        out[...] += pieces[k].astype(f32)
+        total[...] += pieces[k].astype(f32)
         return carry
 
     def last(k, carry):
@@ -270,28 +397,39 @@
         return carry
 
     lax.fori_loop(1, 16, add, 0)
-    out[...] = part[core, me].astype(f32) + landed[me].astype(f32)
+    swap = remote(image, out_image, cx_s.at[1], cx_r.at[1], {"x": (x + 2) % 4})
+    swap.start()
+    halves = remote(half, out_half, cx_s.at[2], cx_r.at[2], other)
+    halves.start()
+    total[...] = part[core, me].astype(f32) + landed[me].astype(f32)
     lax.fori_loop(1, 16, collect, 0)
+    out[core] = total[...]
+    given = remote(out.at[core], out.at[core], cx_s.at[4], cx_r.at[4], other)
+    given.start()
+    for copy in lasts:
+        copy.wait()
+    add_slabs(some, slabs, own_sum)
+    final = remote(own_sum, other_sum, cx_s.at[3], cx_r.at[3], other)
+    final.start()
     lax.fori_loop(1, 16, last, 0)
-    swap.wait()
-    halves.wait()
-
-
-def end_exchange(part, image, half):
-    shape = part.shape[2:]
+    for copy in (given, final, swap, halves):
+        copy.wait()
+
+
+def end_exchange(part, image, half, some):
+    shape, slab = part.shape[2:], some.shape[1:]
     return pl.pallas_call(
         end_kernel,
-        out_shape=(
-            jax.ShapeDtypeStruct(shape, f32),
-            jax.ShapeDtypeStruct(image.shape, bf16),
-            jax.ShapeDtypeStruct(half.shape, bf16),
-        ),
-        in_specs=[VMEM] * 3,
-        out_specs=(VMEM,) * 3,
-        scratch_shapes=[pltpu.VMEM((16,) + shape, bf16)] * 3 + dma_sems(3, 16),
+        out_shape=[jax.ShapeDtypeStruct((2,) + shape, f32)]
+        + [jax.ShapeDtypeStruct(s, bf16) for s in (image.shape, half.shape, slab, slab)],
+        in_specs=[VMEM] * 4,
+        out_specs=[VMEM] * 5,
+        scratch_shapes=[pltpu.VMEM((16,) + shape, bf16)] * 3
+        + [pltpu.VMEM(shape, f32), pltpu.VMEM((3,) + slab, bf16)]
+        + dma_sems(5, 6, 16),
         compiler_params=params(2, 56),
         name="end_exchange",
-    )(part, image, half)
+    )(part, image, half, some)
 
 
 def block_rows(ref, block):
@@ -350,33 +488,51 @@
     return 0.5 * (1.0 + t) + 0.5 * u * (1.0 - t * t) * (c * (1.0 + 3 * 0.044715 * u * u))
 
 
+def attn_weights(weights):
+    w_kv = weights[:, 0:48].reshape(D, 2 * WIDTH)
+    w_q = weights[:, 48:96, :WIDTH].reshape(D, WIDTH)
+    return w_kv, w_q, weights[:, 48:96, WIDTH:].reshape(D, WIDTH)
+
+
 def attend_forward_kernel(follows, *refs):
     if follows:
-        x, att_before, moe_before, small, w_kv, w_qo, dead, q, kv, mixed, att, x_next, *scratch = refs
+        x, att_before, moe_before, small, weights, dead, q, kv, mixed, att, x_next, *scratch = refs
     else:
-        x, small, w_kv, w_qo, dead, q, kv, mixed, att, *scratch = refs
+        x, small, weights, dead, _, q, kv, mixed, att, whole, *scratch = refs
+        *scratch, sp_send, sp_recv = scratch
     part, landed, *sems, kv_send, kv_recv = scratch
-    sums = (False, part, att, landed, *sems)
+    sums = (False, att, part, landed, *sems)
     core = lax.axis_index("core")
-    peers, me = ctx_peers()
-    arrive(peers + sum_peers(False))
+    other, across, me = chip_peers()
+    arrive([other, across] + tp_peers())
+    if not follows:
+        arrive(axis_peers(1, 3))
     if follows:
         x_next[...] = (x[...].astype(f32) + pair_rows(att_before) + pair_rows(moe_before)).astype(bf16)
         x = x_next
     unit, _ = norm_parts(x[own_rows(core)].astype(f32))
     normed = (unit * small[0:1] + small[2:3]).astype(bf16)
-    kv[me] = dot(normed, w_kv[...], NN).astype(bf16)
-    all_here(6)
+    w_kv, w_q, w_out_t = attn_weights(weights)
+    kv[me] = dot(normed, w_kv, NN).astype(bf16)
+    all_here(5 if follows else 9)
+    far = (me + 2) % 4
     copies = [
-        remote(kv.at[me], kv.at[me], kv_send.at[k], kv_recv.at[k], peer)
-        for k, peer in enumerate(peers)
+        remote(kv.at[at], kv.at[at], kv_send.at[k], kv_recv.at[k], peer)
+        for k, (at, peer) in enumerate(((me, across), (me, other), (far, other)))
     ]
-    for copy in copies:
-        copy.start()
-    queries = dot(normed, w_qo[:, :WIDTH], NN).astype(bf16)
+    copies[0].start()
+    copies[1].start()
+    if not follows:
+        nears = spread_near(whole, sp_send, sp_recv)
+        fars = spread_far(whole, sp_send, sp_recv)
+        for copy in nears:
+            copy.start()
+    queries = dot(normed, w_q, NN).astype(bf16)
     q[...] = queries
-    for copy in copies:
-        copy.wait_recv()
+    copies[0].wait_recv()
+    copies[2].start()
+    copies[1].wait_recv()
+    copies[2].wait_recv()
     keys = kv[...].reshape(KEYS, 2 * WIDTH)
     outs = []
     for h in range(HEADS):
@@ -385,25 +541,44 @@
         outs.append(dot(probs, head(keys, HEADS + h), NN))
     heads = jnp.concatenate(outs, axis=1).astype(bf16)
     mixed[...] = heads
-    put_chunks(part, 0, dot(heads, w_qo[:, WIDTH:], NT).astype(bf16))
+    put_chunks(part, 0, dot(heads, w_out_t, NT).astype(bf16))
     sum_start(*sums)
     sum_middle(*sums)
+    if not follows:
+        for copy in nears:
+            copy.wait_recv()
+        for copy in fars:
+            copy.start()
     sum_end(*sums)
     for copy in copies:
         copy.wait_send()
-
-
-def attend_forward(x, before, small, w_kv, w_qo, dead, cid):
-    args = (x, *before, small, w_kv, w_qo, dead)
+    if not follows:
+        for copy in fars:
+            copy.wait()
+        for copy in nears:
+            copy.wait_send()
+
+
+def attend_forward(x, before, small, weights, dead, some, cid):
+    args = (x, *before, small, weights, dead)
     shapes = [(ROWS, WIDTH), (4, ROWS, 2 * WIDTH), (ROWS, WIDTH), (2, 4, 80, 384)]
+    in_specs, out_specs = [VMEM] * len(args), [VMEM] * 5
+    scratch = sum_scratch(False, 80) + dma_sems(3)
     if before:
         shapes.append((PAIR, D))
+    else:
+        args += (some,)
+        shapes.append(some.shape)
+        in_specs.append(pl.BlockSpec(memory_space=pl.ANY))
+        out_specs[4] = pl.BlockSpec(memory_space=pl.ANY)
+        scratch += dma_sems(8)
     return pl.pallas_call(
         functools.partial(attend_forward_kernel, bool(before)),
         out_shape=[jax.ShapeDtypeStruct(s, bf16) for s in shapes],
-        in_specs=[VMEM] * len(args),
-        out_specs=[VMEM] * len(shapes),
-        scratch_shapes=sum_scratch(False, 80) + dma_sems(3),
+        in_specs=in_specs,
+        out_specs=out_specs,
+        scratch_shapes=scratch,
+        input_output_aliases={} if before else {len(args) - 1: 4},
         compiler_params=params(cid, 56),
         name="attend_forward",
     )(*args)
@@ -432,11 +607,11 @@
     x, att, small, routes, weights, result, b, gates, total, out, part, landed, *sems
 ):
     expert = pl.program_id(0)
-    sums = (True, part, out, landed, *sems)
+    sums = (True, out, part, landed, *sems)
 
     @pl.when(expert == 0)
     def _():
-        arrive(sum_peers(True))
+        arrive(tp_peers() + [{"core": 1 - lax.axis_index("core")}])
         experts_setup(x, att, small, routes, b, gates)
         total[...] = jnp.zeros_like(total)
 
@@ -450,7 +625,7 @@
     def _():
         for block in range(2):
             put_chunks(part, block, total[ROWS * block : ROWS * block + ROWS].astype(bf16))
-        all_here(7)
+        all_here(4)
         sum_start(*sums)
         sum_middle(*sums)
         sum_end(*sums)
@@ -482,16 +657,21 @@
 
 
 def experts_backward_kernel(
-    steps, x, att, small, routes, grad, extra, weights, result, moe_part, grad_w,
+    steps, x, att, small, routes, grad, extra, some, weights, result, moe_part, own_sum, grad_w,
     b, gates, total, moe, gate_t, gated_all, grad_u_all, out, part, landed, *sems,
 ):
     step = pl.program_id(0)
-    sums = (True, part, out, landed, *sems)
+    sums = (True, out, part, landed, *sems)
     with_moe = moe_part is not None
+    if not with_moe:
+        *sems, slabs, slab_send, slab_recv = sems
+        sums, lasts = (True, out, part, landed, *sems), last_copies(some, slabs, slab_send, slab_recv)
 
     @pl.when(step == 0)
     def _():
-        arrive(sum_peers(True))
+        arrive(tp_peers() + [{"core": 1 - lax.axis_index("core")}])
+        if not with_moe:
+            arrive(axis_peers(1, 2, 3))
         experts_setup(x, att, small, routes, b, gates)
         total[...] = jnp.zeros_like(total)
         if with_moe:
@@ -526,8 +706,11 @@
             part[block, 0, 80:96, 0:ROWS] = table.astype(bf16)
             if with_moe:
                 put_chunks(moe_part, block, moe[lines].astype(bf16))
-        all_here(7)
+        all_here(4 if with_moe else 10)
         sum_start(*sums)
+        if not with_moe:
+            for copy in lasts:
+                copy.start()
 
     @pl.when((step >= EXPERTS) & (step < 2 * EXPERTS))
     def _():
@@ -550,24 +733,33 @@
     def _():
         sum_end(*sums)
         result[...] = out[...]
-
-
-def experts_backward(x, att, small, routes, grad, extra, weights, first, cid):
+        if not with_moe:
+            for copy in lasts:
+                copy.wait()
+            add_slabs(some, slabs, own_sum)
+
+
+def experts_backward(x, att, small, routes, grad, extra, some, weights, cid):
     args = (x, att, small, routes, grad)
     steps = 2 * EXPERTS
     shapes = [(2, 4, 96, 384)]
     blocks = [fixed((2, 4, 96, 384))]
+    scratch = []
     if extra is None:
         shapes.append((2, 4, 80, 384))
         blocks.append(fixed((2, 4, 80, 384)))
 
         def kernel(*refs):
-            experts_backward_kernel(steps, *refs[:5], None, *refs[5:])
+            experts_backward_kernel(steps, *refs[:5], None, None, *refs[5:8], None, *refs[8:])
     else:
-        args, steps = args + (extra,), steps + 1
+        args, steps = args + (extra, some), steps + 1
+        slab = some.shape[1:]
+        shapes.append(slab)
+        blocks.append(fixed(slab))
+        scratch = [pltpu.VMEM((3,) + slab, bf16)] + dma_sems(6)
 
         def kernel(*refs):
-            experts_backward_kernel(steps, *refs[:8], None, *refs[8:])
+            experts_backward_kernel(steps, *refs[:9], None, *refs[9:])
 
     grads = steps - EXPERTS
     return pl.pallas_call(
@@ -575,7 +767,7 @@
         grid=(steps,),
         out_shape=[jax.ShapeDtypeStruct(s, bf16) for s in shapes + [(16, 96 * grads, FE)]],
         in_specs=[fixed(a.shape) for a in args]
-        + [pl.BlockSpec((16, 96, FE), lambda s: (0, first + jnp.minimum(s, EXPERTS - 1), 0))],
+        + [pl.BlockSpec((16, 96, FE), lambda s: (0, jnp.minimum(s, EXPERTS - 1), 0))],
         out_specs=blocks + [pl.BlockSpec((16, 96, FE), lambda s: (0, jnp.maximum(s - EXPERTS, 0), 0))],
         scratch_shapes=[
             pltpu.VMEM((PAIR, D), bf16),
@@ -587,67 +779,95 @@
             pltpu.VMEM((EXPERTS, PAIR, FE), bf16),
             pltpu.VMEM((2, 4, 96, 384), bf16),
         ]
-        + sum_scratch(True, 96),
+        + sum_scratch(True, 96)
+        + scratch,
         compiler_params=params(cid, 56),
         name="experts_backward",
     )(*args, weights)
 
 
 def attend_backward_kernel(with_moe, *refs):
-    x, att, small, routes_t, grad, back, q, kv, mixed, dead, w_kv, w_qo, *refs = refs
+    x, att, small, routes_t, grad, back, q, kv, mixed, dead, weights, whole, *refs = refs
     if with_moe:
         moe_part, *refs = refs
-    grad_x, grad_small, grad_w, *refs = refs
+    grad_x, grad_small, grad_w, some, *refs = refs
     if with_moe:
         moe, *refs = refs
     grad_h, both_units, parts, kv_landed, back_one, part, landed, *sems = refs
     if with_moe:
-        *sems, moe_landed, ms, mr, ns, nr = sems
-    *sems, kv_send, kv_recv = sems
-    sums = (False, part, back_one, landed, *sems)
+        *sems, moe_landed, ms, mr, ns, nr, moe_crossed, ps, pr = sems
+        moe_sums = (moe_part, moe_crossed, ps, pr)
+    *sems, slabs, passing, fs, fr, ns2, nr2, kv_out, kv_send, kv_recv = sems
+    fars = [toward_far(whole, passing, route, fs, fr) for route in range(2)]
+    nears = [toward_near(whole, passing, slabs, route, ns2, nr2) for route in range(2)]
+    sums = (False, back_one, part, landed, *sems)
     core, tp = lax.axis_index("core"), lax.axis_index("tp")
-    peers, me = ctx_peers()
-    arrive(peers + sum_peers(False) + (sum_peers(True)[4:] if with_moe else []))
+    other, across, me = chip_peers()
+    far = (me + 2) % 4
+    arrive([other, across] + tp_peers() + axis_peers(1, 3))
+    all_here(9)
+    for copy in fars[1] + fars[0]:
+        copy.start()
     unit, scale = norm_parts(x[...].astype(f32) + pair_rows(att))
     b = (unit * small[1:2] + small[3:4]).astype(bf16)
     router = small[4:8]
-    probs = softmax(dot(router.astype(bf16), b, NT), 0)
+    chances = softmax(dot(router.astype(bf16), b, NT), 0)
     ids = lax.broadcasted_iota(jnp.int32, (EXPERTS, PAIR), 0).astype(f32)
     named = (routes_t[0:1] == ids) | (routes_t[1:2] == ids)
     tables = [back[block, 0, 80:96, 0:ROWS].astype(f32)[0:EXPERTS] for block in range(2)]
     gate_grads = jnp.where(named, jnp.concatenate(tables, axis=1), 0.0)
-    grad_logits = probs * (gate_grads - jnp.sum(probs * gate_grads, axis=0, keepdims=True))
+    grad_logits = chances * (gate_grads - jnp.sum(chances * gate_grads, axis=0, keepdims=True))
     grad_b = pair_rows(back) + dot_exact(grad_logits, router, TN)
     grad_h[...] = grad[...].astype(f32) + norm_back(grad_b, unit, scale, small[1:2])
     grad_att = grad_h[own_rows(core)].astype(bf16)
-    grad_mixed = dot(grad_att, w_qo[:, WIDTH:], NN).astype(bf16)
+    w_kv, w_q, w_out_t = attn_weights(weights)
+    grad_mixed = dot(grad_att, w_out_t, NN).astype(bf16)
     keys = kv[...].reshape(KEYS, 2 * WIDTH)
     queries = q[...]
     q_parts, k_parts, v_parts = [], [], []
     for h in range(HEADS):
         q_h, g_h = head(queries, h), head(grad_mixed, h)
         k_h, v_h = head(keys, h), head(keys, HEADS + h)
-        weights = softmax(HD**-0.5 * dot(q_h, k_h, NT) + dead[...], -1)
-        v_parts.append(dot(weights.astype(bf16), g_h, TN))
+        probs = softmax(HD**-0.5 * dot(q_h, k_h, NT) + dead[...], -1)
+        v_parts.append(dot(probs.astype(bf16), g_h, TN))
         grad_weights = dot(g_h, v_h, NT)
-        grad_scores = weights * (
-            grad_weights - jnp.sum(weights * grad_weights, axis=-1, keepdims=True)
+        grad_scores = probs * (
+            grad_weights - jnp.sum(probs * grad_weights, axis=-1, keepdims=True)
         )
         grad_scores = grad_scores.astype(bf16)
         q_parts.append(HD**-0.5 * dot(grad_scores, k_h, NN))
         k_parts.append(HD**-0.5 * dot(grad_scores, q_h, TN))
     total = jnp.concatenate(k_parts + v_parts, axis=1).astype(bf16)
     parts[...] = total.reshape(4, ROWS, 2 * WIDTH)
-    all_here(9 if with_moe else 6)
-    copies = [
-        remote(parts.at[peer["zl"] * 2 + peer["core"]], kv_landed.at[k], kv_send.at[k], kv_recv.at[k], peer)
-        for k, peer in enumerate(peers)
+    crosses = [
+        remote(parts.at[(at + 1 - 2 * core) % 4], kv_landed.at[k], kv_send.at[k], kv_recv.at[k], other)
+        for k, at in enumerate((me, far))
     ]
-    for copy in copies:
-        copy.start()
+    onward = remote(kv_out, kv_landed.at[2], kv_send.at[2], kv_recv.at[2], across)
+    crosses[1].start()
+    crosses[0].start()
     if with_moe:
-        moe_terms = sum_terms(True, moe_part, moe_landed, ms, mr)
+        pre = sum_cores(*moe_sums)
+        pre.start()
+    crosses[1].wait_recv()
+    kv_out[...] = (parts[far].astype(f32) + kv_landed[1].astype(f32)).astype(bf16)
+    onward.start()
+    if with_moe:
+        pre.wait_recv()
+        for j in range(4):
+            moe_sum = moe_part[core, j].astype(f32) + moe_crossed[j].astype(f32)
+            moe_crossed[j] = moe_sum.astype(bf16)
+        moe_terms = [
+            remote(moe_crossed.at[peer["tp"]], moe_landed.at[k], ms.at[k], mr.at[k], peer)
+            for k, peer in enumerate(tp_peers())
+        ]
         for copy in moe_terms:
+            copy.start()
+    for route in (1, 0):
+        for copy in fars[route]:
+            copy.wait_recv()
+        add_passing(whole, passing, route)
+        for copy in nears[route]:
             copy.start()
     grad_q = jnp.concatenate(q_parts, axis=1).astype(bf16)
     grad_w[1, :, WIDTH:] = dot(grad_att, mixed[...], TN).astype(bf16)
@@ -661,19 +881,18 @@
     unit_one, scale_one = norm_parts(x[...].astype(f32))
     both_units[...] = unit_one
     normed = (both_units[own_rows(core)] * small[0:1] + small[2:3]).astype(bf16)
-    grad_kv = parts[me].astype(f32)
-    for k, copy in enumerate(copies):
-        copy.wait_recv()
-        grad_kv = grad_kv + kv_landed[k].astype(f32)
+    crosses[0].wait_recv()
+    onward.wait_recv()
+    grad_kv = parts[me].astype(f32) + kv_landed[0].astype(f32) + kv_landed[2].astype(f32)
     grad_kv = grad_kv.astype(bf16)
-    value = dot(grad_kv, w_kv[...], NT) + dot(grad_q, w_qo[:, :WIDTH], NT)
+    value = dot(grad_kv, w_kv, NT) + dot(grad_q, w_q, NT)
     put_chunks(part, 0, value.astype(bf16))
     sum_start(*sums)
     grad_w[0] = dot(normed, grad_kv, TN).astype(bf16)
     grad_w[1, :, :WIDTH] = dot(normed, grad_q, TN).astype(bf16)
     sum_middle(*sums)
     if with_moe:
-        total = moe_part[core, tp].astype(f32)
+        total = moe_crossed[tp].astype(f32)
         for k, copy in enumerate(moe_terms):
             copy.wait_recv()
             total = total + moe_landed[k].astype(f32)
@@ -689,13 +908,31 @@
     kept = jnp.where(own, grad_a, 0.0)
     grad_small[0:1] = jnp.sum(kept * unit_one, axis=0, keepdims=True)
     grad_small[2:3] = jnp.sum(kept, axis=0, keepdims=True)
-    for copy in copies:
+    for copy in crosses + [onward]:
         copy.wait_send()
     if with_moe:
+        pre.wait_send()
         for copy in moe_terms:
             copy.wait_send()
         for copy in moe_results:
             copy.wait()
+    for route in range(2):
+        for copy in fars[route]:
+            copy.wait_send()
+        for copy in nears[route]:
+            copy.wait()
+    at_x, at_z = places()
+    steps = some.shape[1] // 48
+
+    def add(i, carry):
+        j, at = i % 4, i // 4
+        rows, route = pl.ds(pl.multiple_of(at * 48, 48), 48), at // (steps // 2)
+        own = whole[j * (1 - route) + at_x * route, at_z * (1 - route) + j * route, rows]
+        total = own.astype(f32) + slabs[0, j, rows].astype(f32) + slabs[1, j, rows].astype(f32)
+        some[j, rows] = total.astype(bf16)
+        return carry
+
+    lax.fori_loop(0, 4 * steps, add, 0)
 
 
 def attend_backward(args, moe_part, cid):
@@ -708,15 +945,21 @@
         pltpu.VMEM((3, ROWS, 2 * WIDTH), bf16),
         pltpu.VMEM((2, 4, 80, 384), bf16),
     ]
-    scratch += sum_scratch(False, 80) + dma_sems(3)
+    slab = args[-1].shape[2:]
+    shapes.append(((4,) + slab, bf16))
+    scratch += sum_scratch(False, 80)
+    scratch += [pltpu.VMEM((2, 4) + slab, bf16), pltpu.VMEM((2, 2, 4, 128, FE), bf16)]
+    scratch += dma_sems(4, 8) + [pltpu.VMEM((ROWS, 2 * WIDTH), bf16)] + dma_sems(3)
+    in_specs = [VMEM] * len(args)
     if with_moe:
-        args = args + (moe_part,)
+        args, in_specs = args + (moe_part,), in_specs + [VMEM]
         shapes.append(((4, 80, 384), bf16))
-        scratch += [pltpu.VMEM((7, 80, 384), bf16)] + dma_sems(7, 3)
+        scratch += [pltpu.VMEM((3, 80, 384), bf16)] + dma_sems(3, 3)
+        scratch += [pltpu.VMEM((4, 80, 384), bf16)] + dma_sems(1)
     return pl.pallas_call(
         functools.partial(attend_backward_kernel, with_moe),
         out_shape=[jax.ShapeDtypeStruct(*s) for s in shapes],
-        in_specs=[VMEM] * len(args),
+        in_specs=in_specs,
         out_specs=[VMEM] * len(shapes),
         scratch_shapes=scratch,
         compiler_params=params(cid, 56),
@@ -740,28 +983,26 @@
     )
 
     stacked = jnp.stack([w_in, w_exp_out.transpose(0, 1, 3, 2)], axis=2).reshape(384, 2, FE)
-    attn_one = halves[1].reshape(48, 384)
-    own_half = jnp.concatenate([pick(stacked, core, 1), attn_one])
-    got_half = cross(jnp.concatenate([pick(stacked, 1 - core, 1), attn_one]), 0)
-    low_half = jnp.where(core == 0, own_half, got_half).reshape(18, 24, FE)
-    high_half = jnp.where(core == 0, got_half, own_half).reshape(18, 24, FE)
-    chip = jnp.concatenate([low_half, high_half], axis=1).reshape(864, FE)
-    every = lax.all_gather(chip, CHIPS, axis=0)
-    experts = [every, every]
+    tiny = jnp.concatenate([ln_gains, ln_biases, w_router.transpose(0, 2, 1)], axis=1)
+    tiny = jnp.pad(tiny.transpose(1, 0, 2).reshape(8, 48), ((0, 8), (0, 384 - 48)))
+    attn_one, attn_zero = halves[1].reshape(48, 384), halves[0].reshape(48, 384)
+    own_half = jnp.concatenate([pick(stacked, core, 1), attn_one, attn_zero, tiny])
+    got_half = cross(jnp.concatenate([pick(stacked, 1 - core, 1), attn_one, attn_zero, tiny]), 0)
+    low_half = jnp.where(core == 0, own_half, got_half)
+    high_half = jnp.where(core == 0, got_half, own_half)
+    chip = jnp.concatenate(
+        [low_half[:480].reshape(20, 24, FE), high_half[:480].reshape(20, 24, FE)], axis=1
+    )
+    later = jnp.concatenate([chip[0:8], chip[16:18]]).reshape(480, FE)
+    urgent = jnp.concatenate([chip[18:20].reshape(96, FE), low_half[480:496], high_half[480:496]])
 
     turned = jnp.pad(
         routes[0].astype(bf16).transpose(0, 2, 1), ((0, 0), (0, 14), (0, D - ROWS))
     )
     images = jnp.concatenate([boundary[0], turned], axis=1)
-    tiny = jnp.concatenate([ln_gains, ln_biases, w_router.transpose(0, 2, 1)], axis=1)
-    tiny = jnp.pad(tiny.transpose(1, 0, 2).reshape(8, 48), ((0, 0), (0, D - 48)))
-    pack = jnp.concatenate([jnp.concatenate([halves[0, 0], halves[0, 1]], axis=1), tiny])
-    got_images, packs = start_exchange(images, pack)
-    packs = packs.reshape(32, 32, D)
-    w_kvs, w_qos = [packs[:, 0:24, 0:384].reshape(D, 384)], [packs[:, 0:24, 384:].reshape(D, 384)]
-    w_kvs.append(every[:, 768:816].reshape(D, 384))
-    w_qos.append(every[:, 816:864].reshape(D, 384))
-    tiny = packs[:, 24:32, 0:48].reshape(32, 8, 2, 24).transpose(2, 1, 0, 3).reshape(2, 8, D)
+    got_images, packs, some = start_exchange(images, urgent, later)
+    packs = packs.reshape(16, 128, 384)
+    tiny = packs[:, 96:128].reshape(32, 16, 384)[:, 0:8, 0:48].reshape(32, 8, 2, 24).transpose(2, 1, 0, 3).reshape(2, 8, D)
     smalls = [tiny[0].astype(f32), tiny[1].astype(f32)]
 
     live = jnp.arange(ROWS, dtype=jnp.int32)[None, :] < lengths[:, None]
@@ -777,26 +1018,29 @@
     ]
     route_cols = [rows.T for rows in route_rows]
 
-    q0, kv0, mixed0, att0 = attend_forward(x0, (), smalls[0], w_kvs[0], w_qos[0], dead, 3)
-    moe0 = experts_forward(x0, att0, smalls[0], route_cols[0], experts[0], 4)
+    attn_w0 = packs[:, 0:96]
+    q0, kv0, mixed0, att0, experts_zero = attend_forward(x0, (), smalls[0], attn_w0, dead, some, 3)
+    experts_zero = experts_zero.reshape(16, 480, 384)
+    attn_w1 = experts_zero[:, 384:480]
+    shard, att0 = lax.optimization_barrier((chip[8:16].reshape(384, FE), att0))
+    experts_one = lax.all_gather(shard, CHIPS, axis=0)
+    moe0 = experts_forward(x0, att0, smalls[0], route_cols[0], experts_zero, 4)
     q1, kv1, mixed1, att1, x1 = attend_forward(
-        x0, (att0, moe0), smalls[1], w_kvs[1], w_qos[1], dead, 5
+        x0, (att0, moe0), smalls[1], attn_w1, dead, None, 5
     )
     back, moe_part, grad_experts1 = experts_backward(
-        x1, att1, smalls[1], route_cols[1], cotangent, None, experts[1], EXPERTS, 6
-    )
-    sums1 = lax.psum_scatter(grad_experts1, CHIPS, scatter_dimension=0).reshape(8, 48, FE)
-    grad_x1, grad_small1, grad_attn1, moe1 = attend_backward(
-        (x1, att1, smalls[1], route_rows[1], cotangent, back, q1, kv1, mixed1, dead, w_kvs[1], w_qos[1]),
+        x1, att1, smalls[1], route_cols[1], cotangent, None, None, experts_one, 6
+    )
+    grad_x1, grad_small1, grad_attn1, some, moe1 = attend_backward(
+        (x1, att1, smalls[1], route_rows[1], cotangent, back, q1, kv1, mixed1, dead, attn_w1, grad_experts1.reshape(4, 4, 384, FE)),
         moe_part,
         7,
     )
-    back, grad_experts0 = experts_backward(
-        x0, att0, smalls[0], route_cols[0], grad_x1, grad_attn1, experts[0], 0, 8
-    )
-    sums0 = lax.psum_scatter(grad_experts0, CHIPS, scatter_dimension=0).reshape(10, 48, FE)
-    grad_x0, grad_small0, grad_attn0 = attend_backward(
-        (x0, att0, smalls[0], route_rows[0], grad_x1, back, q0, kv0, mixed0, dead, w_kvs[0], w_qos[0]),
+    back, sums1, grad_experts0 = experts_backward(
+        x0, att0, smalls[0], route_cols[0], grad_x1, grad_attn1, some, experts_zero, 8
+    )
+    grad_x0, grad_small0, grad_attn0, some = attend_backward(
+        (x0, att0, smalls[0], route_rows[0], grad_x1, back, q0, kv0, mixed0, dead, attn_w0, grad_experts0.reshape(4, 4, 480, FE)),
         None,
         9,
     )
@@ -812,35 +1056,31 @@
     mine = jnp.where(own_live[None, :, None], mine, 0.0)
     kept, sent = pick(mine, high, 0), pick(mine, 1 - high, 0).astype(bf16)
 
-    tiny = jnp.stack([grad_small0, grad_small1], axis=1).astype(bf16).reshape(8, 2, 16, 2, 24)
-    tiny = tiny.transpose(3, 2, 0, 1, 4).reshape(2, 16, 8, 48)
-    tiny = jnp.pad(tiny, ((0, 0), (0, 0), (0, 0), (0, D - 48)))
-    packs = grad_attn0.reshape(2, 16, 2, 24, 384).transpose(2, 1, 3, 0, 4).reshape(2, 16, 24, D)
-    packs = jnp.concatenate([packs, tiny], axis=2)
-
-    def by_core(sums, at):
-        return lax.dynamic_slice_in_dim(sums, 24 * at, 24, 1)
-
-    own, landed, got1 = end_exchange(packs, sent, by_core(sums1, 1 - core).reshape(192, FE))
+    tiny = jnp.stack([grad_small0, grad_small1]).astype(bf16).reshape(2, 8, 16, 2, 24)
+    tiny = tiny.transpose(0, 2, 3, 1, 4).reshape(2, 16, 16, 24)
+    tiny = jnp.pad(tiny, ((0, 0), (0, 0), (0, 0), (0, 384 - 24)))
+    packs = jnp.concatenate([grad_attn0.reshape(2, 16, 48, 384), tiny], axis=2)
+    own, landed, got1, own0, got0 = end_exchange(packs, sent, sums1, some)
     landed = landed.astype(f32)
     ends = jnp.where(high == 0, jnp.stack([kept, landed]), jnp.stack([landed, kept]))
-    got0 = cross(by_core(sums0, 1 - core).reshape(240, FE), 10).reshape(10, 24, FE)
-    own0 = by_core(sums0, core)
-    attn1 = own0[8:10].astype(f32) + got0[8:10].astype(f32)
+
+    def own_lines(sums):
+        return lax.dynamic_slice_in_dim(sums.reshape(-1, 48, FE), 24 * core, 24, 1).astype(f32)
+
+    own0, got0, own1, got1 = (own_lines(sums) for sums in (own0, got0, sums1, got1))
+    attn1 = own0[8:10] + got0[8:10]
 
     def both_halves(own_sum, got_sum):
         first = jnp.where(core == 0, own_sum, got_sum)
         second = jnp.where(core == 0, got_sum, own_sum)
-        return jnp.concatenate([first, second], axis=2).reshape(EXPERTS, 2, 24, D).astype(f32)
-
-    full = jnp.stack(
-        [both_halves(own0[0:8], got0[0:8]), both_halves(by_core(sums1, core), got1.reshape(8, 24, FE))]
-    )
-    attn0 = own[0:24].reshape(24, 2, 384).transpose(1, 0, 2)
+        return jnp.concatenate([first, second], axis=2).reshape(EXPERTS, 2, 24, D)
+
+    full = jnp.stack([both_halves(own0[0:8], got0[0:8]), both_halves(own1, got1)])
+    attn0 = lax.dynamic_slice_in_dim(own, 24 * core, 24, 1)
     attn = jnp.stack([attn0, attn1])
     grad_w_qkv = jnp.concatenate([attn[:, 1, :, None, :WIDTH], attn[:, 0].reshape(2, 24, 2, WIDTH)], axis=2)
     grad_w_out = attn[:, 1, :, WIDTH:].transpose(0, 2, 1)
-    tiny = own[24:32, 0:48].reshape(8, 2, 24).transpose(1, 0, 2)
+    tiny = lax.dynamic_slice_in_dim(own[:, 48:64, 0:24], 8 * core, 8, 1)
     return (
         ends[None],
         tiny[:, 0:2],

time: 381 us -> 332 us (0.87)
  waiting for transfers between devices: 50.1 us -> 0.02 us
  local copies, waits for them, and re-layouts: 26.9 us -> 21.4 us
  Pallas kernels: 271 us -> 276 us
    unnamed x5 -> x1, waiting for transfers between devices: 34.5 us -> 0.02 us
    all_gather x1, waiting for transfers between devices: 15.6 us -> 0.01 us  [shards(): experts_one = lax.all_gather(shard, CHIPS, axis=0)]
    pallas_call x2, Pallas kernels: 63.7 us -> 70.1 us  [attend_backward(): pl.pallas_call(functools.partial(attend_backward_kernel, with_moe), out_s...]
    pallas_call x2, Pallas kernels: 58.2 us -> 62.9 us  [attend_forward(): pl.pallas_call(functools.partial(attend_forward_kernel, bool(before)), ou...]
  transfers between devices with their start and end apart: 3 -> 1, of which waited for: 2 -> 0; matrix products, arithmetic and copies ran while one was open for 7% -> 2% of each run, Pallas kernels for 50% -> 15%
where the time goes in v3:
time: 332 us; the launch traced here: 327 us
  Pallas kernels  276 us (83%)
  local copies, waits for them, and re-layouts  21.4 us (6%)
  between operations  14.9 us (4%)
  other arithmetic  14.7 us (4%)
    pallas_call x2, Pallas kernels, attend_backward(): pl.pallas_call(functools.partial(attend_backward_kernel, with_moe), out_s...  70.1 us
    pallas_call x2, Pallas kernels, attend_forward(): pl.pallas_call(functools.partial(attend_forward_kernel, bool(before)), ou...  62.9 us
    pallas_call x2, Pallas kernels, experts_backward(): pl.pallas_call(kernel, grid=(steps,), out_shape=[jax.ShapeDtypeStruct(s,...  53.3 us
    pallas_call x1, Pallas kernels, start_exchange(): pl.pallas_call(start_kernel, out_shape=[jax.ShapeDtypeStruct(s, bf16) for...  34.5 us
    pallas_call x1, Pallas kernels, end_exchange(): pl.pallas_call(end_kernel, out_shape=[jax.ShapeDtypeStruct((2,) + shape,...  30.5 us
    pallas_call x1, Pallas kernels, experts_forward(): pl.pallas_call(experts_forward_kernel, grid=(EXPERTS,), out_shape=jax.Sha...  21.7 us
  transfers between devices with their start and end apart: 1, of which 0 were waited for; matrix products, arithmetic and copies ran while one was open for 2% of the time, Pallas kernels for 15%

profile of v3, /device:TPU:1, one launch (start us, length us, event | category | flops | bytes accessed | tf_op | source)
XLA Modules:
  0.0 326.9 jit_solution(5497719243706526727)
XLA Ops:
  8.0 1.2 pad_maximum_fusion.1
  9.6 1.2 constant_dynamic-slice_fusion.6
  11.1 2.9 cross.1
  17.4 34.5 %start_exchange.1 = (bf16[2,2,176,768]{3,2,1,0:T(8,128)(2,1)}, bf16[4,4,128,384]{3,2,1,0:T(8,128)(2,1)}, bf16[4,4,480,384]{3,2,1,0:T(8,128)(2,1)}) custom-call(bf16[2,176,768]{2,1,0:T(8,128)(2,1)} %fusion.7.images, bf16[128,384]{1,0:T(8,128)(2,1)} %pad_maximum_fusion.11.urgent, bf16[480,384]{1,0:T(8,128)(2,1)} %bitcast.134), custom_call_target="tpu_custom_call" | custom-call | tf_op jit(solution)/shard_map/start_exchange/pallas_call | solution.py:254
  51.9 2.5 slice.155.refs_2_.refs_10_
  54.4 1.0 slice.152
  58.1 35.3 %attend_forward.2 = (bf16[160,192]{1,0:T(8,128)(2,1)}, bf16[4,160,384]{2,1,0:T(8,128)(2,1)}, bf16[160,192]{1,0:T(8,128)(2,1)}, bf16[2,4,80,384]{3,2,1,0:T(8,128)(2,1)}, bf16[4,4,480,384]{3,2,1,0:T(8,128)(2,1)}) custom-call(bf16[320,768]{1,0:T(8,128)(2,1)} %bitcast.115, f32[8,768]{1,0:T(8,128)} %reshape.256.refs_1_.small.refs_2_, ...), custom_call_target="tpu_custom_call", output_to_operand_aliasing={{4}: (4, {})} | custom-call | tf_op jit(solution)/shard_map/attend_forward/pallas_call | solution.py:575
  93.5 2.4 slice.157.refs_4_.refs_10_
  98.7 21.7 %experts_forward.1.refs_2_ = bf16[2,4,80,384]{3,2,1,0:T(8,128)(2,1)} custom-call(bf16[320,768]{1,0:T(8,128)(2,1)} %bitcast.116, bf16[2,4,80,384]{3,2,1,0:T(8,128)(2,1)} %get-tuple-element.47.att.refs_1_, f32[8,768]{1,0:T(8,128)} %reshape.256.refs_1_.small.refs_2_, f32[320,2]{1,0:T(8,128)} %copy.59.routes.refs_3_, bf16[16,480,384]{2,1,0:T(8,128)(2,1)} %bitcast.113), custom_call_target="tpu_custom_call" | custom-call | tf_op jit(solution)/shard_map/experts_forward/pallas_call | solution.py:641
  120.4 27.6 %attend_forward.3 = (bf16[160,192]{1,0:T(8,128)(2,1)}, bf16[4,160,384]{2,1,0:T(8,128)(2,1)}, bf16[160,192]{1,0:T(8,128)(2,1)}, bf16[2,4,80,384]{3,2,1,0:T(8,128)(2,1)}, bf16[320,768]{1,0:T(8,128)(2,1)}) custom-call(bf16[320,768]{1,0:T(8,128)(2,1)} %bitcast.117, bf16[2,4,80,384]{3,2,1,0:T(8,128)(2,1)} %get-tuple-element.47.att.refs_1_, ...), custom_call_target="tpu_custom_call" | custom-call | tf_op jit(solution)/shard_map/attend_forward/pallas_call | solution.py:575
  148.0 1.0 constant_dynamic-slice_fusion.3
  150.5 26.5 %experts_backward.2 = (bf16[2,4,96,384]{3,2,1,0:T(8,128)(2,1)}, bf16[2,4,80,384]{3,2,1,0:T(8,128)(2,1)}, bf16[16,384,384]{2,1,0:T(8,128)(2,1)}) custom-call(bf16[320,768]{1,0:T(8,128)(2,1)} %get-tuple-element.49.refs_0_, bf16[2,4,80,384]{3,2,1,0:T(8,128)(2,1)} %get-tuple-element.50.refs_1_, f32[8,768]{1,0:T(8,128)} %reshape.258.refs_3_.refs_2_, ...), custom_call_target="tpu_custom_call" | custom-call | tf_op jit(solution)/shard_map/experts_backward/pallas_call | solution.py:765
  177.0 32.2 %attend_backward.2 = (bf16[320,768]{1,0:T(8,128)(2,1)}, f32[8,768]{1,0:T(8,128)}, bf16[2,768,384]{2,1,0:T(8,128)(2,1)}, bf16[4,384,384]{2,1,0:T(8,128)(2,1)}, bf16[4,80,384]{2,1,0:T(8,128)(2,1)}) custom-call(bf16[320,768]{1,0:T(8,128)(2,1)} %get-tuple-element.49.refs_0_, bf16[2,4,80,384]{3,2,1,0:T(8,128)(2,1)} %get-tuple-element.50.refs_1_, ...), custom_call_target="tpu_custom_call" | custom-call | tf_op jit(solution)/shard_map/attend_backward/pallas_call | solution.py:959
  209.2 1.1 copy.78
  210.8 26.8 %experts_backward.3 = (bf16[2,4,96,384]{3,2,1,0:T(8,128)(2,1)}, bf16[384,384]{1,0:T(8,128)(2,1)}, bf16[16,480,384]{2,1,0:T(8,128)(2,1)}) custom-call(bf16[320,768]{1,0:T(8,128)(2,1)} %bitcast.118, bf16[2,4,80,384]{3,2,1,0:T(8,128)(2,1)} %get-tuple-element.47.att.refs_1_, f32[8,768]{1,0:T(8,128)} %reshape.256.refs_1_.small.refs_2_, ...), custom_call_target="tpu_custom_call" | custom-call | tf_op jit(solution)/shard_map/experts_backward/pallas_call | solution.py:765
  237.6 37.9 %attend_backward.3 = (bf16[320,768]{1,0:T(8,128)(2,1)}, f32[8,768]{1,0:T(8,128)}, bf16[2,768,384]{2,1,0:T(8,128)(2,1)}, bf16[4,480,384]{2,1,0:T(8,128)(2,1)}) custom-call(bf16[320,768]{1,0:T(8,128)(2,1)} %bitcast.119, bf16[2,4,80,384]{3,2,1,0:T(8,128)(2,1)} %get-tuple-element.47.att.refs_1_, f32[8,768]{1,0:T(8,128)} %reshape.256.refs_1_.small.refs_2_, ...), custom_call_target="tpu_custom_call" | custom-call | tf_op jit(solution)/shard_map/attend_backward/pallas_call | solution.py:959
  275.5 1.0 dynamic-slice_convert_fusion.1
  279.0 1.4 fusion.1.part
  280.5 30.5 %end_exchange.1 = (f32[2,64,384]{2,1,0:T(8,128)}, bf16[160,768]{1,0:T(8,128)(2,1)}, bf16[384,384]{1,0:T(8,128)(2,1)}, bf16[480,384]{1,0:T(8,128)(2,1)}, bf16[480,384]{1,0:T(8,128)(2,1)}) custom-call(bf16[2,16,64,384]{3,2,1,0:T(8,128)(2,1)} %fusion.1.part, bf16[160,768]{1,0:T(8,128)(2,1)} %fusion.11.image, bf16[384,384]{1,0:T(8,128)(2,1)} %get-tuple-element.71.half, ...), custom_call_target="tpu_custom_call" | custom-call | tf_op jit(solution)/shard_map/end_exchange/pallas_call | solution.py:421
  311.0 1.0 dynamic-slice_convert_fusion.2
  312.0 1.0 dynamic-slice_convert_fusion.3
  313.0 0.9 dynamic-slice_bitcast_fusion.1
  317.0 1.1 fusion.6
  318.8 1.0 maximum_select_fusion.1
  (110 shorter events, 18.2 us)
Async XLA Ops:
  7.2 143.4 %all-gather.3.cloned.1.call-start = ((), (), s32[]{:S(2)}) async-start(), calls=%async_computation | async-start | bytes 5013504 | tf_op jit(solution)/shard_map/all_gather | solution.py:1026
  8.0 1.4 slice-start
  8.0 1.5 copy-start.12
  8.0 1.5 copy-start.13
  8.0 1.5 copy-start.14
  9.6 1.3 copy-start.10
  14.2 0.9 copy-start.11
  14.2 1.6 copy-start.4
  51.9 3.6 %copy-start.2 = (bf16[2,2,176,768]{3,2,1,0:T(8,128)(2,1)S(1)}, bf16[2,2,176,768]{3,2,1,0:T(8,128)(2,1)}, u32[]{:S(2)}) copy-start(bf16[2,2,176,768]{3,2,1,0:T(8,128)(2,1)} %get-tuple-element.43) | copy-start | bytes 3244036
  55.5 1.9 copy-start.15
  96.0 24.4 %copy-start.7 = (f32[2,320]{1,0:T(2,128)}, f32[2,320]{1,0:T(2,128)S(1)}, u32[]{:S(2)}) copy-start(f32[2,320]{1,0:T(2,128)S(1)} %reshape.257.refs_3_) | copy-start | bytes 7684
  97.9 22.6 %copy-start.8 = (f32[2,320]{1,0:T(2,128)}, f32[2,320]{1,0:T(2,128)S(1)}, u32[]{:S(2)}) copy-start(f32[2,320]{1,0:T(2,128)S(1)} %reshape.259.refs_3_) | copy-start | bytes 7684
  237.6 39.8 %copy-start.9 = (f32[8,768]{1,0:T(8,128)S(1)}, f32[8,768]{1,0:T(8,128)}, u32[]{:S(2)}) copy-start(f32[8,768]{1,0:T(8,128)} %get-tuple-element.70) | copy-start | bytes 73732
  237.6 40.0 %copy-start = (bf16[320,768]{1,0:T(8,128)(2,1)S(1)}, bf16[320,768]{1,0:T(8,128)(2,1)}, u32[]{:S(2)}) copy-start(bf16[320,768]{1,0:T(8,128)(2,1)} %get-tuple-element.49.refs_0_) | copy-start | bytes 1474564
  277.7 1.4 copy-start.1
  312.0 3.6 %copy-start.5 = (bf16[160,768]{1,0:T(8,128)(2,1)S(1)}, bf16[160,768]{1,0:T(8,128)(2,1)}, u32[]{:S(2)}) copy-start(bf16[160,768]{1,0:T(8,128)(2,1)} %get-tuple-element.73) | copy-start | bytes 737284
  315.5 1.4 copy-start.3
  315.5 1.4 copy-start.6
Sparse Core Ops, SparseCore 0:
  93.6 54.0 all-gather.2

commit v4 on v3

--- a/solution.py
+++ b/solution.py
@@ -32,16 +32,18 @@
     return lax.dot_general(a, b, dims, preferred_element_type=f32)
 
 
-def dot_exact(a, b, dims):
-    return lax.dot_general(
-        a, b, dims, preferred_element_type=f32, precision=lax.Precision.HIGHEST
-    )
+def dot_split(a, b, dims):
+    high = a.astype(bf16)
+    return dot(high, b, dims) + dot((a - high.astype(f32)).astype(bf16), b, dims)
 
 
 def params(cid, mib):
     return pltpu.CompilerParams(
         collective_id=cid, has_side_effects=True, vmem_limit_bytes=mib * 2**20
     )
+
+
+ANY = pl.BlockSpec(memory_space=pl.ANY)
 
 
 def arrive(peers):
@@ -68,93 +70,117 @@
     return [{"tp": (lax.axis_index("tp") + k) % 4} for k in (1, 2, 3)]
 
 
+def pieces_of(rows):
+    return (pl.ds(0, 48), pl.ds(48, rows - 48))
+
+
 def sum_cores(part, crossed, send, recv):
     core = lax.axis_index("core")
-    return remote(part.at[1 - core], crossed, send.at[0], recv.at[0], {"core": 1 - core})
+    return [
+        remote(part.at[1 - core, :, rows], crossed.at[:, rows], send.at[p], recv.at[p], {"core": 1 - core})
+        for p, rows in enumerate(pieces_of(part.shape[2]))
+    ]
 
 
 def sum_terms(both, part, landed, send, recv):
     block = lax.axis_index("core") if both else 0
     return [
-        remote(part.at[block, peer["tp"]], landed.at[k], send.at[k], recv.at[k], peer)
-        for k, peer in enumerate(tp_peers())
+        [
+            remote(
+                part.at[block, peer["tp"], rows], landed.at[k, rows],
+                send.at[3 * p + k], recv.at[3 * p + k], peer,
+            )
+            for k, peer in enumerate(tp_peers())
+        ]
+        for p, rows in enumerate(pieces_of(part.shape[2]))
     ]
 
 
 def sum_results(out, send, recv):
     core, tp = lax.axis_index("core"), lax.axis_index("tp")
     return [
-        remote(out.at[core, tp], out.at[core, tp], send.at[k], recv.at[k], peer)
-        for k, peer in enumerate(tp_peers())
+        [
+            remote(out.at[core, tp, rows], out.at[core, tp, rows], send.at[3 * p + k], recv.at[3 * p + k], peer)
+            for k, peer in enumerate(tp_peers())
+        ]
+        for p, rows in enumerate(pieces_of(out.shape[2]))
     ]
 
 
 def sum_cross(out, send, recv):
     core, tp = lax.axis_index("core"), lax.axis_index("tp")
     return [
-        remote(out.at[core, at], out.at[core, at], send.at[k], recv.at[k], {"core": 1 - core})
-        for k, at in enumerate([(tp + 4 - k) % 4 for k in range(4)])
+        [
+            remote(
+                out.at[core, at, rows], out.at[core, at, rows],
+                send.at[4 * p + k], recv.at[4 * p + k], {"core": 1 - core},
+            )
+            for k, at in enumerate([(tp + 4 - k) % 4 for k in range(4)])
+        ]
+        for p, rows in enumerate(pieces_of(out.shape[2]))
     ]
 
 
 def sum_start(both, out, part, landed, rs, rr, gs, gr, cs, cr, crossed=None, ps=None, pr=None):
+    terms = sum_terms(both, part, landed, rs, rr)
     if both:
         core = lax.axis_index("core")
-        pre = sum_cores(part, crossed, ps, pr)
-        pre.start()
-        pre.wait_recv()
-        for j in range(4):
-            part[core, j] = (part[core, j].astype(f32) + crossed[j].astype(f32)).astype(bf16)
-    for copy in sum_terms(both, part, landed, rs, rr):
-        copy.start()
+        pres = sum_cores(part, crossed, ps, pr)
+        for pre in pres:
+            pre.start()
+    for p, rows in enumerate(pieces_of(part.shape[2])):
+        if both:
+            pres[p].wait_recv()
+            for j in range(4):
+                total = part[core, j, rows].astype(f32) + crossed[j, rows].astype(f32)
+                part[core, j, rows] = total.astype(bf16)
+        for copy in terms[p]:
+            copy.start()
 
 
 def sum_middle(both, out, part, landed, rs, rr, gs, gr, cs, cr, *pre):
     core, tp = lax.axis_index("core"), lax.axis_index("tp")
-    total = part[core if both else 0, tp].astype(f32)
-    for k, copy in enumerate(sum_terms(both, part, landed, rs, rr)):
-        copy.wait_recv()
-        total = total + landed[k].astype(f32)
-    out[core, tp] = total.astype(bf16)
-    for copy in sum_results(out, gs, gr):
-        copy.start()
+    terms, results, crosses = sum_terms(both, part, landed, rs, rr), sum_results(out, gs, gr), sum_cross(out, cs, cr)
+    for p, rows in enumerate(pieces_of(part.shape[2])):
+        total = part[core if both else 0, tp, rows].astype(f32)
+        for k, copy in enumerate(terms[p]):
+            copy.wait_recv()
+            total = total + landed[k, rows].astype(f32)
+        out[core, tp, rows] = total.astype(bf16)
+        for copy in results[p]:
+            copy.start()
+        crosses[p][0].start()
 
 
 def sum_end(both, out, part, landed, rs, rr, gs, gr, cs, cr, *pre):
-    gathers, crosses = sum_results(out, gs, gr), sum_cross(out, cs, cr)
-    for k in range(4):
-        if k > 0:
-            gathers[k - 1].wait_recv()
-        crosses[k].start()
-    for copy in crosses:
-        copy.wait()
-    for copy in sum_terms(both, part, landed, rs, rr) + gathers:
-        copy.wait_send()
+    terms, results, crosses = sum_terms(both, part, landed, rs, rr), sum_results(out, gs, gr), sum_cross(out, cs, cr)
+    for p in range(2):
+        for k in range(3):
+            results[p][k].wait_recv()
+            crosses[p][k + 1].start()
+    for p in range(2):
+        for copy in crosses[p]:
+            copy.wait()
+        for copy in terms[p] + results[p]:
+            copy.wait_send()
     if both:
-        sum_cores(part, *pre).wait_send()
+        for copy in sum_cores(part, *pre):
+            copy.wait_send()
 
 
 def sum_scratch(both, rows):
     scratch = [
         pltpu.VMEM((2 if both else 1, 4, rows, 384), bf16),
         pltpu.VMEM((3, rows, 384), bf16),
-    ] + dma_sems(3, 3, 4)
+    ] + dma_sems(6, 6, 8)
     if both:
-        scratch += [pltpu.VMEM((4, rows, 384), bf16)] + dma_sems(1)
+        scratch += [pltpu.VMEM((4, rows, 384), bf16)] + dma_sems(2)
     return scratch
 
 
 def chip_peers():
     core, zl = lax.axis_index("core"), lax.axis_index("zl")
     return {"core": 1 - core}, {"zl": 1 - zl}, zl * 2 + core
-
-
-def chip_peer(k):
-    x, zh, zl = (lax.axis_index(a) for a in CHIPS)
-    dx, dh, dl = k // 4, (k // 2) % 2, k % 2
-    ahead = ((x + dx) % 4, (zh + dh) % 2, (zl + dl) % 2)
-    back = ((x + 4 - dx) % 4, (zh + 2 - dh) % 2, (zl + 2 - dl) % 2)
-    return dict(zip(CHIPS, ahead)), *(c[0] * 4 + c[1] * 2 + c[2] for c in (ahead, back))
 
 
 def cross_kernel(own, out, send, recv):
@@ -235,11 +261,11 @@
     passed = remote(
         out_images.at[core, 1 - high], out_images.at[core, 1 - high], im_s.at[2], im_r.at[2], other
     )
-    for copy in firsts + [swap, kept]:
+    for copy in firsts + [swap, kept] + laters:
         copy.start()
     for copy in firsts:
         copy.wait_recv()
-    for copy in seconds + laters:
+    for copy in seconds:
         copy.start()
     swap.wait_recv()
     passed.start()
@@ -258,7 +284,7 @@
             for s in ((2,) + images.shape, (4, 4) + urgent.shape, (4, 4) + later.shape)
         ],
         in_specs=[VMEM] * 3,
-        out_specs=[VMEM, VMEM, pl.BlockSpec(memory_space=pl.ANY)],
+        out_specs=[VMEM, VMEM, ANY],
         scratch_shapes=[pltpu.SemaphoreType.DMA] + dma_sems(3, 6, 6, 6),
         compiler_params=params(1, 56),
         name="start_exchange",
@@ -348,7 +374,7 @@
 
 def add_slabs(some, slabs, out):
     x, z = places()
-    steps = out.shape[0] // 48
+    steps = some.shape[1] // 48
 
     def add(i, carry):
         rows, route = pl.ds(pl.multiple_of(i * 48, 48), 48), i // (steps // 2)
@@ -362,74 +388,101 @@
 
 
 def end_kernel(
-    part, image, half, some, out, out_image, out_half, own_sum, other_sum,
-    landed, sums, pieces, total, slabs, cx_s, cx_r, sl_s, sl_r, send, recv,
+    part, image, half_sum, some, some_attn, out, out_image, out_half, own_sum, other_sum,
+    landed, sums, pieces, mids, lands, slabs, attn_slabs, cx_s, cx_r, sl_s, sl_r, at_s, at_r, p1_s, p1_r, p2_s, p2_r,
 ):
     core, x = lax.axis_index("core"), lax.axis_index("x")
     other = {"core": 1 - core}
-    _, me, _ = chip_peer(0)
-    arrive([chip_peer(k)[0] for k in range(1, 16)] + [other])
-    all_here(16)
+    arrive(axis_peers(1, 2, 3) + [other])
+    all_here(7)
     crossing = remote(part.at[1 - core], landed, cx_s.at[0], cx_r.at[0], other)
     crossing.start()
     lasts = last_copies(some, slabs, sl_s, sl_r)
-    for copy in lasts:
+    firsts, seconds = [], []
+    for route in range(2):
+        rows = half(64, route)
+        for k in range(1, 4):
+            peer, at = axis_peer(route == 0, k)
+            n = 3 * route + k - 1
+            lasts.append(
+                remote(some_attn.at[route, at], attn_slabs.at[route, k - 1], at_s.at[n], at_r.at[n], peer)
+            )
+            seconds.append(remote(mids.at[at, rows], lands.at[k - 1, rows], p2_s.at[n], p2_r.at[n], peer))
+            peer, at = axis_peer(route == 1, k)
+            firsts.append(
+                remote(line(sums, route, at, rows), pieces.at[k - 1, :, rows], p1_s.at[n], p1_r.at[n], peer)
+            )
+    swap = remote(image, out_image, cx_s.at[1], cx_r.at[1], {"x": (x + 2) % 4})
+    halves = remote(half_sum, out_half, cx_s.at[2], cx_r.at[2], other)
+    for copy in lasts + [halves]:
         copy.start()
     crossing.wait()
 
-    def push(k):
-        peer, at, _ = chip_peer(k)
-        return remote(sums.at[at], pieces.at[k], send.at[k], recv.at[k], peer)
-
-    def add(k, carry):
-        _, at, _ = chip_peer(k)
-        sums[at] = (part[core, at].astype(f32) + landed[at].astype(f32)).astype(bf16)
-        push(k).start()
+    def add(i, carry):
+        total = part[core, i // 4, i % 4].astype(f32) + landed[i // 4, i % 4].astype(f32)
+        sums[i // 4, i % 4] = total.astype(bf16)
         return carry
 
-    def collect(k, carry):
-        push(k).wait_recv()
-        total[...] += pieces[k].astype(f32)
-        return carry
-
-    def last(k, carry):
-        push(k).wait_send()
-        return carry
-
-    lax.fori_loop(1, 16, add, 0)
-    swap = remote(image, out_image, cx_s.at[1], cx_r.at[1], {"x": (x + 2) % 4})
-    swap.start()
-    halves = remote(half, out_half, cx_s.at[2], cx_r.at[2], other)
-    halves.start()
-    total[...] = part[core, me].astype(f32) + landed[me].astype(f32)
-    lax.fori_loop(1, 16, collect, 0)
-    out[core] = total[...]
-    given = remote(out.at[core], out.at[core], cx_s.at[4], cx_r.at[4], other)
-    given.start()
+    lax.fori_loop(0, 16, add, 0)
+    for copy in firsts + [swap]:
+        copy.start()
+    for copy in firsts:
+        copy.wait_recv()
+    at_x, at_z = places()
+    for route in range(2):
+        rows = half(64, route)
+
+        def gather(j, carry, route=route, rows=rows):
+            total = (sums[j, at_z, rows] if route == 0 else sums[at_x, j, rows]).astype(f32)
+            for k in range(3):
+                total = total + pieces[k, j, rows].astype(f32)
+            mids[j, rows] = total.astype(bf16)
+            return carry
+
+        lax.fori_loop(0, 4, gather, 0)
+    for copy in seconds:
+        copy.start()
     for copy in lasts:
         copy.wait()
     add_slabs(some, slabs, own_sum)
+    for route in range(2):
+        attn = some_attn[route, places()[route]].astype(f32)
+        for k in range(3):
+            attn = attn + attn_slabs[route, k].astype(f32)
+        first = 384 + 48 * route
+        own_sum[first : first + 48] = attn.astype(bf16)
     final = remote(own_sum, other_sum, cx_s.at[3], cx_r.at[3], other)
     final.start()
-    lax.fori_loop(1, 16, last, 0)
+    for copy in seconds:
+        copy.wait()
+    for route in range(2):
+        rows = half(64, route)
+        total = mids[places()[route], rows].astype(f32)
+        for k in range(3):
+            total = total + lands[k, rows].astype(f32)
+        out[core, rows] = total
+    given = remote(out.at[core], out.at[core], cx_s.at[4], cx_r.at[4], other)
+    given.start()
+    for copy in firsts:
+        copy.wait_send()
     for copy in (given, final, swap, halves):
         copy.wait()
 
 
-def end_exchange(part, image, half, some):
-    shape, slab = part.shape[2:], some.shape[1:]
+def end_exchange(part, image, half_sum, some, some_attn):
+    slab = (480, FE)
+    scratch = [(4, 4, 64, FE)] * 2 + [(3, 4, 64, FE), (4, 64, FE), (3, 64, FE)]
+    scratch += [(3,) + some.shape[1:], (2, 3, 48, FE)]
     return pl.pallas_call(
         end_kernel,
-        out_shape=[jax.ShapeDtypeStruct((2,) + shape, f32)]
-        + [jax.ShapeDtypeStruct(s, bf16) for s in (image.shape, half.shape, slab, slab)],
-        in_specs=[VMEM] * 4,
+        out_shape=[jax.ShapeDtypeStruct((2, 64, FE), f32)]
+        + [jax.ShapeDtypeStruct(s, bf16) for s in (image.shape, half_sum.shape, slab, slab)],
+        in_specs=[VMEM] * 5,
         out_specs=[VMEM] * 5,
-        scratch_shapes=[pltpu.VMEM((16,) + shape, bf16)] * 3
-        + [pltpu.VMEM(shape, f32), pltpu.VMEM((3,) + slab, bf16)]
-        + dma_sems(5, 6, 16),
+        scratch_shapes=[pltpu.VMEM(s, bf16) for s in scratch] + dma_sems(5, 6, 6, 6, 6),
         compiler_params=params(2, 56),
         name="end_exchange",
-    )(part, image, half, some)
+    )(part, image, half_sum, some, some_attn)
 
 
 def block_rows(ref, block):
@@ -498,15 +551,15 @@
     if follows:
         x, att_before, moe_before, small, weights, dead, q, kv, mixed, att, x_next, *scratch = refs
     else:
-        x, small, weights, dead, _, q, kv, mixed, att, whole, *scratch = refs
-        *scratch, sp_send, sp_recv = scratch
+        x, small, weights, dead, ahead, _, q, kv, mixed, att, whole, all_ahead, *scratch = refs
+        *scratch, sp_send, sp_recv, ah_send, ah_recv, own_sem = scratch
     part, landed, *sems, kv_send, kv_recv = scratch
     sums = (False, att, part, landed, *sems)
     core = lax.axis_index("core")
     other, across, me = chip_peers()
     arrive([other, across] + tp_peers())
     if not follows:
-        arrive(axis_peers(1, 3))
+        arrive(axis_peers(1, 2, 3))
     if follows:
         x_next[...] = (x[...].astype(f32) + pair_rows(att_before) + pair_rows(moe_before)).astype(bf16)
         x = x_next
@@ -514,7 +567,7 @@
     normed = (unit * small[0:1] + small[2:3]).astype(bf16)
     w_kv, w_q, w_out_t = attn_weights(weights)
     kv[me] = dot(normed, w_kv, NN).astype(bf16)
-    all_here(5 if follows else 9)
+    all_here(5 if follows else 11)
     far = (me + 2) % 4
     copies = [
         remote(kv.at[at], kv.at[at], kv_send.at[k], kv_recv.at[k], peer)
@@ -525,7 +578,16 @@
     if not follows:
         nears = spread_near(whole, sp_send, sp_recv)
         fars = spread_far(whole, sp_send, sp_recv)
-        for copy in nears:
+        at_x, at_z = places()
+        aheads = [pltpu.make_async_copy(ahead, all_ahead.at[at_x, at_z], own_sem)]
+        for route in range(2):
+            rows = half(ahead.shape[0], route)
+            for k in range(1, 4):
+                n, peer = 3 * route + k - 1, axis_peer(route == 0, k)[0]
+                aheads.append(
+                    remote(ahead.at[rows], all_ahead.at[at_x, at_z, rows], ah_send.at[n], ah_recv.at[n], peer)
+                )
+        for copy in nears + aheads:
             copy.start()
     queries = dot(normed, w_q, NN).astype(bf16)
     q[...] = queries
@@ -553,13 +615,13 @@
     for copy in copies:
         copy.wait_send()
     if not follows:
-        for copy in fars:
+        for copy in fars + aheads:
             copy.wait()
         for copy in nears:
             copy.wait_send()
 
 
-def attend_forward(x, before, small, weights, dead, some, cid):
+def attend_forward(x, before, small, weights, dead, some, ahead, cid):
     args = (x, *before, small, weights, dead)
     shapes = [(ROWS, WIDTH), (4, ROWS, 2 * WIDTH), (ROWS, WIDTH), (2, 4, 80, 384)]
     in_specs, out_specs = [VMEM] * len(args), [VMEM] * 5
@@ -567,11 +629,11 @@
     if before:
         shapes.append((PAIR, D))
     else:
-        args += (some,)
-        shapes.append(some.shape)
-        in_specs.append(pl.BlockSpec(memory_space=pl.ANY))
-        out_specs[4] = pl.BlockSpec(memory_space=pl.ANY)
-        scratch += dma_sems(8)
+        args += (ahead, some)
+        shapes += [some.shape, (4, 4) + ahead.shape]
+        in_specs += [VMEM, ANY]
+        out_specs[4:] = [ANY, ANY]
+        scratch += dma_sems(8, 6) + [pltpu.SemaphoreType.DMA]
     return pl.pallas_call(
         functools.partial(attend_forward_kernel, bool(before)),
         out_shape=[jax.ShapeDtypeStruct(s, bf16) for s in shapes],
@@ -604,16 +666,25 @@
 
 
 def experts_forward_kernel(
-    x, att, small, routes, weights, result, b, gates, total, out, part, landed, *sems
+    x, att, small, routes, _, weights, result, ahead, b, gates, total, ah_send, ah_recv, out, part, landed, *sems
 ):
     expert = pl.program_id(0)
     sums = (True, out, part, landed, *sems)
+    aheads = []
+    for route in range(2):
+        slabs = line(ahead, route, places()[1 - route], half(ahead.shape[2], route))
+        for k in range(1, 4):
+            n, peer = 3 * route + k - 1, axis_peer(route == 1, k)[0]
+            aheads.append(remote(slabs, slabs, ah_send.at[n], ah_recv.at[n], peer))
 
     @pl.when(expert == 0)
     def _():
-        arrive(tp_peers() + [{"core": 1 - lax.axis_index("core")}])
+        arrive(tp_peers() + [{"core": 1 - lax.axis_index("core")}] + axis_peers(1, 2, 3))
         experts_setup(x, att, small, routes, b, gates)
         total[...] = jnp.zeros_like(total)
+        all_here(10)
+        for copy in aheads:
+            copy.start()
 
     w_in, w_out_t = expert_weights(weights)
     u = dot(b[...], w_in, NN)
@@ -625,47 +696,55 @@
     def _():
         for block in range(2):
             put_chunks(part, block, total[ROWS * block : ROWS * block + ROWS].astype(bf16))
-        all_here(4)
         sum_start(*sums)
         sum_middle(*sums)
         sum_end(*sums)
         result[...] = out[...]
+        for copy in aheads:
+            copy.wait()
 
 
 def fixed(shape):
     return pl.BlockSpec(shape, lambda e: (0,) * len(shape))
 
 
-def experts_forward(x, att, small, routes, weights, cid):
+def experts_forward(x, att, small, routes, ahead, weights, cid):
     args = (x, att, small, routes)
     return pl.pallas_call(
         experts_forward_kernel,
         grid=(EXPERTS,),
-        out_shape=jax.ShapeDtypeStruct((2, 4, 80, 384), bf16),
-        in_specs=[fixed(a.shape) for a in args] + [pl.BlockSpec((16, 96, FE), lambda e: (0, e, 0))],
-        out_specs=fixed((2, 4, 80, 384)),
+        out_shape=[jax.ShapeDtypeStruct((2, 4, 80, 384), bf16), jax.ShapeDtypeStruct(ahead.shape, bf16)],
+        in_specs=[fixed(a.shape) for a in args] + [ANY, pl.BlockSpec((16, 96, FE), lambda e: (0, e, 0))],
+        out_specs=[fixed((2, 4, 80, 384)), ANY],
         scratch_shapes=[
             pltpu.VMEM((PAIR, D), bf16),
             pltpu.VMEM((PAIR, EXPERTS), f32),
             pltpu.VMEM((PAIR, D), f32),
-            pltpu.VMEM((2, 4, 80, 384), bf16),
         ]
+        + dma_sems(6)
+        + [pltpu.VMEM((2, 4, 80, 384), bf16)]
         + sum_scratch(True, 80),
+        input_output_aliases={4: 1},
         compiler_params=params(cid, 56),
         name="experts_forward",
-    )(*args, weights)
+    )(*args, ahead, weights)
 
 
 def experts_backward_kernel(
-    steps, x, att, small, routes, grad, extra, some, weights, result, moe_part, own_sum, grad_w,
-    b, gates, total, moe, gate_t, gated_all, grad_u_all, out, part, landed, *sems,
+    x, att, small, routes, grad, extra, some, weights, result, moe_part, own_sum, some_attn, grad_w,
+    b, gates, total, moe, gate_grads, gated_all, grad_u_all, out, part, landed, *sems,
 ):
     step = pl.program_id(0)
     sums = (True, out, part, landed, *sems)
     with_moe = moe_part is not None
     if not with_moe:
-        *sems, slabs, slab_send, slab_recv = sems
+        *sems, slabs, slab_send, slab_recv, attn_slabs, at_send, at_recv = sems
         sums, lasts = (True, out, part, landed, *sems), last_copies(some, slabs, slab_send, slab_recv)
+        for route in range(2):
+            for k in range(1, 4):
+                n, (peer, to) = 3 * route + k - 1, axis_peer(route == 1, k)
+                slab = extra.at[0, :, to] if route == 0 else extra.at[1, to]
+                lasts.append(remote(slab, attn_slabs.at[route, k - 1], at_send.at[n], at_recv.at[n], peer))
 
     @pl.when(step == 0)
     def _():
@@ -674,8 +753,13 @@
             arrive(axis_peers(1, 2, 3))
         experts_setup(x, att, small, routes, b, gates)
         total[...] = jnp.zeros_like(total)
+        gate_grads[...] = jnp.zeros_like(gate_grads)
         if with_moe:
             moe[...] = jnp.zeros_like(moe)
+        all_here(4 if with_moe else 10)
+        if not with_moe:
+            for copy in lasts:
+                copy.start()
 
     @pl.when(step < EXPERTS)
     def _():
@@ -689,7 +773,9 @@
         if with_moe:
             moe[...] += dot(gated, w_out_t, NT)
         back = dot(grad[...], w_out_t, NN)
-        gate_t[step] = dot_exact(jnp.ones((8, FE), f32), back * active, NT)
+        ids = lax.broadcasted_iota(jnp.int32, (PAIR, 128), 1)
+        gate_grad = jnp.sum(back * active, axis=1, keepdims=True)
+        gate_grads[...] = jnp.where(ids == step, gate_grad, gate_grads[...])
         grad_u = (gate * back * gelu_slope(u, t)).astype(bf16)
         grad_u_all[step] = grad_u
         total[...] += dot(grad_u, w_in, NT)
@@ -697,22 +783,17 @@
     @pl.when(step == EXPERTS - 1)
     def _():
         part[...] = jnp.zeros_like(part)
+        pick = lax.broadcasted_iota(jnp.int32, (16, 128), 0) == lax.broadcasted_iota(jnp.int32, (16, 128), 1)
+        pick = (pick & (lax.broadcasted_iota(jnp.int32, (16, 128), 0) < EXPERTS)).astype(f32).astype(bf16)
         for block in range(2):
             lines = slice(ROWS * block, ROWS * block + ROWS)
             put_chunks(part, block, total[lines].astype(bf16))
-            table = jnp.concatenate(
-                [gate_t[e, 0:1, lines] for e in range(EXPERTS)] + [jnp.zeros((12, ROWS), f32)], axis=0
-            )
-            part[block, 0, 80:96, 0:ROWS] = table.astype(bf16)
+            part[block, 0, 80:96, 0:ROWS] = dot(pick, gate_grads[lines].astype(bf16), NT).astype(bf16)
             if with_moe:
                 put_chunks(moe_part, block, moe[lines].astype(bf16))
-        all_here(4 if with_moe else 10)
         sum_start(*sums)
-        if not with_moe:
-            for copy in lasts:
-                copy.start()
-
-    @pl.when((step >= EXPERTS) & (step < 2 * EXPERTS))
+
+    @pl.when(step >= EXPERTS)
     def _():
         at = step - EXPERTS
         grad_w[:, 0:48] = dot(b[...], grad_u_all[at], TN).astype(bf16).reshape(16, 48, FE)
@@ -722,50 +803,55 @@
     def _():
         sum_middle(*sums)
 
-    if steps > 2 * EXPERTS:
-
-        @pl.when(step == 2 * EXPERTS)
+    if not with_moe:
+
+        @pl.when(step == 2 * EXPERTS - 2)
         def _():
-            grad_w[:, 0:48] = extra[0].reshape(16, 48, FE)
-            grad_w[:, 48:96] = extra[1].reshape(16, 48, FE)
-
-    @pl.when(step == steps - 1)
+            for copy in lasts:
+                copy.wait()
+            add_slabs(some, slabs, own_sum)
+            at_x, at_z = places()
+            for route in range(2):
+
+                def add(j, carry, route=route):
+                    attn = (extra[0, j, at_z] if route == 0 else extra[1, at_x, j]).astype(f32)
+                    for k in range(3):
+                        attn = attn + attn_slabs[route, k, j].astype(f32)
+                    some_attn[route, j] = attn.astype(bf16)
+                    return carry
+
+                lax.fori_loop(0, 4, add, 0)
+
+    @pl.when(step == 2 * EXPERTS - 1)
     def _():
         sum_end(*sums)
         result[...] = out[...]
-        if not with_moe:
-            for copy in lasts:
-                copy.wait()
-            add_slabs(some, slabs, own_sum)
 
 
 def experts_backward(x, att, small, routes, grad, extra, some, weights, cid):
     args = (x, att, small, routes, grad)
-    steps = 2 * EXPERTS
     shapes = [(2, 4, 96, 384)]
-    blocks = [fixed((2, 4, 96, 384))]
     scratch = []
     if extra is None:
         shapes.append((2, 4, 80, 384))
-        blocks.append(fixed((2, 4, 80, 384)))
 
         def kernel(*refs):
-            experts_backward_kernel(steps, *refs[:5], None, None, *refs[5:8], None, *refs[8:])
+            experts_backward_kernel(*refs[:5], None, None, *refs[5:8], None, None, *refs[8:])
     else:
-        args, steps = args + (extra, some), steps + 1
+        args += (extra, some)
         slab = some.shape[1:]
-        shapes.append(slab)
-        blocks.append(fixed(slab))
+        shapes += [slab, (2, 4, 48, FE)]
         scratch = [pltpu.VMEM((3,) + slab, bf16)] + dma_sems(6)
+        scratch += [pltpu.VMEM((2, 3, 4, 48, FE), bf16)] + dma_sems(6)
 
         def kernel(*refs):
-            experts_backward_kernel(steps, *refs[:9], None, *refs[9:])
-
-    grads = steps - EXPERTS
+            experts_backward_kernel(*refs[:9], None, *refs[9:])
+
+    blocks = [fixed(shape) for shape in shapes]
     return pl.pallas_call(
         kernel,
-        grid=(steps,),
-        out_shape=[jax.ShapeDtypeStruct(s, bf16) for s in shapes + [(16, 96 * grads, FE)]],
+        grid=(2 * EXPERTS,),
+        out_shape=[jax.ShapeDtypeStruct(s, bf16) for s in shapes + [(16, 96 * EXPERTS, FE)]],
         in_specs=[fixed(a.shape) for a in args]
         + [pl.BlockSpec((16, 96, FE), lambda s: (0, jnp.minimum(s, EXPERTS - 1), 0))],
         out_specs=blocks + [pl.BlockSpec((16, 96, FE), lambda s: (0, jnp.maximum(s - EXPERTS, 0), 0))],
@@ -774,7 +860,7 @@
             pltpu.VMEM((PAIR, EXPERTS), f32),
             pltpu.VMEM((PAIR, D), f32),
             pltpu.VMEM((PAIR, D), f32),
-            pltpu.VMEM((EXPERTS, 8, PAIR), f32),
+            pltpu.VMEM((PAIR, 128), f32),
             pltpu.VMEM((EXPERTS, PAIR, FE), bf16),
             pltpu.VMEM((EXPERTS, PAIR, FE), bf16),
             pltpu.VMEM((2, 4, 96, 384), bf16),
@@ -817,7 +903,7 @@
     tables = [back[block, 0, 80:96, 0:ROWS].astype(f32)[0:EXPERTS] for block in range(2)]
     gate_grads = jnp.where(named, jnp.concatenate(tables, axis=1), 0.0)
     grad_logits = chances * (gate_grads - jnp.sum(chances * gate_grads, axis=0, keepdims=True))
-    grad_b = pair_rows(back) + dot_exact(grad_logits, router, TN)
+    grad_b = pair_rows(back) + dot_split(grad_logits, router.astype(bf16), TN)
     grad_h[...] = grad[...].astype(f32) + norm_back(grad_b, unit, scale, small[1:2])
     grad_att = grad_h[own_rows(core)].astype(bf16)
     w_kv, w_q, w_out_t = attn_weights(weights)
@@ -847,13 +933,15 @@
     crosses[1].start()
     crosses[0].start()
     if with_moe:
-        pre = sum_cores(*moe_sums)
-        pre.start()
+        pres = sum_cores(*moe_sums)
+        for copy in pres:
+            copy.start()
     crosses[1].wait_recv()
     kv_out[...] = (parts[far].astype(f32) + kv_landed[1].astype(f32)).astype(bf16)
     onward.start()
     if with_moe:
-        pre.wait_recv()
+        for copy in pres:
+            copy.wait_recv()
         for j in range(4):
             moe_sum = moe_part[core, j].astype(f32) + moe_crossed[j].astype(f32)
             moe_crossed[j] = moe_sum.astype(bf16)
@@ -877,7 +965,7 @@
     kept = jnp.where(own, grad_b, 0.0)
     grad_small[1:2] = jnp.sum(kept * unit, axis=0, keepdims=True)
     grad_small[3:4] = jnp.sum(kept, axis=0, keepdims=True)
-    grad_small[4:8] = dot_exact(jnp.where(own_lanes, grad_logits, 0.0), b.astype(f32), NN)
+    grad_small[4:8] = dot_split(jnp.where(own_lanes, grad_logits, 0.0), b, NN)
     unit_one, scale_one = norm_parts(x[...].astype(f32))
     both_units[...] = unit_one
     normed = (both_units[own_rows(core)] * small[0:1] + small[2:3]).astype(bf16)
@@ -911,7 +999,8 @@
     for copy in crosses + [onward]:
         copy.wait_send()
     if with_moe:
-        pre.wait_send()
+        for copy in pres:
+            copy.wait_send()
         for copy in moe_terms:
             copy.wait_send()
         for copy in moe_results:
@@ -955,7 +1044,7 @@
         args, in_specs = args + (moe_part,), in_specs + [VMEM]
         shapes.append(((4, 80, 384), bf16))
         scratch += [pltpu.VMEM((3, 80, 384), bf16)] + dma_sems(3, 3)
-        scratch += [pltpu.VMEM((4, 80, 384), bf16)] + dma_sems(1)
+        scratch += [pltpu.VMEM((4, 80, 384), bf16)] + dma_sems(2)
     return pl.pallas_call(
         functools.partial(attend_backward_kernel, with_moe),
         out_shape=[jax.ShapeDtypeStruct(*s) for s in shapes],
@@ -993,7 +1082,7 @@
     chip = jnp.concatenate(
         [low_half[:480].reshape(20, 24, FE), high_half[:480].reshape(20, 24, FE)], axis=1
     )
-    later = jnp.concatenate([chip[0:8], chip[16:18]]).reshape(480, FE)
+    later, ahead = chip[0:8].reshape(384, FE), chip[16:18].reshape(96, FE)
     urgent = jnp.concatenate([chip[18:20].reshape(96, FE), low_half[480:496], high_half[480:496]])
 
     turned = jnp.pad(
@@ -1018,15 +1107,14 @@
     ]
     route_cols = [rows.T for rows in route_rows]
 
-    attn_w0 = packs[:, 0:96]
-    q0, kv0, mixed0, att0, experts_zero = attend_forward(x0, (), smalls[0], attn_w0, dead, some, 3)
-    experts_zero = experts_zero.reshape(16, 480, 384)
-    attn_w1 = experts_zero[:, 384:480]
+    q0, kv0, mixed0, att0, experts_zero, ahead = attend_forward(x0, (), smalls[0], packs, dead, some, ahead, 3)
+    experts_zero = experts_zero.reshape(16, 384, FE)
     shard, att0 = lax.optimization_barrier((chip[8:16].reshape(384, FE), att0))
     experts_one = lax.all_gather(shard, CHIPS, axis=0)
-    moe0 = experts_forward(x0, att0, smalls[0], route_cols[0], experts_zero, 4)
+    moe0, attn_w1 = experts_forward(x0, att0, smalls[0], route_cols[0], ahead, experts_zero, 4)
+    attn_w1 = attn_w1.reshape(16, 96, FE)
     q1, kv1, mixed1, att1, x1 = attend_forward(
-        x0, (att0, moe0), smalls[1], attn_w1, dead, None, 5
+        x0, (att0, moe0), smalls[1], attn_w1, dead, None, None, 5
     )
     back, moe_part, grad_experts1 = experts_backward(
         x1, att1, smalls[1], route_cols[1], cotangent, None, None, experts_one, 6
@@ -1036,11 +1124,12 @@
         moe_part,
         7,
     )
-    back, sums1, grad_experts0 = experts_backward(
+    grad_attn1 = grad_attn1.reshape(2, 4, 4, 48, FE)
+    back, sums1, some_attn, grad_experts0 = experts_backward(
         x0, att0, smalls[0], route_cols[0], grad_x1, grad_attn1, some, experts_zero, 8
     )
     grad_x0, grad_small0, grad_attn0, some = attend_backward(
-        (x0, att0, smalls[0], route_rows[0], grad_x1, back, q0, kv0, mixed0, dead, attn_w0, grad_experts0.reshape(4, 4, 480, FE)),
+        (x0, att0, smalls[0], route_rows[0], grad_x1, back, q0, kv0, mixed0, dead, packs, grad_experts0.reshape(4, 4, 384, FE)),
         None,
         9,
     )
@@ -1059,8 +1148,8 @@
     tiny = jnp.stack([grad_small0, grad_small1]).astype(bf16).reshape(2, 8, 16, 2, 24)
     tiny = tiny.transpose(0, 2, 3, 1, 4).reshape(2, 16, 16, 24)
     tiny = jnp.pad(tiny, ((0, 0), (0, 0), (0, 0), (0, 384 - 24)))
-    packs = jnp.concatenate([grad_attn0.reshape(2, 16, 48, 384), tiny], axis=2)
-    own, landed, got1, own0, got0 = end_exchange(packs, sent, sums1, some)
+    packs = jnp.concatenate([grad_attn0.reshape(2, 16, 48, 384), tiny], axis=2).reshape(2, 4, 4, 64, FE)
+    own, landed, got1, own0, got0 = end_exchange(packs, sent, sums1, some, some_attn)
     landed = landed.astype(f32)
     ends = jnp.where(high == 0, jnp.stack([kept, landed]), jnp.stack([landed, kept]))
 

time: 332 us -> 307 us (0.925); the launches traced: 327 us -> 307 us
  Pallas kernels: 276 us -> 254 us
    pallas_call x2, Pallas kernels: 62.9 us -> 51.5 us  [attend_forward(): pl.pallas_call(functools.partial(attend_forward_kernel, bool(before)), ou...]
    pallas_call x2, Pallas kernels: 70.1 us -> 63.5 us  [attend_backward(): pl.pallas_call(functools.partial(attend_backward_kernel, with_moe), out_s...]
    slice x2 -> x0, local copies, waits for them, and re-layouts: 4.93 us -> none  [the longest x1 2.53 us: shards(): attn_w0 = packs[:, 0:96]]
  transfers between devices with their start and end apart: 1 -> 1, of which waited for: 0 -> 1; matrix products, arithmetic and copies ran while one was open for 2% -> 2% of each run, Pallas kernels for 15% -> 15%
where the time goes in v4:
time: 307 us
  Pallas kernels  254 us (83%)
  local copies, waits for them, and re-layouts  18.9 us (6%)
  other arithmetic  15.5 us (5%)
  between operations  14.6 us (5%)
  waiting for transfers between devices  3.21 us (1%)
    pallas_call x2, Pallas kernels, attend_backward(): pl.pallas_call(functools.partial(attend_backward_kernel, with_moe), out_s...  63.5 us
    pallas_call x2, Pallas kernels, attend_forward(): pl.pallas_call(functools.partial(attend_forward_kernel, bool(before)), ou...  51.5 us
    pallas_call x2, Pallas kernels, experts_backward(): pl.pallas_call(kernel, grid=(2 * EXPERTS,), out_shape=[jax.ShapeDtypeStru...  51.1 us
    pallas_call x1, Pallas kernels, start_exchange(): pl.pallas_call(start_kernel, out_shape=[jax.ShapeDtypeStruct(s, bf16) for...  32.9 us
    pallas_call x1, Pallas kernels, end_exchange(): pl.pallas_call(end_kernel, out_shape=[jax.ShapeDtypeStruct((2, 64, FE), f...  29.1 us
    pallas_call x1, Pallas kernels, experts_forward(): pl.pallas_call(experts_forward_kernel, grid=(EXPERTS,), out_shape=[jax.Sh...  23.4 us
  transfers between devices with their start and end apart: 1, of which 1 were waited for; matrix products, arithmetic and copies ran while one was open for 2% of the time, Pallas kernels for 15%

profile of v4, /device:TPU:1, one launch (start us, length us, event | category | flops | bytes accessed | tf_op | source)
XLA Modules:
  0.0 306.6 jit_solution(3428032778941853428)
XLA Ops:
  8.0 1.1 pad_maximum_fusion.2
  10.2 1.2 constant_dynamic-slice_fusion.6
  12.3 2.9 cross.1
  18.4 32.9 %start_exchange.1 = (bf16[2,2,176,768]{3,2,1,0:T(8,128)(2,1)}, bf16[4,4,128,384]{3,2,1,0:T(8,128)(2,1)}, bf16[4,4,384,384]{3,2,1,0:T(8,128)(2,1)}) custom-call(bf16[2,176,768]{2,1,0:T(8,128)(2,1)} %fusion.5.images, bf16[128,384]{1,0:T(8,128)(2,1)} %pad_maximum_fusion.10.urgent, bf16[384,384]{1,0:T(8,128)(2,1)} %bitcast.144), custom_call_target="tpu_custom_call" | custom-call | tf_op jit(solution)/shard_map/start_exchange/pallas_call | solution.py:280
  51.3 2.0 fusion.19
  53.3 1.1 slice.144
  56.1 28.8 %attend_forward.2 = (bf16[160,192]{1,0:T(8,128)(2,1)}, bf16[4,160,384]{2,1,0:T(8,128)(2,1)}, bf16[160,192]{1,0:T(8,128)(2,1)}, bf16[2,4,80,384]{3,2,1,0:T(8,128)...) custom-call(bf16[320,768]{1,0:T(8,128)(2,1)} %bitcast.119, ...), custom_call_target="tpu_custom_call", output_to_operand_aliasing={{4}: (5, {})} | custom-call | tf_op jit(solution)/shard_map/attend_forward/pallas_call | solution.py:637
  88.5 23.4 %experts_forward.1 = (bf16[2,4,80,384]{3,2,1,0:T(8,128)(2,1)}, bf16[4,4,96,384]{3,2,1,0:T(8,128)(2,1)}) custom-call(bf16[320,768]{1,0:T(8,128)(2,1)} %bitcast.120, bf16[2,4,80,384]{3,2,1,0:T(8,128)(2,1)} %get-tuple-element.51.att.refs_1_, f32[8,768]{1,0:T(8,128)} %reshape.269.refs_1_.small.refs_2_, ...), custom_call_target="tpu_custom_call", output_to_operand_aliasing={{1}: (4, {})} | custom-call | tf_op jit(solution)/shard_map/experts_forward/pallas_call | solution.py:713
  111.9 22.8 %attend_forward.3 = (bf16[160,192]{1,0:T(8,128)(2,1)}, bf16[4,160,384]{2,1,0:T(8,128)(2,1)}, bf16[160,192]{1,0:T(8,128)(2,1)}, bf16[2,4,80,384]{3,2,1,0:T(8,128)(2,1)}, bf16[320,768]{1,0:T(8,128)(2,1)}) custom-call(bf16[320,768]{1,0:T(8,128)(2,1)} %bitcast.121, bf16[2,4,80,384]{3,2,1,0:T(8,128)(2,1)} %get-tuple-element.51.att.refs_1_, ...), custom_call_target="tpu_custom_call" | custom-call | tf_op jit(solution)/shard_map/attend_forward/pallas_call | solution.py:637
  134.6 1.0 constant_dynamic-slice_fusion.3
  137.2 3.2 %all-gather.3.cloned.1.call-done = bf16[6144,384]{1,0:T(8,128)(2,1)} async-done(((bf16[384,384]{1,0:T(8,128)(2,1)}), bf16[6144,384]{1,0:T(8,128)(2,1)}) %all-gather.3.cloned.1.call-update) | async-done | bytes 4718608 | tf_op jit(solution)/shard_map/all_gather | solution.py:1113
  140.4 26.0 %experts_backward.2 = (bf16[2,4,96,384]{3,2,1,0:T(8,128)(2,1)}, bf16[2,4,80,384]{3,2,1,0:T(8,128)(2,1)}, bf16[16,384,384]{2,1,0:T(8,128)(2,1)}) custom-call(bf16[320,768]{1,0:T(8,128)(2,1)} %get-tuple-element.56.refs_0_, bf16[2,4,80,384]{3,2,1,0:T(8,128)(2,1)} %get-tuple-element.57.refs_1_, f32[8,768]{1,0:T(8,128)} %reshape.271.refs_3_.refs_2_, ...), custom_call_target="tpu_custom_call" | custom-call | tf_op jit(solution)/shard_map/experts_backward/pallas_call | solution.py:851
  166.4 32.4 %attend_backward.2 = (bf16[320,768]{1,0:T(8,128)(2,1)}, f32[8,768]{1,0:T(8,128)}, bf16[2,768,384]{2,1,0:T(8,128)(2,1)}, bf16[4,384,384]{2,1,0:T(8,128)(2,1)}, bf16[4,80,384]{2,1,0:T(8,128)(2,1)}) custom-call(bf16[320,768]{1,0:T(8,128)(2,1)} %get-tuple-element.56.refs_0_, bf16[2,4,80,384]{3,2,1,0:T(8,128)(2,1)} %get-tuple-element.57.refs_1_, ...), custom_call_target="tpu_custom_call" | custom-call | tf_op jit(solution)/shard_map/attend_backward/pallas_call | solution.py:1048
  198.8 1.1 copy.77
  200.3 25.1 %experts_backward.3 = (bf16[2,4,96,384]{3,2,1,0:T(8,128)(2,1)}, bf16[384,384]{1,0:T(8,128)(2,1)}, bf16[2,4,48,384]{3,2,1,0:T(8,128)(2,1)}, bf16[16,384,384]{2,1,0:T(8,128)(2,1)}) custom-call(bf16[320,768]{1,0:T(8,128)(2,1)} %bitcast.122, bf16[2,4,80,384]{3,2,1,0:T(8,128)(2,1)} %get-tuple-element.51.att.refs_1_, f32[8,768]{1,0:T(8,128)} %reshape.269.refs_1_.small.refs_2_, ...), custom_call_target="tpu_custom_call" | custom-call | tf_op jit(solution)/shard_map/experts_backward/pallas_call | solution.py:851
  225.4 31.2 %attend_backward.3 = (bf16[320,768]{1,0:T(8,128)(2,1)}, f32[8,768]{1,0:T(8,128)}, bf16[2,768,384]{2,1,0:T(8,128)(2,1)}, bf16[4,384,384]{2,1,0:T(8,128)(2,1)}) custom-call(bf16[320,768]{1,0:T(8,128)(2,1)} %bitcast.123, bf16[2,4,80,384]{3,2,1,0:T(8,128)(2,1)} %get-tuple-element.51.att.refs_1_, f32[8,768]{1,0:T(8,128)} %reshape.269.refs_1_.small.refs_2_, ...), custom_call_target="tpu_custom_call" | custom-call | tf_op jit(solution)/shard_map/attend_backward/pallas_call | solution.py:1048
  256.6 1.0 dynamic-slice_convert_fusion.1
  260.4 1.4 pad_maximum_fusion.part
  261.8 29.1 %end_exchange.1 = (f32[2,64,384]{2,1,0:T(8,128)}, bf16[160,768]{1,0:T(8,128)(2,1)}, bf16[384,384]{1,0:T(8,128)(2,1)}, bf16[480,384]{1,0:T(8,128)(2,1)}, bf16[480,384]{1,0:T(8,128)(2,1)}) custom-call(bf16[2,4,4,64,384]{4,3,2,1,0:T(8,128)(2,1)} %pad_maximum_fusion.part, bf16[160,768]{1,0:T(8,128)(2,1)} %fusion.10.image, ...), custom_call_target="tpu_custom_call" | custom-call | tf_op jit(solution)/shard_map/end_exchange/pallas_call | solution.py:476
  291.0 1.0 dynamic-slice_convert_fusion.2
  291.9 1.0 dynamic-slice_convert_fusion.3
  293.0 0.9 dynamic-slice_bitcast_fusion.1
  297.0 1.1 fusion.4
  298.7 1.0 maximum_select_fusion.1
  (105 shorter events, 19.4 us)
Async XLA Ops:
  7.2 133.2 %all-gather.3.cloned.1.call-start = ((), (), s32[]{:S(2)}) async-start(), calls=%async_computation | async-start | bytes 5013504 | tf_op jit(solution)/shard_map/all_gather | solution.py:1113
  9.1 0.8 slice-start
  9.1 0.9 copy-start.11
  9.1 0.9 copy-start.12
  9.1 0.9 copy-start.13
  11.4 0.7 copy-start.9
  15.4 1.6 copy-start.10
  15.4 1.5 copy-start.3
  53.3 2.1 copy-start.14
  85.7 26.1 %copy-start.6 = (f32[2,320]{1,0:T(2,128)}, f32[2,320]{1,0:T(2,128)S(1)}, u32[]{:S(2)}) copy-start(f32[2,320]{1,0:T(2,128)S(1)} %reshape.270.refs_3_) | copy-start | bytes 7684
  87.7 24.2 %copy-start.7 = (f32[2,320]{1,0:T(2,128)}, f32[2,320]{1,0:T(2,128)S(1)}, u32[]{:S(2)}) copy-start(f32[2,320]{1,0:T(2,128)S(1)} %reshape.272.refs_3_) | copy-start | bytes 7684
  225.4 33.1 %copy-start.8 = (f32[8,768]{1,0:T(8,128)S(1)}, f32[8,768]{1,0:T(8,128)}, u32[]{:S(2)}) copy-start(f32[8,768]{1,0:T(8,128)} %get-tuple-element.77) | copy-start | bytes 73732
  256.5 2.4 copy-start
  259.0 1.4 copy-start.1
  292.9 2.6 copy-start.4
  295.5 1.3 copy-start.2
  295.5 1.3 copy-start.5
Sparse Core Ops, SparseCore 0:
  85.0 55.3 all-gather.2

commit v5 on v4

--- a/solution.py
+++ b/solution.py
@@ -220,6 +220,11 @@
     return pl.ds(route * (rows // 2), rows // 2)
 
 
+def uneven(rows, route):
+    first = {128: 80, 64: 48}[rows]
+    return pl.ds(first, rows - first) if route else pl.ds(0, first)
+
+
 def line(whole, route, second, rows):
     return whole.at[:, second, rows] if route == 0 else whole.at[second, :, rows]
 
@@ -244,7 +249,7 @@
     firsts, seconds, laters = [], [], []
     for route in range(2):
         b = (at_z, at_x)[route]
-        rows, late = half(urgent.shape[0], route), half(later.shape[0], route)
+        rows, late = uneven(urgent.shape[0], route), half(later.shape[0], route)
         for k in range(1, 4):
             peer, _ = axis_peer(route == 0, k)
             n = 3 * route + k - 1
@@ -388,9 +393,21 @@
 
 
 def end_kernel(
-    part, image, half_sum, some, some_attn, out, out_image, out_half, own_sum, other_sum,
-    landed, sums, pieces, mids, lands, slabs, attn_slabs, cx_s, cx_r, sl_s, sl_r, at_s, at_r, p1_s, p1_r, p2_s, p2_r,
+    part, image, half_sum, some, some_attn, tiny, out_image, grad_in, grad_out, grad_attn,
+    out, out_half, own_sum, other_sum, landed, sums, pieces, mids, lands, slabs, attn_slabs, cx_s, cx_r, sl_s, sl_r, at_s, at_r, p1_s, p1_r, p2_s, p2_r,
 ):
+    def own_lines(rows):
+        rows = rows.astype(f32)
+        return jnp.where(core == 0, rows[0:24], rows[24:48])
+
+    def put_experts(layer, own, got):
+        for at in range(2 * EXPERTS):
+            rows = slice(48 * at, 48 * at + 48)
+            mine, others = own_lines(own[rows]), own_lines(got[rows])
+            ref = grad_out if at % 2 else grad_in
+            ref[layer, at // 2, :, 0:FE] = jnp.where(core == 0, mine, others)
+            ref[layer, at // 2, :, FE:] = jnp.where(core == 0, others, mine)
+
     core, x = lax.axis_index("core"), lax.axis_index("x")
     other = {"core": 1 - core}
     arrive(axis_peers(1, 2, 3) + [other])
@@ -400,7 +417,7 @@
     lasts = last_copies(some, slabs, sl_s, sl_r)
     firsts, seconds = [], []
     for route in range(2):
-        rows = half(64, route)
+        rows = uneven(64, route)
         for k in range(1, 4):
             peer, at = axis_peer(route == 0, k)
             n = 3 * route + k - 1
@@ -426,11 +443,13 @@
     lax.fori_loop(0, 16, add, 0)
     for copy in firsts + [swap]:
         copy.start()
+    halves.wait_recv()
+    put_experts(1, half_sum, out_half)
     for copy in firsts:
         copy.wait_recv()
     at_x, at_z = places()
     for route in range(2):
-        rows = half(64, route)
+        rows = uneven(64, route)
 
         def gather(j, carry, route=route, rows=rows):
             total = (sums[j, at_z, rows] if route == 0 else sums[at_x, j, rows]).astype(f32)
@@ -456,30 +475,45 @@
     for copy in seconds:
         copy.wait()
     for route in range(2):
-        rows = half(64, route)
+        rows = uneven(64, route)
         total = mids[places()[route], rows].astype(f32)
         for k in range(3):
             total = total + lands[k, rows].astype(f32)
         out[core, rows] = total
     given = remote(out.at[core], out.at[core], cx_s.at[4], cx_r.at[4], other)
     given.start()
-    for copy in firsts:
+    final.wait()
+    put_experts(0, own_sum, other_sum)
+    given.wait()
+    for route in range(2):
+        first = 384 + 48 * route
+        rows = slice(first, first + 48)
+        grad_attn[0, route] = own_lines(out[route, 0:48])
+        grad_attn[1, route] = own_lines(own_sum[rows]) + own_lines(other_sum[rows])
+        tiny[route] = jnp.where(core == 0, out[route, 48:56], out[route, 56:64])
+    for copy in firsts + [halves]:
         copy.wait_send()
-    for copy in (given, final, swap, halves):
-        copy.wait()
+    swap.wait()
 
 
 def end_exchange(part, image, half_sum, some, some_attn):
     slab = (480, FE)
-    scratch = [(4, 4, 64, FE)] * 2 + [(3, 4, 64, FE), (4, 64, FE), (3, 64, FE)]
+    scratch = [half_sum.shape, slab, slab] + [(4, 4, 64, FE)] * 2 + [(3, 4, 64, FE), (4, 64, FE), (3, 64, FE)]
     scratch += [(3,) + some.shape[1:], (2, 3, 48, FE)]
     return pl.pallas_call(
         end_kernel,
-        out_shape=[jax.ShapeDtypeStruct((2, 64, FE), f32)]
-        + [jax.ShapeDtypeStruct(s, bf16) for s in (image.shape, half_sum.shape, slab, slab)],
+        out_shape=[
+            jax.ShapeDtypeStruct((2, 8, FE), f32),
+            jax.ShapeDtypeStruct(image.shape, bf16),
+            jax.ShapeDtypeStruct((2, EXPERTS, 24, D), f32),
+            jax.ShapeDtypeStruct((2, EXPERTS, 24, D), f32),
+            jax.ShapeDtypeStruct((2, 2, 24, FE), f32),
+        ],
         in_specs=[VMEM] * 5,
         out_specs=[VMEM] * 5,
-        scratch_shapes=[pltpu.VMEM(s, bf16) for s in scratch] + dma_sems(5, 6, 6, 6, 6),
+        scratch_shapes=[pltpu.VMEM((2, 64, FE), f32)]
+        + [pltpu.VMEM(s, bf16) for s in scratch]
+        + dma_sems(5, 6, 6, 6, 6),
         compiler_params=params(2, 56),
         name="end_exchange",
     )(part, image, half_sum, some, some_attn)
@@ -654,9 +688,15 @@
 def experts_setup(x, att, small, routes, b, gates):
     unit, _ = norm_parts(x[...].astype(f32) + pair_rows(att))
     b[...] = (unit * small[1:2] + small[3:4]).astype(bf16)
+    put_gates(b, small, routes, gates)
+
+
+def put_gates(b, small, routes, gates):
     probs = softmax(dot(b[...], small[4:8].astype(bf16), NT), -1)
     ids = lax.broadcasted_iota(jnp.int32, (PAIR, EXPERTS), 1).astype(f32)
-    named = (routes[:, 0:1] == ids) | (routes[:, 1:2] == ids)
+    ones = lax.broadcasted_iota(jnp.int32, (16, 16), 0) == lax.broadcasted_iota(jnp.int32, (16, 16), 1)
+    lines = dot(routes[...], ones.astype(f32).astype(bf16), TN)
+    named = (lines[:, 0:1] == ids) | (lines[:, 1:2] == ids)
     gates[...] = jnp.where(named, probs, 0.0)
 
 
@@ -730,33 +770,52 @@
     )(*args, ahead, weights)
 
 
-def experts_backward_kernel(
-    x, att, small, routes, grad, extra, some, weights, result, moe_part, own_sum, some_attn, grad_w,
-    b, gates, total, moe, gate_grads, gated_all, grad_u_all, out, part, landed, *sems,
-):
-    step = pl.program_id(0)
-    sums = (True, out, part, landed, *sems)
-    with_moe = moe_part is not None
+def layer_backward_kernel(with_moe, *refs):
+    x, att, small, routes, grad, q, kv, mixed, dead, attn_w, *refs = refs
     if not with_moe:
-        *sems, slabs, slab_send, slab_recv, attn_slabs, at_send, at_recv = sems
-        sums, lasts = (True, out, part, landed, *sems), last_copies(some, slabs, slab_send, slab_recv)
+        extra, some_before, *refs = refs
+    weights, grad_x, grad_small, grad_w, some, *refs = refs
+    if with_moe:
+        moe_result, *refs = refs
+    else:
+        own_sum, some_attn, *refs = refs
+    b, gates, unit_two, scale_two, total, gate_grads, gated_all, grad_u_all, *refs = refs
+    whole, slabs, passing, all_probs, grad_h, unit_one, parts, kv_landed, kv_out, back, back_one, *refs = refs
+    fs, fr, ns, nr, kv_send, kv_recv, *refs = refs
+    sums_two, sums_one, refs = (True, back, *refs[:11]), (False, back_one, *refs[11:19]), refs[19:]
+    part_two, part_one = sums_two[2], sums_one[2]
+    if with_moe:
+        moe, moe_part, moe_out, moe_landed, ms, mr, mg, mh, moe_crossed, ps, pr = refs
+        moe_sums = (moe_part, moe_crossed, ps, pr)
+    else:
+        last_slabs, ls, lr, attn_slabs, as_, ar = refs
+        lasts = last_copies(some_before, last_slabs, ls, lr)
         for route in range(2):
             for k in range(1, 4):
                 n, (peer, to) = 3 * route + k - 1, axis_peer(route == 1, k)
                 slab = extra.at[0, :, to] if route == 0 else extra.at[1, to]
-                lasts.append(remote(slab, attn_slabs.at[route, k - 1], at_send.at[n], at_recv.at[n], peer))
+                lasts.append(remote(slab, attn_slabs.at[route, k - 1], as_.at[n], ar.at[n], peer))
+    fars = [toward_far(whole, passing, route, fs, fr) for route in range(2)]
+    nears = [toward_near(whole, passing, slabs, route, ns, nr) for route in range(2)]
+    core, tp = lax.axis_index("core"), lax.axis_index("tp")
+    at_x, at_z = places()
+    other, across, me = chip_peers()
+    far = (me + 2) % 4
+    step = pl.program_id(0)
 
     @pl.when(step == 0)
     def _():
-        arrive(tp_peers() + [{"core": 1 - lax.axis_index("core")}])
-        if not with_moe:
-            arrive(axis_peers(1, 2, 3))
-        experts_setup(x, att, small, routes, b, gates)
+        arrive([other, across] + tp_peers() + axis_peers(1, 2, 3))
+        unit, scale = norm_parts(x[...].astype(f32) + pair_rows(att))
+        unit_two[...] = unit
+        scale_two[...] = scale
+        b[...] = (unit * small[1:2] + small[3:4]).astype(bf16)
+        put_gates(b, small, routes, gates)
         total[...] = jnp.zeros_like(total)
         gate_grads[...] = jnp.zeros_like(gate_grads)
         if with_moe:
             moe[...] = jnp.zeros_like(moe)
-        all_here(4 if with_moe else 10)
+        all_here(11)
         if not with_moe:
             for copy in lasts:
                 copy.start()
@@ -772,45 +831,49 @@
         gated_all[step] = gated
         if with_moe:
             moe[...] += dot(gated, w_out_t, NT)
-        back = dot(grad[...], w_out_t, NN)
+        grad_active = dot(grad[...], w_out_t, NN)
         ids = lax.broadcasted_iota(jnp.int32, (PAIR, 128), 1)
-        gate_grad = jnp.sum(back * active, axis=1, keepdims=True)
+        gate_grad = jnp.sum(grad_active * active, axis=1, keepdims=True)
         gate_grads[...] = jnp.where(ids == step, gate_grad, gate_grads[...])
-        grad_u = (gate * back * gelu_slope(u, t)).astype(bf16)
+        grad_u = (gate * grad_active * gelu_slope(u, t)).astype(bf16)
         grad_u_all[step] = grad_u
         total[...] += dot(grad_u, w_in, NT)
 
     @pl.when(step == EXPERTS - 1)
     def _():
-        part[...] = jnp.zeros_like(part)
-        pick = lax.broadcasted_iota(jnp.int32, (16, 128), 0) == lax.broadcasted_iota(jnp.int32, (16, 128), 1)
-        pick = (pick & (lax.broadcasted_iota(jnp.int32, (16, 128), 0) < EXPERTS)).astype(f32).astype(bf16)
+        part_two[...] = jnp.zeros_like(part_two)
+        lines, lanes = (lax.broadcasted_iota(jnp.int32, (16, 128), axis) for axis in range(2))
+        ones = ((lines == lanes) & (lines < EXPERTS)).astype(f32).astype(bf16)
         for block in range(2):
-            lines = slice(ROWS * block, ROWS * block + ROWS)
-            put_chunks(part, block, total[lines].astype(bf16))
-            part[block, 0, 80:96, 0:ROWS] = dot(pick, gate_grads[lines].astype(bf16), NT).astype(bf16)
+            rows = slice(ROWS * block, ROWS * block + ROWS)
+            put_chunks(part_two, block, total[rows].astype(bf16))
+            part_two[block, 0, 80:96, 0:ROWS] = dot(ones, gate_grads[rows].astype(bf16), NT).astype(bf16)
             if with_moe:
-                put_chunks(moe_part, block, moe[lines].astype(bf16))
-        sum_start(*sums)
+                put_chunks(moe_part, block, moe[rows].astype(bf16))
+        sum_start(*sums_two)
 
     @pl.when(step >= EXPERTS)
     def _():
         at = step - EXPERTS
-        grad_w[:, 0:48] = dot(b[...], grad_u_all[at], TN).astype(bf16).reshape(16, 48, FE)
-        grad_w[:, 48:96] = dot(grad[...], gated_all[at], TN).astype(bf16).reshape(16, 48, FE)
+        first = pl.multiple_of(96 * at, 96)
+        grad_in = dot(b[...], grad_u_all[at], TN).astype(bf16)
+        whole[:, :, pl.ds(first, 48)] = grad_in.reshape(4, 4, 48, FE)
+        grad_out = dot(grad[...], gated_all[at], TN).astype(bf16)
+        whole[:, :, pl.ds(first + 48, 48)] = grad_out.reshape(4, 4, 48, FE)
 
     @pl.when(step == EXPERTS + 1)
     def _():
-        sum_middle(*sums)
-
-    if not with_moe:
-
-        @pl.when(step == 2 * EXPERTS - 2)
-        def _():
+        sum_middle(*sums_two)
+
+    @pl.when(step == 2 * EXPERTS - 2)
+    def _():
+        keys = kv[...].reshape(KEYS, 2 * WIDTH)
+        for h in range(HEADS):
+            all_probs[h] = softmax(HD**-0.5 * dot(head(q[...], h), head(keys, h), NT) + dead[...], -1)
+        if not with_moe:
             for copy in lasts:
                 copy.wait()
-            add_slabs(some, slabs, own_sum)
-            at_x, at_z = places()
+            add_slabs(some_before, last_slabs, own_sum)
             for route in range(2):
 
                 def add(j, carry, route=route):
@@ -824,236 +887,183 @@
 
     @pl.when(step == 2 * EXPERTS - 1)
     def _():
-        sum_end(*sums)
-        result[...] = out[...]
-
-
-def experts_backward(x, att, small, routes, grad, extra, some, weights, cid):
-    args = (x, att, small, routes, grad)
-    shapes = [(2, 4, 96, 384)]
-    scratch = []
-    if extra is None:
-        shapes.append((2, 4, 80, 384))
-
-        def kernel(*refs):
-            experts_backward_kernel(*refs[:5], None, None, *refs[5:8], None, None, *refs[8:])
+        for copy in fars[1] + fars[0]:
+            copy.start()
+        sum_end(*sums_two)
+        router = small[4:8]
+        chances = softmax(dot(router.astype(bf16), b[...], NT), 0)
+        ids = lax.broadcasted_iota(jnp.int32, (EXPERTS, PAIR), 0).astype(f32)
+        lines = routes[...].astype(f32)
+        named = (lines[0:1] == ids) | (lines[1:2] == ids)
+        tables = [back[block, 0, 80:96, 0:ROWS].astype(f32)[0:EXPERTS] for block in range(2)]
+        gate_rows = jnp.where(named, jnp.concatenate(tables, axis=1), 0.0)
+        grad_logits = chances * (gate_rows - jnp.sum(chances * gate_rows, axis=0, keepdims=True))
+        grad_b = pair_rows(back) + dot_split(grad_logits, router.astype(bf16), TN)
+        grad_h[...] = grad[...].astype(f32) + norm_back(grad_b, unit_two[...], scale_two[...], small[1:2])
+        grad_att = grad_h[own_rows(core)].astype(bf16)
+        w_kv, w_q, w_out_t = attn_weights(attn_w)
+        grad_mixed = dot(grad_att, w_out_t, NN).astype(bf16)
+        keys = kv[...].reshape(KEYS, 2 * WIDTH)
+        queries = q[...]
+        q_parts, k_parts, v_parts = [], [], []
+        for h in range(HEADS):
+            q_h, g_h = head(queries, h), head(grad_mixed, h)
+            k_h, v_h = head(keys, h), head(keys, HEADS + h)
+            probs = all_probs[h]
+            v_parts.append(dot(probs.astype(bf16), g_h, TN))
+            grad_weights = dot(g_h, v_h, NT)
+            grad_scores = probs * (grad_weights - jnp.sum(probs * grad_weights, axis=-1, keepdims=True))
+            grad_scores = grad_scores.astype(bf16)
+            q_parts.append(HD**-0.5 * dot(grad_scores, k_h, NN))
+            k_parts.append(HD**-0.5 * dot(grad_scores, q_h, TN))
+        grad_keys = jnp.concatenate(k_parts + v_parts, axis=1).astype(bf16)
+        parts[...] = grad_keys.reshape(4, ROWS, 2 * WIDTH)
+        crosses = [
+            remote(parts.at[(at + 1 - 2 * core) % 4], kv_landed.at[k], kv_send.at[k], kv_recv.at[k], other)
+            for k, at in enumerate((me, far))
+        ]
+        onward = remote(kv_out, kv_landed.at[2], kv_send.at[2], kv_recv.at[2], across)
+        crosses[1].start()
+        crosses[0].start()
+        if with_moe:
+            pres = sum_cores(*moe_sums)
+            for copy in pres:
+                copy.start()
+        crosses[1].wait_recv()
+        kv_out[...] = (parts[far].astype(f32) + kv_landed[1].astype(f32)).astype(bf16)
+        onward.start()
+        if with_moe:
+            for copy in pres:
+                copy.wait_recv()
+            for j in range(4):
+                moe_sum = moe_part[core, j].astype(f32) + moe_crossed[j].astype(f32)
+                moe_crossed[j] = moe_sum.astype(bf16)
+            moe_terms = [
+                remote(moe_crossed.at[peer["tp"]], moe_landed.at[k], ms.at[k], mr.at[k], peer)
+                for k, peer in enumerate(tp_peers())
+            ]
+            for copy in moe_terms:
+                copy.start()
+        for route in (1, 0):
+            for copy in fars[route]:
+                copy.wait_recv()
+            add_passing(whole, passing, route)
+            for copy in nears[route]:
+                copy.start()
+        grad_q = jnp.concatenate(q_parts, axis=1).astype(bf16)
+        grad_w[1, :, WIDTH:] = dot(grad_att, mixed[...], TN).astype(bf16)
+        lanes = lax.broadcasted_iota(jnp.int32, (EXPERTS, PAIR), 1)
+        own_lanes = (lanes < ROWS) == (core == 0)
+        own = (lax.broadcasted_iota(jnp.int32, (PAIR, 1), 0) < ROWS) == (core == 0)
+        kept = jnp.where(own, grad_b, 0.0)
+        grad_small[1:2] = jnp.sum(kept * unit_two[...], axis=0, keepdims=True)
+        grad_small[3:4] = jnp.sum(kept, axis=0, keepdims=True)
+        grad_small[4:8] = dot_split(jnp.where(own_lanes, grad_logits, 0.0), b[...], NN)
+        unit, scale_one = norm_parts(x[...].astype(f32))
+        unit_one[...] = unit
+        normed = (unit_one[own_rows(core)] * small[0:1] + small[2:3]).astype(bf16)
+        crosses[0].wait_recv()
+        onward.wait_recv()
+        grad_kv = parts[me].astype(f32) + kv_landed[0].astype(f32) + kv_landed[2].astype(f32)
+        grad_kv = grad_kv.astype(bf16)
+        value = dot(grad_kv, w_kv, NT) + dot(grad_q, w_q, NT)
+        put_chunks(part_one, 0, value.astype(bf16))
+        sum_start(*sums_one)
+        grad_w[0] = dot(normed, grad_kv, TN).astype(bf16)
+        grad_w[1, :, :WIDTH] = dot(normed, grad_q, TN).astype(bf16)
+        sum_middle(*sums_one)
+        if with_moe:
+            moe_total = moe_crossed[tp].astype(f32)
+            for k, copy in enumerate(moe_terms):
+                copy.wait_recv()
+                moe_total = moe_total + moe_landed[k].astype(f32)
+            moe_out[tp] = moe_total.astype(bf16)
+            moe_results = [
+                remote(moe_out.at[tp], moe_out.at[tp], mg.at[k], mh.at[k], peer)
+                for k, peer in enumerate(tp_peers())
+            ]
+            for copy in moe_results:
+                copy.start()
+        for route in range(2):
+            for copy in fars[route]:
+                copy.wait_send()
+            for copy in nears[route]:
+                copy.wait()
+        steps = some.shape[1] // 48
+
+        def add(i, carry):
+            j, at = i % 4, i // 4
+            rows, route = pl.ds(pl.multiple_of(at * 48, 48), 48), at // (steps // 2)
+            mine = whole[j * (1 - route) + at_x * route, at_z * (1 - route) + j * route, rows]
+            total = mine.astype(f32) + slabs[0, j, rows].astype(f32) + slabs[1, j, rows].astype(f32)
+            some[j, rows] = total.astype(bf16)
+            return carry
+
+        lax.fori_loop(0, 4 * steps, add, 0)
+        sum_end(*sums_one)
+        grad_a = pair_rows(back_one)
+        grad_x[...] = (grad_h[...] + norm_back(grad_a, unit_one[...], scale_one, small[0:1])).astype(bf16)
+        kept = jnp.where(own, grad_a, 0.0)
+        grad_small[0:1] = jnp.sum(kept * unit_one[...], axis=0, keepdims=True)
+        grad_small[2:3] = jnp.sum(kept, axis=0, keepdims=True)
+        for copy in crosses + [onward]:
+            copy.wait_send()
+        if with_moe:
+            for copy in pres + moe_terms:
+                copy.wait_send()
+            for copy in moe_results:
+                copy.wait()
+            moe_result[...] = moe_out[...]
+
+
+def layer_backward(args, others, weights, cid):
+    with_moe = not others
+    slab = (384, FE)
+    shapes = [((PAIR, D), bf16), ((8, D), f32), ((2, D, 2 * WIDTH), bf16), ((4,) + slab, bf16)]
+    scratch = [
+        ((PAIR, D), bf16),
+        ((PAIR, EXPERTS), f32),
+        ((PAIR, D), f32),
+        ((PAIR, 1), f32),
+        ((PAIR, D), f32),
+        ((PAIR, 128), f32),
+        ((EXPERTS, PAIR, FE), bf16),
+        ((EXPERTS, PAIR, FE), bf16),
+        ((4, 4) + slab, bf16),
+        ((2, 4) + slab, bf16),
+        ((2, 2, 4, 96, FE), bf16),
+        ((HEADS, ROWS, KEYS), f32),
+        ((PAIR, D), f32),
+        ((PAIR, D), f32),
+        ((4, ROWS, 2 * WIDTH), bf16),
+        ((3, ROWS, 2 * WIDTH), bf16),
+        ((ROWS, 2 * WIDTH), bf16),
+        ((2, 4, 96, 384), bf16),
+        ((2, 4, 80, 384), bf16),
+    ]
+    scratch = [pltpu.VMEM(*s) for s in scratch] + dma_sems(4, 8, 3)
+    scratch += sum_scratch(True, 96) + sum_scratch(False, 80)
+    if with_moe:
+        shapes.append(((4, 80, 384), bf16))
+        scratch += [pltpu.VMEM((PAIR, D), f32), pltpu.VMEM((2, 4, 80, 384), bf16)]
+        scratch += [pltpu.VMEM((4, 80, 384), bf16), pltpu.VMEM((3, 80, 384), bf16)] + dma_sems(3, 3)
+        scratch += [pltpu.VMEM((4, 80, 384), bf16)] + dma_sems(2)
     else:
-        args += (extra, some)
-        slab = some.shape[1:]
-        shapes += [slab, (2, 4, 48, FE)]
-        scratch = [pltpu.VMEM((3,) + slab, bf16)] + dma_sems(6)
+        shapes += [(slab, bf16), ((2, 4, 48, FE), bf16)]
+        scratch += [pltpu.VMEM((3,) + slab, bf16)] + dma_sems(6)
         scratch += [pltpu.VMEM((2, 3, 4, 48, FE), bf16)] + dma_sems(6)
-
-        def kernel(*refs):
-            experts_backward_kernel(*refs[:9], None, *refs[9:])
-
-    blocks = [fixed(shape) for shape in shapes]
+    args = args + others
     return pl.pallas_call(
-        kernel,
+        functools.partial(layer_backward_kernel, with_moe),
         grid=(2 * EXPERTS,),
-        out_shape=[jax.ShapeDtypeStruct(s, bf16) for s in shapes + [(16, 96 * EXPERTS, FE)]],
+        out_shape=[jax.ShapeDtypeStruct(*s) for s in shapes],
         in_specs=[fixed(a.shape) for a in args]
         + [pl.BlockSpec((16, 96, FE), lambda s: (0, jnp.minimum(s, EXPERTS - 1), 0))],
-        out_specs=blocks + [pl.BlockSpec((16, 96, FE), lambda s: (0, jnp.maximum(s - EXPERTS, 0), 0))],
-        scratch_shapes=[
-            pltpu.VMEM((PAIR, D), bf16),
-            pltpu.VMEM((PAIR, EXPERTS), f32),
-            pltpu.VMEM((PAIR, D), f32),
-            pltpu.VMEM((PAIR, D), f32),
-            pltpu.VMEM((PAIR, 128), f32),
-            pltpu.VMEM((EXPERTS, PAIR, FE), bf16),
-            pltpu.VMEM((EXPERTS, PAIR, FE), bf16),
-            pltpu.VMEM((2, 4, 96, 384), bf16),
-        ]
-        + sum_scratch(True, 96)
-        + scratch,
-        compiler_params=params(cid, 56),
-        name="experts_backward",
+        out_specs=[fixed(s) for s, _ in shapes],
+        scratch_shapes=scratch,
+        compiler_params=params(cid, 60),
+        name="layer_backward",
     )(*args, weights)
-
-
-def attend_backward_kernel(with_moe, *refs):
-    x, att, small, routes_t, grad, back, q, kv, mixed, dead, weights, whole, *refs = refs
-    if with_moe:
-        moe_part, *refs = refs
-    grad_x, grad_small, grad_w, some, *refs = refs
-    if with_moe:
-        moe, *refs = refs
-    grad_h, both_units, parts, kv_landed, back_one, part, landed, *sems = refs
-    if with_moe:
-        *sems, moe_landed, ms, mr, ns, nr, moe_crossed, ps, pr = sems
-        moe_sums = (moe_part, moe_crossed, ps, pr)
-    *sems, slabs, passing, fs, fr, ns2, nr2, kv_out, kv_send, kv_recv = sems
-    fars = [toward_far(whole, passing, route, fs, fr) for route in range(2)]
-    nears = [toward_near(whole, passing, slabs, route, ns2, nr2) for route in range(2)]
-    sums = (False, back_one, part, landed, *sems)
-    core, tp = lax.axis_index("core"), lax.axis_index("tp")
-    other, across, me = chip_peers()
-    far = (me + 2) % 4
-    arrive([other, across] + tp_peers() + axis_peers(1, 3))
-    all_here(9)
-    for copy in fars[1] + fars[0]:
-        copy.start()
-    unit, scale = norm_parts(x[...].astype(f32) + pair_rows(att))
-    b = (unit * small[1:2] + small[3:4]).astype(bf16)
-    router = small[4:8]
-    chances = softmax(dot(router.astype(bf16), b, NT), 0)
-    ids = lax.broadcasted_iota(jnp.int32, (EXPERTS, PAIR), 0).astype(f32)
-    named = (routes_t[0:1] == ids) | (routes_t[1:2] == ids)
-    tables = [back[block, 0, 80:96, 0:ROWS].astype(f32)[0:EXPERTS] for block in range(2)]
-    gate_grads = jnp.where(named, jnp.concatenate(tables, axis=1), 0.0)
-    grad_logits = chances * (gate_grads - jnp.sum(chances * gate_grads, axis=0, keepdims=True))
-    grad_b = pair_rows(back) + dot_split(grad_logits, router.astype(bf16), TN)
-    grad_h[...] = grad[...].astype(f32) + norm_back(grad_b, unit, scale, small[1:2])
-    grad_att = grad_h[own_rows(core)].astype(bf16)
-    w_kv, w_q, w_out_t = attn_weights(weights)
-    grad_mixed = dot(grad_att, w_out_t, NN).astype(bf16)
-    keys = kv[...].reshape(KEYS, 2 * WIDTH)
-    queries = q[...]
-    q_parts, k_parts, v_parts = [], [], []
-    for h in range(HEADS):
-        q_h, g_h = head(queries, h), head(grad_mixed, h)
-        k_h, v_h = head(keys, h), head(keys, HEADS + h)
-        probs = softmax(HD**-0.5 * dot(q_h, k_h, NT) + dead[...], -1)
-        v_parts.append(dot(probs.astype(bf16), g_h, TN))
-        grad_weights = dot(g_h, v_h, NT)
-        grad_scores = probs * (
-            grad_weights - jnp.sum(probs * grad_weights, axis=-1, keepdims=True)
-        )
-        grad_scores = grad_scores.astype(bf16)
-        q_parts.append(HD**-0.5 * dot(grad_scores, k_h, NN))
-        k_parts.append(HD**-0.5 * dot(grad_scores, q_h, TN))
-    total = jnp.concatenate(k_parts + v_parts, axis=1).astype(bf16)
-    parts[...] = total.reshape(4, ROWS, 2 * WIDTH)
-    crosses = [
-        remote(parts.at[(at + 1 - 2 * core) % 4], kv_landed.at[k], kv_send.at[k], kv_recv.at[k], other)
-        for k, at in enumerate((me, far))
-    ]
-    onward = remote(kv_out, kv_landed.at[2], kv_send.at[2], kv_recv.at[2], across)
-    crosses[1].start()
-    crosses[0].start()
-    if with_moe:
-        pres = sum_cores(*moe_sums)
-        for copy in pres:
-            copy.start()
-    crosses[1].wait_recv()
-    kv_out[...] = (parts[far].astype(f32) + kv_landed[1].astype(f32)).astype(bf16)
-    onward.start()
-    if with_moe:
-        for copy in pres:
-            copy.wait_recv()
-        for j in range(4):
-            moe_sum = moe_part[core, j].astype(f32) + moe_crossed[j].astype(f32)
-            moe_crossed[j] = moe_sum.astype(bf16)
-        moe_terms = [
-            remote(moe_crossed.at[peer["tp"]], moe_landed.at[k], ms.at[k], mr.at[k], peer)
-            for k, peer in enumerate(tp_peers())
-        ]
-        for copy in moe_terms:
-            copy.start()
-    for route in (1, 0):
-        for copy in fars[route]:
-            copy.wait_recv()
-        add_passing(whole, passing, route)
-        for copy in nears[route]:
-            copy.start()
-    grad_q = jnp.concatenate(q_parts, axis=1).astype(bf16)
-    grad_w[1, :, WIDTH:] = dot(grad_att, mixed[...], TN).astype(bf16)
-    lanes = lax.broadcasted_iota(jnp.int32, (EXPERTS, PAIR), 1)
-    own_lanes = (lanes < ROWS) == (core == 0)
-    own = (lax.broadcasted_iota(jnp.int32, (PAIR, 1), 0) < ROWS) == (core == 0)
-    kept = jnp.where(own, grad_b, 0.0)
-    grad_small[1:2] = jnp.sum(kept * unit, axis=0, keepdims=True)
-    grad_small[3:4] = jnp.sum(kept, axis=0, keepdims=True)
-    grad_small[4:8] = dot_split(jnp.where(own_lanes, grad_logits, 0.0), b, NN)
-    unit_one, scale_one = norm_parts(x[...].astype(f32))
-    both_units[...] = unit_one
-    normed = (both_units[own_rows(core)] * small[0:1] + small[2:3]).astype(bf16)
-    crosses[0].wait_recv()
-    onward.wait_recv()
-    grad_kv = parts[me].astype(f32) + kv_landed[0].astype(f32) + kv_landed[2].astype(f32)
-    grad_kv = grad_kv.astype(bf16)
-    value = dot(grad_kv, w_kv, NT) + dot(grad_q, w_q, NT)
-    put_chunks(part, 0, value.astype(bf16))
-    sum_start(*sums)
-    grad_w[0] = dot(normed, grad_kv, TN).astype(bf16)
-    grad_w[1, :, :WIDTH] = dot(normed, grad_q, TN).astype(bf16)
-    sum_middle(*sums)
-    if with_moe:
-        total = moe_crossed[tp].astype(f32)
-        for k, copy in enumerate(moe_terms):
-            copy.wait_recv()
-            total = total + moe_landed[k].astype(f32)
-        moe[tp] = total.astype(bf16)
-        moe_results = [
-            remote(moe.at[tp], moe.at[tp], ns.at[k], nr.at[k], {"tp": (tp + k + 1) % 4}) for k in range(3)
-        ]
-        for copy in moe_results:
-            copy.start()
-    sum_end(*sums)
-    grad_a = pair_rows(back_one)
-    grad_x[...] = (grad_h[...] + norm_back(grad_a, unit_one, scale_one, small[0:1])).astype(bf16)
-    kept = jnp.where(own, grad_a, 0.0)
-    grad_small[0:1] = jnp.sum(kept * unit_one, axis=0, keepdims=True)
-    grad_small[2:3] = jnp.sum(kept, axis=0, keepdims=True)
-    for copy in crosses + [onward]:
-        copy.wait_send()
-    if with_moe:
-        for copy in pres:
-            copy.wait_send()
-        for copy in moe_terms:
-            copy.wait_send()
-        for copy in moe_results:
-            copy.wait()
-    for route in range(2):
-        for copy in fars[route]:
-            copy.wait_send()
-        for copy in nears[route]:
-            copy.wait()
-    at_x, at_z = places()
-    steps = some.shape[1] // 48
-
-    def add(i, carry):
-        j, at = i % 4, i // 4
-        rows, route = pl.ds(pl.multiple_of(at * 48, 48), 48), at // (steps // 2)
-        own = whole[j * (1 - route) + at_x * route, at_z * (1 - route) + j * route, rows]
-        total = own.astype(f32) + slabs[0, j, rows].astype(f32) + slabs[1, j, rows].astype(f32)
-        some[j, rows] = total.astype(bf16)
-        return carry
-
-    lax.fori_loop(0, 4 * steps, add, 0)
-
-
-def attend_backward(args, moe_part, cid):
-    with_moe = moe_part is not None
-    shapes = [((PAIR, D), bf16), ((8, D), f32), ((2, D, 2 * WIDTH), bf16)]
-    scratch = [
-        pltpu.VMEM((PAIR, D), f32),
-        pltpu.VMEM((PAIR, D), f32),
-        pltpu.VMEM((4, ROWS, 2 * WIDTH), bf16),
-        pltpu.VMEM((3, ROWS, 2 * WIDTH), bf16),
-        pltpu.VMEM((2, 4, 80, 384), bf16),
-    ]
-    slab = args[-1].shape[2:]
-    shapes.append(((4,) + slab, bf16))
-    scratch += sum_scratch(False, 80)
-    scratch += [pltpu.VMEM((2, 4) + slab, bf16), pltpu.VMEM((2, 2, 4, 128, FE), bf16)]
-    scratch += dma_sems(4, 8) + [pltpu.VMEM((ROWS, 2 * WIDTH), bf16)] + dma_sems(3)
-    in_specs = [VMEM] * len(args)
-    if with_moe:
-        args, in_specs = args + (moe_part,), in_specs + [VMEM]
-        shapes.append(((4, 80, 384), bf16))
-        scratch += [pltpu.VMEM((3, 80, 384), bf16)] + dma_sems(3, 3)
-        scratch += [pltpu.VMEM((4, 80, 384), bf16)] + dma_sems(2)
-    return pl.pallas_call(
-        functools.partial(attend_backward_kernel, with_moe),
-        out_shape=[jax.ShapeDtypeStruct(*s) for s in shapes],
-        in_specs=in_specs,
-        out_specs=[VMEM] * len(shapes),
-        scratch_shapes=scratch,
-        compiler_params=params(cid, 56),
-        name="attend_backward",
-    )(*args)
 
 
 def shards(boundary, routes, lengths, ln_gains, ln_biases, w_qkv, w_out, w_router, w_in, w_exp_out):
@@ -1102,36 +1112,26 @@
     x0 = got_images[:, 0, 0:ROWS].reshape(PAIR, D)
     cotangent = jnp.where(chip_live[:, :, None], got_images[:, 1, 0:ROWS], 0).reshape(PAIR, D)
     route_rows = [
-        got_images[:, kind, ROWS : ROWS + 2, 0:ROWS].transpose(1, 0, 2).reshape(2, PAIR).astype(f32)
-        for kind in range(2)
+        got_images[:, kind, ROWS:, 0:ROWS].transpose(1, 0, 2).reshape(16, PAIR) for kind in range(2)
     ]
-    route_cols = [rows.T for rows in route_rows]
 
     q0, kv0, mixed0, att0, experts_zero, ahead = attend_forward(x0, (), smalls[0], packs, dead, some, ahead, 3)
     experts_zero = experts_zero.reshape(16, 384, FE)
     shard, att0 = lax.optimization_barrier((chip[8:16].reshape(384, FE), att0))
     experts_one = lax.all_gather(shard, CHIPS, axis=0)
-    moe0, attn_w1 = experts_forward(x0, att0, smalls[0], route_cols[0], ahead, experts_zero, 4)
+    moe0, attn_w1 = experts_forward(x0, att0, smalls[0], route_rows[0], ahead, experts_zero, 4)
     attn_w1 = attn_w1.reshape(16, 96, FE)
     q1, kv1, mixed1, att1, x1 = attend_forward(
         x0, (att0, moe0), smalls[1], attn_w1, dead, None, None, 5
     )
-    back, moe_part, grad_experts1 = experts_backward(
-        x1, att1, smalls[1], route_cols[1], cotangent, None, None, experts_one, 6
+    grad_x1, grad_small1, grad_attn1, some, moe1 = layer_backward(
+        (x1, att1, smalls[1], route_rows[1], cotangent, q1, kv1, mixed1, dead, attn_w1), (), experts_one, 6
     )
-    grad_x1, grad_small1, grad_attn1, some, moe1 = attend_backward(
-        (x1, att1, smalls[1], route_rows[1], cotangent, back, q1, kv1, mixed1, dead, attn_w1, grad_experts1.reshape(4, 4, 384, FE)),
-        moe_part,
+    grad_x0, grad_small0, grad_attn0, some, sums1, some_attn = layer_backward(
+        (x0, att0, smalls[0], route_rows[0], grad_x1, q0, kv0, mixed0, dead, packs),
+        (grad_attn1.reshape(2, 4, 4, 48, FE), some),
+        experts_zero,
         7,
-    )
-    grad_attn1 = grad_attn1.reshape(2, 4, 4, 48, FE)
-    back, sums1, some_attn, grad_experts0 = experts_backward(
-        x0, att0, smalls[0], route_cols[0], grad_x1, grad_attn1, some, experts_zero, 8
-    )
-    grad_x0, grad_small0, grad_attn0, some = attend_backward(
-        (x0, att0, smalls[0], route_rows[0], grad_x1, back, q0, kv0, mixed0, dead, packs, grad_experts0.reshape(4, 4, 384, FE)),
-        None,
-        9,
     )
 
     def own_block(value):
@@ -1149,27 +1149,12 @@
     tiny = tiny.transpose(0, 2, 3, 1, 4).reshape(2, 16, 16, 24)
     tiny = jnp.pad(tiny, ((0, 0), (0, 0), (0, 0), (0, 384 - 24)))
     packs = jnp.concatenate([grad_attn0.reshape(2, 16, 48, 384), tiny], axis=2).reshape(2, 4, 4, 64, FE)
-    own, landed, got1, own0, got0 = end_exchange(packs, sent, sums1, some, some_attn)
+    tiny, landed, grad_w_in, grad_w_exp_out, attn = end_exchange(packs, sent, sums1, some, some_attn)
     landed = landed.astype(f32)
     ends = jnp.where(high == 0, jnp.stack([kept, landed]), jnp.stack([landed, kept]))
-
-    def own_lines(sums):
-        return lax.dynamic_slice_in_dim(sums.reshape(-1, 48, FE), 24 * core, 24, 1).astype(f32)
-
-    own0, got0, own1, got1 = (own_lines(sums) for sums in (own0, got0, sums1, got1))
-    attn1 = own0[8:10] + got0[8:10]
-
-    def both_halves(own_sum, got_sum):
-        first = jnp.where(core == 0, own_sum, got_sum)
-        second = jnp.where(core == 0, got_sum, own_sum)
-        return jnp.concatenate([first, second], axis=2).reshape(EXPERTS, 2, 24, D)
-
-    full = jnp.stack([both_halves(own0[0:8], got0[0:8]), both_halves(own1, got1)])
-    attn0 = lax.dynamic_slice_in_dim(own, 24 * core, 24, 1)
-    attn = jnp.stack([attn0, attn1])
     grad_w_qkv = jnp.concatenate([attn[:, 1, :, None, :WIDTH], attn[:, 0].reshape(2, 24, 2, WIDTH)], axis=2)
     grad_w_out = attn[:, 1, :, WIDTH:].transpose(0, 2, 1)
-    tiny = lax.dynamic_slice_in_dim(own[:, 48:64, 0:24], 8 * core, 8, 1)
+    tiny = tiny[:, :, 0:24]
     return (
         ends[None],
         tiny[:, 0:2],
@@ -1177,8 +1162,8 @@
         grad_w_qkv,
         grad_w_out,
         tiny[:, 4:8].transpose(0, 2, 1),
-        full[:, :, 0],
-        full[:, :, 1].transpose(0, 1, 3, 2),
+        grad_w_in,
+        grad_w_exp_out.transpose(0, 1, 3, 2),
     )
 
 

time: 307 us -> 295 us (0.961)
  Pallas kernels: 254 us -> 242 us
  other arithmetic: 15.5 us -> 11.5 us
  local copies, waits for them, and re-layouts: 18.9 us -> 22.5 us
    pallas_call x5 -> x3, Pallas kernels: 144 us -> 133 us  [the longest x2 105 us: layer_backward(): pl.pallas_call(functools.partial(layer_backward_kernel, with_moe), grid=(...]
  transfers between devices with their start and end apart: 1 -> 1, of which waited for: 1 -> 1; matrix products, arithmetic and copies ran while one was open for 2% -> 2% of each run, Pallas kernels for 15% -> 16%
where the time goes in v5:
time: 295 us; the launch traced here: 294 us
  Pallas kernels  242 us (82%)
  local copies, waits for them, and re-layouts  22.5 us (8%)
  between operations  14.5 us (5%)
  other arithmetic  11.5 us (4%)
  waiting for transfers between devices  3.7 us (1%)
    pallas_call x2, Pallas kernels, layer_backward(): pl.pallas_call(functools.partial(layer_backward_kernel, with_moe), grid=(...  105 us
    pallas_call x2, Pallas kernels, attend_forward(): pl.pallas_call(functools.partial(attend_forward_kernel, bool(before)), ou...  51 us
    pallas_call x1, Pallas kernels, start_exchange(): pl.pallas_call(start_kernel, out_shape=[jax.ShapeDtypeStruct(s, bf16) for...  31.2 us
    pallas_call x1, Pallas kernels, end_exchange(): pl.pallas_call(end_kernel, out_shape=[jax.ShapeDtypeStruct((2, 8, FE), f3...  28.3 us
    pallas_call x1, Pallas kernels, experts_forward(): pl.pallas_call(experts_forward_kernel, grid=(EXPERTS,), out_shape=[jax.Sh...  23.6 us
  transfers between devices with their start and end apart: 1, of which 1 were waited for; matrix products, arithmetic and copies ran while one was open for 2% of the time, Pallas kernels for 16%

profile of v5, /device:TPU:1, one launch (start us, length us, event | category | flops | bytes accessed | tf_op | source)
XLA Modules:
  0.0 293.7 jit_solution(3244704875580960489)
XLA Ops:
  9.7 1.1 pad_maximum_fusion.1
  11.7 1.2 constant_dynamic-slice_fusion.3
  13.0 2.9 cross.1
  16.9 0.9 fusion.5
  18.5 0.8 fusion.2.images
  20.0 31.2 %start_exchange.1 = (bf16[2,2,176,768]{3,2,1,0:T(8,128)(2,1)}, bf16[4,4,128,384]{3,2,1,0:T(8,128)(2,1)}, bf16[4,4,384,384]{3,2,1,0:T(8,128)(2,1)}) custom-call(bf16[2,176,768]{2,1,0:T(8,128)(2,1)} %fusion.2.images, bf16[128,384]{1,0:T(8,128)(2,1)} %pad_maximum_fusion.7.urgent, bf16[384,384]{1,0:T(8,128)(2,1)} %bitcast.116), custom_call_target="tpu_custom_call" | custom-call | tf_op jit(solution)/shard_map/start_exchange/pallas_call | solution.py:285
  51.2 2.0 fusion.9
  53.2 1.0 slice.120
  55.3 28.8 %attend_forward.2 = (bf16[160,192]{1,0:T(8,128)(2,1)}, bf16[4,160,384]{2,1,0:T(8,128)(2,1)}, bf16[160,192]{1,0:T(8,128)(2,1)}, bf16[2,4,80,384]{3,2,1,0:T(8,128)...) custom-call(bf16[320,768]{1,0:T(8,128)(2,1)} %bitcast.98, ...), custom_call_target="tpu_custom_call", output_to_operand_aliasing={{4}: (5, {})} | custom-call | tf_op jit(solution)/shard_map/attend_forward/pallas_call | solution.py:671
  87.3 23.6 %experts_forward.1 = (bf16[2,4,80,384]{3,2,1,0:T(8,128)(2,1)}, bf16[4,4,96,384]{3,2,1,0:T(8,128)(2,1)}) custom-call(bf16[320,768]{1,0:T(8,128)(2,1)} %bitcast.99, bf16[2,4,80,384]{3,2,1,0:T(8,128)(2,1)} %get-tuple-element.46.att.refs_1_, f32[8,768]{1,0:T(8,128)} %reshape.243.refs_1_.small.refs_2_, ...), custom_call_target="tpu_custom_call", output_to_operand_aliasing={{1}: (4, {})} | custom-call | tf_op jit(solution)/shard_map/experts_forward/pallas_call | solution.py:753
  110.8 22.2 %attend_forward.3 = (bf16[160,192]{1,0:T(8,128)(2,1)}, bf16[4,160,384]{2,1,0:T(8,128)(2,1)}, bf16[160,192]{1,0:T(8,128)(2,1)}, bf16[2,4,80,384]{3,2,1,0:T(8,128)(2,1)}, bf16[320,768]{1,0:T(8,128)(2,1)}) custom-call(bf16[320,768]{1,0:T(8,128)(2,1)} %bitcast.100, bf16[2,4,80,384]{3,2,1,0:T(8,128)(2,1)} %get-tuple-element.46.att.refs_1_, ...), custom_call_target="tpu_custom_call" | custom-call | tf_op jit(solution)/shard_map/attend_forward/pallas_call | solution.py:671
  133.0 1.0 constant_dynamic-slice_fusion
  134.7 0.9 bitcast_select_fusion.refs_4_
  135.5 3.7 %all-gather.3.cloned.1.call-done = bf16[6144,384]{1,0:T(8,128)(2,1)} async-done(((bf16[384,384]{1,0:T(8,128)(2,1)}), bf16[6144,384]{1,0:T(8,128)(2,1)}) %all-gather.3.cloned.1.call-update) | async-done | bytes 4718608 | tf_op jit(solution)/shard_map/all_gather | solution.py:1121
  139.2 52.9 %layer_backward.2 = (bf16[320,768]{1,0:T(8,128)(2,1)}, f32[8,768]{1,0:T(8,128)}, bf16[2,768,384]{2,1,0:T(8,128)(2,1)}, bf16[4,384,384]{2,1,0:T(8,128)(2,1)}, bf16[4,80,384]{2,1,0:T(8,128)(2,1)}) custom-call(bf16[320,768]{1,0:T(8,128)(2,1)} %get-tuple-element.51.refs_0_, bf16[2,4,80,384]{3,2,1,0:T(8,128)(2,1)} %get-tuple-element.52.refs_1_, ...), custom_call_target="tpu_custom_call" | custom-call | tf_op jit(solution)/shard_map/layer_backward/pallas_call | solution.py:1056
  192.1 51.8 %layer_backward.3 = (bf16[320,768]{1,0:T(8,128)(2,1)}, f32[8,768]{1,0:T(8,128)}, bf16[2,768,384]{2,1,0:T(8,128)(2,1)}, bf16[4,384,384]{2,1,0:T(8,128)(2,1)}, bf1...) custom-call(bf16[320,768]{1,0:T(8,128)(2,1)} %bitcast.101, bf16[2,4,80,384]{3,2,1,0:T(8,128)(2,1)} %get-tuple-element.46.att.refs_1_, ...), custom_call_target="tpu_custom_call" | custom-call | tf_op jit(solution)/shard_map/layer_backward/pallas_call | solution.py:1056
  243.9 1.0 dynamic-slice_convert_fusion.1
  247.5 1.4 pad_maximum_fusion.part
  249.9 28.3 %end_exchange.1 = (f32[2,8,384]{2,1,0:T(8,128)}, bf16[160,768]{1,0:T(8,128)(2,1)}, f32[2,4,24,768]{3,2,1,0:T(8,128)}, f32[2,4,24,768]{3,2,1,0:T(8,128)}, f32[2,2,24,384]{3,2,1,0:T(8,128)}) custom-call(bf16[2,4,4,64,384]{4,3,2,1,0:T(8,128)(2,1)} %pad_maximum_fusion.part, bf16[160,768]{1,0:T(8,128)(2,1)} %fusion.7.image, ...), custom_call_target="tpu_custom_call" | custom-call | tf_op jit(solution)/shard_map/end_exchange/pallas_call | solution.py:503
  278.2 1.3 slice_bitcast_fusion.5
  279.5 1.4 fusion.10
  280.9 0.9 slice.107
  281.8 1.6 slice_bitcast_fusion
  284.2 1.0 maximum_select_fusion.1
  (84 shorter events, 16.4 us)
Async XLA Ops:
  7.2 132.1 %all-gather.3.cloned.1.call-start = ((), (), s32[]{:S(2)}) async-start(), calls=%async_computation | async-start | bytes 5013504 | tf_op jit(solution)/shard_map/all_gather | solution.py:1121
  10.8 0.7 copy-start.8
  16.2 1.6 copy-start.9
  16.2 1.6 copy-start.10
  16.2 2.3 copy-start.4
  192.1 53.6 %copy-start.7 = (f32[8,768]{1,0:T(8,128)S(1)}, f32[8,768]{1,0:T(8,128)}, u32[]{:S(2)}) copy-start(f32[8,768]{1,0:T(8,128)} %get-tuple-element.67) | copy-start | bytes 73732
  243.9 2.3 copy-start.5
  246.2 1.3 copy-start
  247.5 1.4 copy-start.1
  278.2 5.3 %copy-start.6 = (bf16[160,768]{1,0:T(8,128)(2,1)S(1)}, bf16[160,768]{1,0:T(8,128)(2,1)}, u32[]{:S(2)}) copy-start(bf16[160,768]{1,0:T(8,128)(2,1)} %get-tuple-element.71) | copy-start | bytes 737284
  283.6 1.7 copy-start.3
  284.2 1.8 copy-start.2
Sparse Core Ops, SparseCore 0:
  84.2 54.9 all-gather.2

commit v6 on v5

--- a/solution.py
+++ b/solution.py
@@ -576,9 +576,10 @@
 
 
 def attn_weights(weights):
-    w_kv = weights[:, 0:48].reshape(D, 2 * WIDTH)
-    w_q = weights[:, 48:96, :WIDTH].reshape(D, WIDTH)
-    return w_kv, w_q, weights[:, 48:96, WIDTH:].reshape(D, WIDTH)
+    chips = (slice(None),) * (len(weights.shape) - 2)
+    w_kv = weights[(*chips, slice(0, 48))].reshape(D, 2 * WIDTH)
+    w_q = weights[(*chips, slice(48, 96), slice(0, WIDTH))].reshape(D, WIDTH)
+    return w_kv, w_q, weights[(*chips, slice(48, 96), slice(WIDTH, None))].reshape(D, WIDTH)
 
 
 def attend_forward_kernel(follows, *refs):
@@ -705,25 +706,55 @@
     return jnp.sum(jnp.where(ids == expert, gates[...], 0.0), axis=1, keepdims=True)
 
 
-def experts_forward_kernel(
-    x, att, small, routes, _, weights, result, ahead, b, gates, total, ah_send, ah_recv, out, part, landed, *sems
+def fixed(shape):
+    return pl.BlockSpec(shape, lambda e: (0,) * len(shape))
+
+
+def middle_kernel(
+    x, att, small, routes, small_next, dead, ahead, later, weights,
+    q, kv_result, mixed, att_result, x_next, attn_result, whole,
+    b, gates, total, moe, attn_w, kv, att_next,
+    ah_send, ah_recv, l_send, l_recv, sp_send, sp_recv, kv_send, kv_recv, own_sem, *sems,
 ):
     expert = pl.program_id(0)
-    sums = (True, out, part, landed, *sems)
-    aheads = []
+    sums, sums_next = (True, moe, *sems[:11]), (False, att_next, *sems[11:])
+    part, part_next = sums[2], sums_next[2]
+    core = lax.axis_index("core")
+    at_x, at_z = places()
+    other, across, me = chip_peers()
+    far = (me + 2) % 4
+    aheads, laters = [], []
     for route in range(2):
-        slabs = line(ahead, route, places()[1 - route], half(ahead.shape[2], route))
+        second, rows, late = (at_z, at_x)[route], half(ahead.shape[2], route), half(later.shape[0], route)
         for k in range(1, 4):
-            n, peer = 3 * route + k - 1, axis_peer(route == 1, k)[0]
-            aheads.append(remote(slabs, slabs, ah_send.at[n], ah_recv.at[n], peer))
+            n = 3 * route + k - 1
+            aheads.append(
+                remote(
+                    line(ahead, route, second, rows), line(attn_w, route, second, rows),
+                    ah_send.at[n], ah_recv.at[n], axis_peer(route == 1, k)[0],
+                )
+            )
+            laters.append(
+                remote(
+                    later.at[late], whole.at[at_x, at_z, late],
+                    l_send.at[n], l_recv.at[n], axis_peer(route == 0, k)[0],
+                )
+            )
+    own = pltpu.make_async_copy(later, whole.at[at_x, at_z], own_sem)
+    nears, fars = spread_near(whole, sp_send, sp_recv), spread_far(whole, sp_send, sp_recv)
 
     @pl.when(expert == 0)
     def _():
-        arrive(tp_peers() + [{"core": 1 - lax.axis_index("core")}] + axis_peers(1, 2, 3))
+        arrive([other, across] + tp_peers() + axis_peers(1, 2, 3))
         experts_setup(x, att, small, routes, b, gates)
         total[...] = jnp.zeros_like(total)
-        all_here(10)
-        for copy in aheads:
+        for j in range(4):
+            rows = half(ahead.shape[2], 0)
+            attn_w[j, at_z, rows] = ahead[j, at_z, rows]
+            rows = half(ahead.shape[2], 1)
+            attn_w[at_x, j, rows] = ahead[at_x, j, rows]
+        all_here(11)
+        for copy in aheads + laters + [own]:
             copy.start()
 
     w_in, w_out_t = expert_weights(weights)
@@ -737,37 +768,82 @@
         for block in range(2):
             put_chunks(part, block, total[ROWS * block : ROWS * block + ROWS].astype(bf16))
         sum_start(*sums)
+        for copy in laters:
+            copy.wait_recv()
+        own.wait()
+        for copy in nears:
+            copy.start()
         sum_middle(*sums)
         sum_end(*sums)
-        result[...] = out[...]
+        x_next[...] = (x[...].astype(f32) + pair_rows(att) + pair_rows(moe)).astype(bf16)
+        unit, _ = norm_parts(x_next[own_rows(core)].astype(f32))
+        normed = (unit * small_next[0:1] + small_next[2:3]).astype(bf16)
         for copy in aheads:
+            copy.wait_recv()
+        w_kv, w_q, w_out = attn_weights(attn_w)
+        kv[me] = dot(normed, w_kv, NN).astype(bf16)
+        copies = [
+            remote(kv.at[at], kv.at[at], kv_send.at[k], kv_recv.at[k], peer)
+            for k, (at, peer) in enumerate(((me, across), (me, other), (far, other)))
+        ]
+        copies[0].start()
+        copies[1].start()
+        queries = dot(normed, w_q, NN).astype(bf16)
+        q[...] = queries
+        attn_result[...] = attn_w[...]
+        copies[0].wait_recv()
+        copies[2].start()
+        copies[1].wait_recv()
+        copies[2].wait_recv()
+        keys = kv[...].reshape(KEYS, 2 * WIDTH)
+        outs = []
+        for h in range(HEADS):
+            scores = HD**-0.5 * dot(head(queries, h), head(keys, h), NT) + dead[...]
+            probs = softmax(scores, -1).astype(bf16)
+            outs.append(dot(probs, head(keys, HEADS + h), NN))
+        heads = jnp.concatenate(outs, axis=1).astype(bf16)
+        mixed[...] = heads
+        put_chunks(part_next, 0, dot(heads, w_out, NT).astype(bf16))
+        sum_start(*sums_next)
+        for copy in nears:
+            copy.wait_recv()
+        for copy in fars:
+            copy.start()
+        kv_result[...] = kv[...]
+        sum_middle(*sums_next)
+        sum_end(*sums_next)
+        att_result[...] = att_next[...]
+        for copy in copies + nears + laters + aheads:
+            copy.wait_send()
+        for copy in fars:
             copy.wait()
 
 
-def fixed(shape):
-    return pl.BlockSpec(shape, lambda e: (0,) * len(shape))
-
-
-def experts_forward(x, att, small, routes, ahead, weights, cid):
-    args = (x, att, small, routes)
+def middle(x, att, small, routes, small_next, dead, ahead, later, weights, cid):
+    args = (x, att, small, routes, small_next, dead, ahead, later)
+    shapes = [(ROWS, WIDTH), (4, ROWS, 2 * WIDTH), (ROWS, WIDTH), (2, 4, 80, 384), (PAIR, D), ahead.shape]
     return pl.pallas_call(
-        experts_forward_kernel,
+        middle_kernel,
         grid=(EXPERTS,),
-        out_shape=[jax.ShapeDtypeStruct((2, 4, 80, 384), bf16), jax.ShapeDtypeStruct(ahead.shape, bf16)],
-        in_specs=[fixed(a.shape) for a in args] + [ANY, pl.BlockSpec((16, 96, FE), lambda e: (0, e, 0))],
-        out_specs=[fixed((2, 4, 80, 384)), ANY],
+        out_shape=[jax.ShapeDtypeStruct(s, bf16) for s in shapes + [(4, 4) + later.shape]],
+        in_specs=[fixed(a.shape) for a in args] + [pl.BlockSpec((16, 96, FE), lambda e: (0, e, 0))],
+        out_specs=[fixed(s) for s in shapes] + [ANY],
         scratch_shapes=[
             pltpu.VMEM((PAIR, D), bf16),
             pltpu.VMEM((PAIR, EXPERTS), f32),
             pltpu.VMEM((PAIR, D), f32),
+            pltpu.VMEM((2, 4, 80, 384), bf16),
+            pltpu.VMEM(ahead.shape, bf16),
+            pltpu.VMEM((4, ROWS, 2 * WIDTH), bf16),
+            pltpu.VMEM((2, 4, 80, 384), bf16),
         ]
-        + dma_sems(6)
-        + [pltpu.VMEM((2, 4, 80, 384), bf16)]
-        + sum_scratch(True, 80),
-        input_output_aliases={4: 1},
+        + dma_sems(6, 6, 8, 3)
+        + [pltpu.SemaphoreType.DMA]
+        + sum_scratch(True, 80)
+        + sum_scratch(False, 80),
         compiler_params=params(cid, 56),
-        name="experts_forward",
-    )(*args, ahead, weights)
+        name="middle",
+    )(*args, weights)
 
 
 def layer_backward_kernel(with_moe, *refs):
@@ -1117,13 +1193,10 @@
 
     q0, kv0, mixed0, att0, experts_zero, ahead = attend_forward(x0, (), smalls[0], packs, dead, some, ahead, 3)
     experts_zero = experts_zero.reshape(16, 384, FE)
-    shard, att0 = lax.optimization_barrier((chip[8:16].reshape(384, FE), att0))
-    experts_one = lax.all_gather(shard, CHIPS, axis=0)
-    moe0, attn_w1 = experts_forward(x0, att0, smalls[0], route_rows[0], ahead, experts_zero, 4)
-    attn_w1 = attn_w1.reshape(16, 96, FE)
-    q1, kv1, mixed1, att1, x1 = attend_forward(
-        x0, (att0, moe0), smalls[1], attn_w1, dead, None, None, 5
+    q1, kv1, mixed1, att1, x1, attn_w1, experts_one = middle(
+        x0, att0, smalls[0], route_rows[0], smalls[1], dead, ahead, chip[8:16].reshape(384, FE), experts_zero, 4
     )
+    experts_one = experts_one.reshape(16, 384, FE)
     grad_x1, grad_small1, grad_attn1, some, moe1 = layer_backward(
         (x1, att1, smalls[1], route_rows[1], cotangent, q1, kv1, mixed1, dead, attn_w1), (), experts_one, 6
     )

time: 295 us -> 285 us (0.966)
  between operations: 14.5 us -> 1.07 us
  Pallas kernels: 242 us -> 248 us
  waiting for transfers between devices: 3.7 us -> 0 us
    pallas_call x1, Pallas kernels: 23.6 us -> 53.5 us  [middle(): pl.pallas_call(middle_kernel, grid=(EXPERTS,), out_shape=[jax.ShapeDtypeS...]
    pallas_call x2 -> x1, Pallas kernels: 51 us -> 28.8 us  [attend_forward(): pl.pallas_call(functools.partial(attend_forward_kernel, bool(before)), ou...]
    all_gather x1 -> x0, waiting for transfers between devices: 3.69 us -> none  [shards(): experts_one = lax.all_gather(shard, CHIPS, axis=0)]
  transfers between devices with their start and end apart: 1 -> 0, of which waited for: 1 -> 0; matrix products, arithmetic and copies ran while one was open for 2% -> 0% of each run, Pallas kernels for 16% -> 0%
where the time goes in v6:
time: 285 us; the launch traced here: 284 us
  Pallas kernels  248 us (87%)
  local copies, waits for them, and re-layouts  20.7 us (7%)
  other arithmetic  14.2 us (5%)
    pallas_call x2, Pallas kernels, layer_backward(): pl.pallas_call(functools.partial(layer_backward_kernel, with_moe), grid=(...  103 us
    pallas_call x1, Pallas kernels, middle(): pl.pallas_call(middle_kernel, grid=(EXPERTS,), out_shape=[jax.ShapeDtypeS...  53.5 us
    pallas_call x1, Pallas kernels, start_exchange(): pl.pallas_call(start_kernel, out_shape=[jax.ShapeDtypeStruct(s, bf16) for...  31.3 us
    pallas_call x1, Pallas kernels, attend_forward(): pl.pallas_call(functools.partial(attend_forward_kernel, bool(before)), ou...  28.8 us
    pallas_call x1, Pallas kernels, end_exchange(): pl.pallas_call(end_kernel, out_shape=[jax.ShapeDtypeStruct((2, 8, FE), f3...  28.5 us

profile of v6, /device:TPU:1, one launch (start us, length us, event | category | flops | bytes accessed | tf_op | source)
XLA Modules:
  0.0 283.6 jit_solution(16448697157268463177)
XLA Ops:
  0.7 0.8 iota_compare_fusion.2
  5.2 0.8 maximum_bitcast_fusion.1
  6.1 0.8 slice.84
  7.0 1.9 fusion.2.images
  9.1 1.2 constant_dynamic-slice_fusion.3
  10.5 2.9 %cross.1 = bf16[496,384]{1,0:T(8,128)(2,1)S(1)} custom-call(bf16[496,384]{1,0:T(8,128)(2,1)S(1)} %fusion.4.own), custom_call_target="tpu_custom_call" | custom-call | tf_op jit(solution)/shard_map/cross/pallas_call | solution.py:196
  14.3 0.9 pad_maximum_fusion.6
  15.8 31.3 %start_exchange.1 = (bf16[2,2,176,768]{3,2,1,0:T(8,128)(2,1)}, bf16[4,4,128,384]{3,2,1,0:T(8,128)(2,1)}, bf16[4,4,384,384]{3,2,1,0:T(8,128)(2,1)}) custom-call(bf16[2,176,768]{2,1,0:T(8,128)(2,1)} %fusion.2.images, bf16[128,384]{1,0:T(8,128)(2,1)} %pad_maximum_fusion.8.urgent, bf16[384,384]{1,0:T(8,128)(2,1)} %bitcast.113), custom_call_target="tpu_custom_call" | custom-call | tf_op jit(solution)/shard_map/start_exchange/pallas_call | solution.py:285
  47.9 2.0 fusion.9
  49.9 0.9 bitcast_select_fusion.refs_4_
  52.2 1.0 slice.118
  55.0 28.8 %attend_forward.1 = (bf16[160,192]{1,0:T(8,128)(2,1)}, bf16[4,160,384]{2,1,0:T(8,128)(2,1)}, bf16[160,192]{1,0:T(8,128)(2,1)}, bf16[2,4,80,384]{3,2,1,0:T(8,128)...) custom-call(bf16[320,768]{1,0:T(8,128)(2,1)} %bitcast.100, ...), custom_call_target="tpu_custom_call", output_to_operand_aliasing={{4}: (5, {})} | custom-call | tf_op jit(solution)/shard_map/attend_forward/pallas_call | solution.py:672
  83.8 53.5 %middle.1 = (bf16[160,192]{1,0:T(8,128)(2,1)}, bf16[4,160,384]{2,1,0:T(8,128)(2,1)}, bf16[160,192]{1,0:T(8,128)(2,1)}, bf16[2,4,80,384]{3,2,1,0:T(8,128)(2,1)}, ...) custom-call(bf16[320,768]{1,0:T(8,128)(2,1)} %bitcast.101, ...), custom_call_target="tpu_custom_call" | custom-call | tf_op jit(solution)/shard_map/middle/pallas_call | solution.py:825
  137.3 51.5 %layer_backward.2 = (bf16[320,768]{1,0:T(8,128)(2,1)}, f32[8,768]{1,0:T(8,128)}, bf16[2,768,384]{2,1,0:T(8,128)(2,1)}, bf16[4,384,384]{2,1,0:T(8,128)(2,1)}, bf16[4,80,384]{2,1,0:T(8,128)(2,1)}) custom-call(bf16[320,768]{1,0:T(8,128)(2,1)} %get-tuple-element.46.refs_0_, bf16[2,4,80,384]{3,2,1,0:T(8,128)(2,1)} %get-tuple-element.47.refs_1_, ...), custom_call_target="tpu_custom_call" | custom-call | tf_op jit(solution)/shard_map/layer_backward/pallas_call | solution.py:1132
  189.0 51.1 %layer_backward.3 = (bf16[320,768]{1,0:T(8,128)(2,1)}, f32[8,768]{1,0:T(8,128)}, bf16[2,768,384]{2,1,0:T(8,128)(2,1)}, bf16[4,384,384]{2,1,0:T(8,128)(2,1)}, bf1...) custom-call(bf16[320,768]{1,0:T(8,128)(2,1)} %bitcast.102, bf16[2,4,80,384]{3,2,1,0:T(8,128)(2,1)} %get-tuple-element.43.att.refs_1_, ...), custom_call_target="tpu_custom_call" | custom-call | tf_op jit(solution)/shard_map/layer_backward/pallas_call | solution.py:1132
  240.1 1.0 dynamic-slice_convert_fusion.1
  243.7 1.4 pad_maximum_fusion.part
  247.1 28.5 %end_exchange.1 = (f32[2,8,384]{2,1,0:T(8,128)}, bf16[160,768]{1,0:T(8,128)(2,1)}, f32[2,4,24,768]{3,2,1,0:T(8,128)}, f32[2,4,24,768]{3,2,1,0:T(8,128)}, f32[2,2,24,384]{3,2,1,0:T(8,128)}) custom-call(bf16[2,4,4,64,384]{4,3,2,1,0:T(8,128)(2,1)} %pad_maximum_fusion.part, bf16[160,768]{1,0:T(8,128)(2,1)} %fusion.6.image, ...), custom_call_target="tpu_custom_call" | custom-call | tf_op jit(solution)/shard_map/end_exchange/pallas_call | solution.py:503
  275.6 1.4 slice_bitcast_fusion.5
  277.0 1.4 fusion.10
  278.4 0.9 slice.107
  280.8 1.0 maximum_select_fusion.1
  282.0 0.8 copy.73
  282.8 0.8 copy.74
  (80 shorter events, 15.9 us)
Async XLA Ops:
  0.6 8.3 %copy-start.5 = (bf16[2,4,768,24]{2,3,1,0:T(8,128)(2,1)S(1)}, bf16[2,4,768,24]{2,3,1,0:T(8,128)(2,1)}, u32[]{:S(2)}) copy-start(bf16[2,4,768,24]{2,3,1,0:T(8,128)(2,1)} %param.19) | copy-start | bytes 884740
  0.6 8.3 %copy-start.6 = (bf16[2,4,24,768]{3,2,1,0:T(8,128)(2,1)S(1)}, bf16[2,4,24,768]{3,2,1,0:T(8,128)(2,1)}, u32[]{:S(2)}) copy-start(bf16[2,4,24,768]{3,2,1,0:T(8,128)(2,1)} %param.18) | copy-start | bytes 884740
  137.3 51.6 %copy-start.2 = (bf16[2,4,80,384]{3,2,1,0:T(8,128)(2,1)S(1)}, bf16[2,4,80,384]{3,2,1,0:T(8,128)(2,1)}, u32[]{:S(2)}) copy-start(bf16[2,4,80,384]{3,2,1,0:T(8,128)(2,1)} %get-tuple-element.47.refs_1_) | copy-start | bytes 1474564
  188.9 52.9 %copy-start.10 = (f32[8,768]{1,0:T(8,128)S(1)}, f32[8,768]{1,0:T(8,128)}, u32[]{:S(2)}) copy-start(f32[8,768]{1,0:T(8,128)} %get-tuple-element.63) | copy-start | bytes 73732
  242.4 1.3 copy-start
  243.7 1.4 copy-start.7
  245.1 1.0 copy-start.1
  275.5 3.7 %copy-start.9 = (f32[2,2,24,384]{3,2,1,0:T(8,128)S(1)}, f32[2,2,24,384]{3,2,1,0:T(8,128)}, u32[]{:S(2)}) copy-start(f32[2,2,24,384]{3,2,1,0:T(8,128)} %get-tuple-element.69) | copy-start | bytes 442372
  275.5 5.2 %copy-start.8 = (bf16[160,768]{1,0:T(8,128)(2,1)S(1)}, bf16[160,768]{1,0:T(8,128)(2,1)}, u32[]{:S(2)}) copy-start(bf16[160,768]{1,0:T(8,128)(2,1)} %get-tuple-element.67) | copy-start | bytes 737284
  280.8 1.2 copy-start.4
  280.8 2.0 copy-start.3

commit v7 on v6

--- a/solution.py
+++ b/solution.py
@@ -234,7 +234,8 @@
 
 
 def start_kernel(
-    images, urgent, later, out_images, all_urgent, all_later, own_sem, im_s, im_r, u1_s, u1_r, u2_s, u2_r, l_s, l_r
+    lengths, images, routes, urgent, later, x_out, cot_out, out_routes, dead, all_urgent, all_later,
+    got, own_sem, im_s, im_r, u1_s, u1_r, u2_s, u2_r, l_s, l_r,
 ):
     core = lax.axis_index("core")
     at_x, at_z = places()
@@ -242,7 +243,13 @@
     other = {"core": 1 - core}
     arrive(axis_peers(1, 2, 3) + [other])
     all_urgent[at_x, at_z] = urgent[...]
-    out_images[core, high] = images[high]
+    got[high, core] = images[high]
+    out_routes[high, core] = routes[high]
+    lanes = lax.broadcasted_iota(jnp.int32, (1, KEYS), 1)
+    live = lanes < lengths[0]
+    for block in range(1, 4):
+        live = live | ((lanes >= ROWS * block) & (lanes < ROWS * block + lengths[block]))
+    dead[...] = jnp.where(live, 0.0, -1e30)
     own = pltpu.make_async_copy(later, all_later.at[at_x, at_z], own_sem)
     own.start()
     all_here(7)
@@ -261,39 +268,49 @@
             )
             slabs = line(all_urgent, route, b, rows)
             seconds.append(remote(slabs, slabs, u2_s.at[n], u2_r.at[n], axis_peer(route == 1, k)[0]))
-    swap = remote(images.at[1 - high], out_images.at[core, high], im_s.at[0], im_r.at[0], {"x": (at_x + 2) % 4})
-    kept = remote(images.at[high], out_images.at[core, high], im_s.at[1], im_r.at[1], other)
-    passed = remote(
-        out_images.at[core, 1 - high], out_images.at[core, 1 - high], im_s.at[2], im_r.at[2], other
-    )
-    for copy in firsts + [swap, kept] + laters:
+    swaps, kepts, passes = [], [], []
+    for n, (source, target) in enumerate(((images, got), (routes, out_routes))):
+        here, there = target.at[high, core], target.at[1 - high, core]
+        swaps.append(remote(source.at[1 - high], here, im_s.at[n], im_r.at[n], {"x": (at_x + 2) % 4}))
+        kepts.append(remote(source.at[high], here, im_s.at[2 + n], im_r.at[2 + n], other))
+        passes.append(remote(there, there, im_s.at[4 + n], im_r.at[4 + n], other))
+    for copy in firsts + swaps + kepts + laters:
         copy.start()
     for copy in firsts:
         copy.wait_recv()
     for copy in seconds:
         copy.start()
-    swap.wait_recv()
-    passed.start()
-    for copy in seconds + laters + [kept, passed]:
+    for swap, onward in zip(swaps, passes):
+        swap.wait_recv()
+        onward.start()
+    for copy in kepts + passes:
         copy.wait()
-    for copy in firsts + [swap]:
+    x_out[...] = got[0]
+    lines = lax.broadcasted_iota(jnp.int32, (ROWS, 1), 0)
+    for block in range(2):
+        live = lines < lengths[2 * lax.axis_index("zl") + block]
+        cot_out[block] = jnp.where(live, got[1, block].astype(f32), 0.0).astype(bf16)
+    for copy in seconds + laters:
+        copy.wait()
+    for copy in firsts + swaps:
         copy.wait_send()
     own.wait()
 
 
-def start_exchange(images, urgent, later):
+def start_exchange(lengths, images, routes, urgent, later):
+    shapes = [images.shape, images.shape, (2,) + routes.shape]
+    slabs = [(4, 4) + urgent.shape, (4, 4) + later.shape]
     return pl.pallas_call(
         start_kernel,
-        out_shape=[
-            jax.ShapeDtypeStruct(s, bf16)
-            for s in ((2,) + images.shape, (4, 4) + urgent.shape, (4, 4) + later.shape)
-        ],
-        in_specs=[VMEM] * 3,
-        out_specs=[VMEM, VMEM, ANY],
-        scratch_shapes=[pltpu.SemaphoreType.DMA] + dma_sems(3, 6, 6, 6),
+        out_shape=[jax.ShapeDtypeStruct(s, bf16) for s in shapes]
+        + [jax.ShapeDtypeStruct((1, KEYS), f32)]
+        + [jax.ShapeDtypeStruct(s, bf16) for s in slabs],
+        in_specs=[SMEM] + [VMEM] * 4,
+        out_specs=[VMEM] * 5 + [ANY],
+        scratch_shapes=[pltpu.VMEM((2,) + images.shape, bf16), pltpu.SemaphoreType.DMA] + dma_sems(6, 6, 6, 6),
         compiler_params=params(1, 56),
         name="start_exchange",
-    )(images, urgent, later)
+    )(lengths, images, routes, urgent, later)
 
 
 def spread_near(whole, send, recv):
@@ -1171,26 +1188,16 @@
     later, ahead = chip[0:8].reshape(384, FE), chip[16:18].reshape(96, FE)
     urgent = jnp.concatenate([chip[18:20].reshape(96, FE), low_half[480:496], high_half[480:496]])
 
-    turned = jnp.pad(
-        routes[0].astype(bf16).transpose(0, 2, 1), ((0, 0), (0, 14), (0, D - ROWS))
-    )
-    images = jnp.concatenate([boundary[0], turned], axis=1)
-    got_images, packs, some = start_exchange(images, urgent, later)
+    turned = jnp.pad(routes[0].astype(bf16).transpose(0, 2, 1), ((0, 0), (0, 14), (0, 256 - ROWS)))
+    x0, cotangent, got_routes, dead, packs, some = start_exchange(lengths, boundary[0], turned, urgent, later)
+    x0, cotangent = x0.reshape(PAIR, D), cotangent.reshape(PAIR, D)
     packs = packs.reshape(16, 128, 384)
     tiny = packs[:, 96:128].reshape(32, 16, 384)[:, 0:8, 0:48].reshape(32, 8, 2, 24).transpose(2, 1, 0, 3).reshape(2, 8, D)
     smalls = [tiny[0].astype(f32), tiny[1].astype(f32)]
 
-    live = jnp.arange(ROWS, dtype=jnp.int32)[None, :] < lengths[:, None]
-    dead = jnp.where(live.reshape(1, KEYS), 0.0, -1e30).astype(f32)
-    chip_live = lax.dynamic_slice_in_dim(live, 2 * lax.axis_index("zl"), 2, 0)
-    own_live = pick(chip_live, core, 0)
-
-    x0 = got_images[:, 0, 0:ROWS].reshape(PAIR, D)
-    cotangent = jnp.where(chip_live[:, :, None], got_images[:, 1, 0:ROWS], 0).reshape(PAIR, D)
-    route_rows = [
-        got_images[:, kind, ROWS:, 0:ROWS].transpose(1, 0, 2).reshape(16, PAIR) for kind in range(2)
-    ]
-
+    own_length = pick(lengths, 2 * lax.axis_index("zl") + core, 0)
+    own_live = jnp.arange(ROWS, dtype=jnp.int32) < own_length
+    route_rows = [kind[:, :, 0:ROWS].transpose(1, 0, 2).reshape(16, PAIR) for kind in got_routes]
     q0, kv0, mixed0, att0, experts_zero, ahead = attend_forward(x0, (), smalls[0], packs, dead, some, ahead, 3)
     experts_zero = experts_zero.reshape(16, 384, FE)
     q1, kv1, mixed1, att1, x1, attn_w1, experts_one = middle(

time: 285 us -> 277 us (0.972)
  other arithmetic: 14.2 us -> 9.77 us
where the time goes in v7:
time: 277 us; the launch traced here: 276 us
  Pallas kernels  247 us (89%)
  local copies, waits for them, and re-layouts  18.1 us (7%)
  other arithmetic  9.77 us (4%)
    pallas_call x2, Pallas kernels, layer_backward(): pl.pallas_call(functools.partial(layer_backward_kernel, with_moe), grid=(...  102 us
    pallas_call x1, Pallas kernels, middle(): pl.pallas_call(middle_kernel, grid=(EXPERTS,), out_shape=[jax.ShapeDtypeS...  53.8 us
    pallas_call x1, Pallas kernels, start_exchange(): pl.pallas_call(start_kernel, out_shape=[jax.ShapeDtypeStruct(s, bf16) for...  31 us
    pallas_call x1, Pallas kernels, attend_forward(): pl.pallas_call(functools.partial(attend_forward_kernel, bool(before)), ou...  28.8 us
    pallas_call x1, Pallas kernels, end_exchange(): pl.pallas_call(end_kernel, out_shape=[jax.ShapeDtypeStruct((2, 8, FE), f3...  28.4 us

profile of v7, /device:TPU:1, one launch (start us, length us, event | category | flops | bytes accessed | tf_op | source)
XLA Modules:
  0.0 275.9 jit_solution(3160316594138100314)
XLA Ops:
  0.6 1.1 pad_maximum_fusion.1
  1.9 1.2 constant_dynamic-slice_fusion.2
  4.4 2.9 %cross.1 = bf16[496,384]{1,0:T(8,128)(2,1)S(1)} custom-call(bf16[496,384]{1,0:T(8,128)(2,1)S(1)} %fusion.2.own), custom_call_target="tpu_custom_call" | custom-call | tf_op jit(solution)/shard_map/cross/pallas_call | solution.py:196
  7.5 0.9 pad_maximum_fusion.6
  10.3 31.0 %start_exchange.1 = (bf16[2,160,768]{2,1,0:T(8,128)(2,1)}, bf16[2,160,768]{2,1,0:T(8,128)(2,1)}, bf16[2,2,16,256]{3,2,1,0:T(8,128)(2,1)}, f32[1,640]{1,0:T(1,128...) custom-call(s32[4]{0:T(128)} %lengths.1, bf16[2,160,768]{2,1,0:T(8,128)(2,1)} %bitcast.120, ...), custom_call_target="tpu_custom_call" | custom-call | tf_op jit(solution)/shard_map/start_exchange/pallas_call | solution.py:303
  41.3 1.0 slice.110
  42.6 0.7 reshape.218.refs_1_.small.refs_2_
  43.3 28.8 %attend_forward.1 = (bf16[160,192]{1,0:T(8,128)(2,1)}, bf16[4,160,384]{2,1,0:T(8,128)(2,1)}, bf16[160,192]{1,0:T(8,128)(2,1)}, bf16[2,4,80,384]{3,2,1,0:T(8,128)...) custom-call(bf16[320,768]{1,0:T(8,128)(2,1)} %bitcast.101, ...), custom_call_target="tpu_custom_call", output_to_operand_aliasing={{4}: (5, {})} | custom-call | tf_op jit(solution)/shard_map/attend_forward/pallas_call | solution.py:689
  72.3 0.7 reshape.219.small_next.refs_2_
  73.7 53.8 %middle.1 = (bf16[160,192]{1,0:T(8,128)(2,1)}, bf16[4,160,384]{2,1,0:T(8,128)(2,1)}, bf16[160,192]{1,0:T(8,128)(2,1)}, bf16[2,4,80,384]{3,2,1,0:T(8,128)(2,1)}, ...) custom-call(bf16[320,768]{1,0:T(8,128)(2,1)} %bitcast.102, ...), custom_call_target="tpu_custom_call" | custom-call | tf_op jit(solution)/shard_map/middle/pallas_call | solution.py:842
  128.3 50.7 %layer_backward.2 = (bf16[320,768]{1,0:T(8,128)(2,1)}, f32[8,768]{1,0:T(8,128)}, bf16[2,768,384]{2,1,0:T(8,128)(2,1)}, bf16[4,384,384]{2,1,0:T(8,128)(2,1)}, bf16[4,80,384]{2,1,0:T(8,128)(2,1)}) custom-call(bf16[320,768]{1,0:T(8,128)(2,1)} %get-tuple-element.51.refs_0_, bf16[2,4,80,384]{3,2,1,0:T(8,128)(2,1)} %get-tuple-element.52.refs_1_, ...), custom_call_target="tpu_custom_call" | custom-call | tf_op jit(solution)/shard_map/layer_backward/pallas_call | solution.py:1149
  179.0 1.2 copy.67
  181.4 51.2 %layer_backward.3 = (bf16[320,768]{1,0:T(8,128)(2,1)}, f32[8,768]{1,0:T(8,128)}, bf16[2,768,384]{2,1,0:T(8,128)(2,1)}, bf16[4,384,384]{2,1,0:T(8,128)(2,1)}, bf1...) custom-call(bf16[320,768]{1,0:T(8,128)(2,1)} %bitcast.103, bf16[2,4,80,384]{3,2,1,0:T(8,128)(2,1)} %get-tuple-element.47.att.refs_1_, ...), custom_call_target="tpu_custom_call" | custom-call | tf_op jit(solution)/shard_map/layer_backward/pallas_call | solution.py:1149
  232.6 1.0 dynamic-slice_convert_fusion.1
  236.4 1.4 pad_maximum_fusion.part
  237.9 28.4 %end_exchange.1 = (f32[2,8,384]{2,1,0:T(8,128)}, bf16[160,768]{1,0:T(8,128)(2,1)}, f32[2,4,24,768]{3,2,1,0:T(8,128)}, f32[2,4,24,768]{3,2,1,0:T(8,128)}, f32[2,2,24,384]{3,2,1,0:T(8,128)}) custom-call(bf16[2,4,4,64,384]{4,3,2,1,0:T(8,128)(2,1)} %pad_maximum_fusion.part, bf16[160,768]{1,0:T(8,128)(2,1)} %fusion.4.image, ...), custom_call_target="tpu_custom_call" | custom-call | tf_op jit(solution)/shard_map/end_exchange/pallas_call | solution.py:520
  266.3 0.9 slice.99
  267.3 1.6 slice_bitcast_fusion
  269.6 1.0 bitcast_convert_fusion
  270.6 1.0 maximum_select_fusion.1
  271.6 1.4 fusion.7
  273.0 1.3 slice_bitcast_fusion.7
  274.3 0.8 copy.73
  275.1 0.8 copy.74
  (85 shorter events, 9.8 us)
Async XLA Ops:
  1.9 1.4 slice-start
  3.2 0.9 copy-start.5
  3.2 0.9 copy-start.9
  3.2 1.0 copy-start.11
  3.2 1.0 copy-start.12
  3.2 1.0 copy-start.13
  7.4 2.2 copy-start.10
  43.3 29.7 %copy-start.6 = (bf16[2,2,16,256]{3,2,1,0:T(8,128)(2,1)S(1)}, bf16[2,2,16,256]{3,2,1,0:T(8,128)(2,1)}, u32[]{:S(2)}) copy-start(bf16[2,2,16,256]{3,2,1,0:T(8,128)(2,1)} %get-tuple-element.48) | copy-start | bytes 98308
  179.0 1.6 copy-start.2
  180.2 1.1 copy-start.1
  181.4 52.3 %copy-start.14 = (s32[4]{0:T(128)S(1)}, s32[4]{0:T(128)}, u32[]{:S(2)}) copy-start(s32[4]{0:T(128)} %lengths.1) | copy-start | bytes 52
  232.6 3.2 %copy-start.8 = (f32[8,768]{1,0:T(8,128)S(1)}, f32[8,768]{1,0:T(8,128)}, u32[]{:S(2)}) copy-start(f32[8,768]{1,0:T(8,128)} %get-tuple-element.68) | copy-start | bytes 73732
  232.6 3.3 %copy-start.7 = (f32[8,768]{1,0:T(8,128)S(1)}, f32[8,768]{1,0:T(8,128)}, u32[]{:S(2)}) copy-start(f32[8,768]{1,0:T(8,128)} %get-tuple-element.69) | copy-start | bytes 73732
  234.9 1.5 copy-start
  270.5 3.7 %copy-start.4 = (f32[2,4,24,768]{3,2,1,0:T(8,128)S(1)}, f32[2,4,24,768]{3,2,1,0:T(8,128)}, u32[]{:S(2)}) copy-start(f32[2,4,24,768]{3,2,1,0:T(8,128)} %get-tuple-element.112) | copy-start | bytes 1769476
  270.6 4.5 %copy-start.3 = (f32[2,4,24,768]{3,2,1,0:T(8,128)S(1)}, f32[2,4,24,768]{3,2,1,0:T(8,128)}, u32[]{:S(2)}) copy-start(f32[2,4,24,768]{3,2,1,0:T(8,128)} %get-tuple-element.77) | copy-start | bytes 1769476

commit v8 on v7

--- a/solution.py
+++ b/solution.py
@@ -410,8 +410,8 @@
 
 
 def end_kernel(
-    part, image, half_sum, some, some_attn, tiny, out_image, grad_in, grad_out, grad_attn,
-    out, out_half, own_sum, other_sum, landed, sums, pieces, mids, lands, slabs, attn_slabs, cx_s, cx_r, sl_s, sl_r, at_s, at_r, p1_s, p1_r, p2_s, p2_r,
+    part, image, kept, half_sum, some, some_attn, tiny, ends, grad_in, grad_out, grad_attn,
+    out, out_image, out_half, own_sum, other_sum, landed, sums, pieces, mids, lands, slabs, attn_slabs, cx_s, cx_r, sl_s, sl_r, at_s, at_r, p1_s, p1_r, p2_s, p2_r,
 ):
     def own_lines(rows):
         rows = rows.astype(f32)
@@ -511,29 +511,31 @@
     for copy in firsts + [halves]:
         copy.wait_send()
     swap.wait()
-
-
-def end_exchange(part, image, half_sum, some, some_attn):
+    ends[x // 2] = kept[...]
+    ends[1 - x // 2] = out_image[...].astype(f32)
+
+
+def end_exchange(part, image, kept, half_sum, some, some_attn):
     slab = (480, FE)
-    scratch = [half_sum.shape, slab, slab] + [(4, 4, 64, FE)] * 2 + [(3, 4, 64, FE), (4, 64, FE), (3, 64, FE)]
+    scratch = [image.shape, half_sum.shape, slab, slab] + [(4, 4, 64, FE)] * 2 + [(3, 4, 64, FE), (4, 64, FE), (3, 64, FE)]
     scratch += [(3,) + some.shape[1:], (2, 3, 48, FE)]
     return pl.pallas_call(
         end_kernel,
         out_shape=[
             jax.ShapeDtypeStruct((2, 8, FE), f32),
-            jax.ShapeDtypeStruct(image.shape, bf16),
+            jax.ShapeDtypeStruct((2,) + image.shape, f32),
             jax.ShapeDtypeStruct((2, EXPERTS, 24, D), f32),
             jax.ShapeDtypeStruct((2, EXPERTS, 24, D), f32),
             jax.ShapeDtypeStruct((2, 2, 24, FE), f32),
         ],
-        in_specs=[VMEM] * 5,
+        in_specs=[VMEM] * 6,
         out_specs=[VMEM] * 5,
         scratch_shapes=[pltpu.VMEM((2, 64, FE), f32)]
         + [pltpu.VMEM(s, bf16) for s in scratch]
         + dma_sems(5, 6, 6, 6, 6),
         compiler_params=params(2, 56),
         name="end_exchange",
-    )(part, image, half_sum, some, some_attn)
+    )(part, image, kept, half_sum, some, some_attn)
 
 
 def block_rows(ref, block):
@@ -771,7 +773,7 @@
             rows = half(ahead.shape[2], 1)
             attn_w[at_x, j, rows] = ahead[at_x, j, rows]
         all_here(11)
-        for copy in aheads + laters + [own]:
+        for copy in laters + [own] + aheads:
             copy.start()
 
     w_in, w_out_t = expert_weights(weights)
@@ -788,7 +790,7 @@
         for copy in laters:
             copy.wait_recv()
         own.wait()
-        for copy in nears:
+        for copy in nears[2:]:
             copy.start()
         sum_middle(*sums)
         sum_end(*sums)
@@ -805,6 +807,8 @@
         ]
         copies[0].start()
         copies[1].start()
+        for copy in nears[:2]:
+            copy.start()
         queries = dot(normed, w_q, NN).astype(bf16)
         q[...] = queries
         attn_result[...] = attn_w[...]
@@ -1229,9 +1233,7 @@
     tiny = tiny.transpose(0, 2, 3, 1, 4).reshape(2, 16, 16, 24)
     tiny = jnp.pad(tiny, ((0, 0), (0, 0), (0, 0), (0, 384 - 24)))
     packs = jnp.concatenate([grad_attn0.reshape(2, 16, 48, 384), tiny], axis=2).reshape(2, 4, 4, 64, FE)
-    tiny, landed, grad_w_in, grad_w_exp_out, attn = end_exchange(packs, sent, sums1, some, some_attn)
-    landed = landed.astype(f32)
-    ends = jnp.where(high == 0, jnp.stack([kept, landed]), jnp.stack([landed, kept]))
+    tiny, ends, grad_w_in, grad_w_exp_out, attn = end_exchange(packs, sent, kept, sums1, some, some_attn)
     grad_w_qkv = jnp.concatenate([attn[:, 1, :, None, :WIDTH], attn[:, 0].reshape(2, 24, 2, WIDTH)], axis=2)
     grad_w_out = attn[:, 1, :, WIDTH:].transpose(0, 2, 1)
     tiny = tiny[:, :, 0:24]

time: 277 us -> 276 us (level)
  no operation moved by 1% of the time
where the time goes in v8:
time: 276 us; the launch traced here: 275 us
  Pallas kernels  247 us (89%)
  local copies, waits for them, and re-layouts  19.9 us (7%)
  other arithmetic  7.77 us (3%)
    pallas_call x2, Pallas kernels, layer_backward(): pl.pallas_call(functools.partial(layer_backward_kernel, with_moe), grid=(...  104 us
    pallas_call x1, Pallas kernels, middle(): pl.pallas_call(middle_kernel, grid=(EXPERTS,), out_shape=[jax.ShapeDtypeS...  52.1 us
    pallas_call x1, Pallas kernels, start_exchange(): pl.pallas_call(start_kernel, out_shape=[jax.ShapeDtypeStruct(s, bf16) for...  31 us
    pallas_call x1, Pallas kernels, attend_forward(): pl.pallas_call(functools.partial(attend_forward_kernel, bool(before)), ou...  28.8 us
    pallas_call x1, Pallas kernels, end_exchange(): pl.pallas_call(end_kernel, out_shape=[jax.ShapeDtypeStruct((2, 8, FE), f3...  27.9 us

profile of v8, /device:TPU:1, one launch (start us, length us, event | category | flops | bytes accessed | tf_op | source)
XLA Modules:
  0.0 275.4 jit_solution(9712688667071052126)
XLA Ops:
  0.6 1.1 pad_maximum_fusion.1
  1.9 1.2 constant_dynamic-slice_fusion.2
  4.4 2.9 %cross.1 = bf16[496,384]{1,0:T(8,128)(2,1)S(1)} custom-call(bf16[496,384]{1,0:T(8,128)(2,1)S(1)} %fusion.2.own), custom_call_target="tpu_custom_call" | custom-call | tf_op jit(solution)/shard_map/cross/pallas_call | solution.py:196
  7.5 0.9 pad_maximum_fusion.6
  10.3 31.0 %start_exchange.1 = (bf16[2,160,768]{2,1,0:T(8,128)(2,1)}, bf16[2,160,768]{2,1,0:T(8,128)(2,1)}, bf16[2,2,16,256]{3,2,1,0:T(8,128)(2,1)}, f32[1,640]{1,0:T(1,128...) custom-call(s32[4]{0:T(128)} %lengths.1, bf16[2,160,768]{2,1,0:T(8,128)(2,1)} %bitcast.119, ...), custom_call_target="tpu_custom_call" | custom-call | tf_op jit(solution)/shard_map/start_exchange/pallas_call | solution.py:303
  41.3 1.0 slice.110
  42.6 0.7 reshape.160.refs_1_.small.refs_2_
  43.4 28.8 %attend_forward.1 = (bf16[160,192]{1,0:T(8,128)(2,1)}, bf16[4,160,384]{2,1,0:T(8,128)(2,1)}, bf16[160,192]{1,0:T(8,128)(2,1)}, bf16[2,4,80,384]{3,2,1,0:T(8,128)...) custom-call(bf16[320,768]{1,0:T(8,128)(2,1)} %bitcast.99, ...), custom_call_target="tpu_custom_call", output_to_operand_aliasing={{4}: (5, {})} | custom-call | tf_op jit(solution)/shard_map/attend_forward/pallas_call | solution.py:691
  72.3 0.7 reshape.161.small_next.refs_2_
  73.8 52.1 %middle.1 = (bf16[160,192]{1,0:T(8,128)(2,1)}, bf16[4,160,384]{2,1,0:T(8,128)(2,1)}, bf16[160,192]{1,0:T(8,128)(2,1)}, bf16[2,4,80,384]{3,2,1,0:T(8,128)(2,1)}, ...) custom-call(bf16[320,768]{1,0:T(8,128)(2,1)} %bitcast.100, ...), custom_call_target="tpu_custom_call" | custom-call | tf_op jit(solution)/shard_map/middle/pallas_call | solution.py:846
  126.6 51.7 %layer_backward.2 = (bf16[320,768]{1,0:T(8,128)(2,1)}, f32[8,768]{1,0:T(8,128)}, bf16[2,768,384]{2,1,0:T(8,128)(2,1)}, bf16[4,384,384]{2,1,0:T(8,128)(2,1)}, bf16[4,80,384]{2,1,0:T(8,128)(2,1)}) custom-call(bf16[320,768]{1,0:T(8,128)(2,1)} %get-tuple-element.51.refs_0_, bf16[2,4,80,384]{3,2,1,0:T(8,128)(2,1)} %get-tuple-element.52.refs_1_, ...), custom_call_target="tpu_custom_call" | custom-call | tf_op jit(solution)/shard_map/layer_backward/pallas_call | solution.py:1153
  178.3 1.2 copy.67
  180.6 52.1 %layer_backward.3 = (bf16[320,768]{1,0:T(8,128)(2,1)}, f32[8,768]{1,0:T(8,128)}, bf16[2,768,384]{2,1,0:T(8,128)(2,1)}, bf16[4,384,384]{2,1,0:T(8,128)(2,1)}, bf1...) custom-call(bf16[320,768]{1,0:T(8,128)(2,1)} %bitcast.101, bf16[2,4,80,384]{3,2,1,0:T(8,128)(2,1)} %get-tuple-element.47.att.refs_1_, ...), custom_call_target="tpu_custom_call" | custom-call | tf_op jit(solution)/shard_map/layer_backward/pallas_call | solution.py:1153
  232.8 1.0 dynamic-slice_convert_fusion.1
  235.2 0.8 dynamic-slice_bitcast_fusion.kept
  237.4 1.4 pad_maximum_fusion.part
  238.8 27.9 %end_exchange.1 = (f32[2,8,384]{2,1,0:T(8,128)}, f32[2,160,768]{2,1,0:T(8,128)}, f32[2,4,24,768]{3,2,1,0:T(8,128)}, f32[2,4,24,768]{3,2,1,0:T(8,128)}, f32[2,2,24,384]{3,2,1,0:T(8,128)}) custom-call(bf16[2,4,4,64,384]{4,3,2,1,0:T(8,128)(2,1)} %pad_maximum_fusion.part, bf16[160,768]{1,0:T(8,128)(2,1)} %fusion.4.image, ...), custom_call_target="tpu_custom_call" | custom-call | tf_op jit(solution)/shard_map/end_exchange/pallas_call | solution.py:522
  266.8 1.0 slice.99
  267.9 1.6 slice_bitcast_fusion
  270.2 1.4 fusion.7
  271.5 1.3 slice_bitcast_fusion.7
  272.8 0.9 copy.74
  273.8 0.8 copy.75
  274.6 0.8 copy.76
  (86 shorter events, 9.8 us)
Async XLA Ops:
  1.9 1.4 slice-start
  3.2 0.9 copy-start.6
  3.2 0.9 copy-start.10
  3.2 1.0 copy-start.12
  3.2 1.0 copy-start.13
  3.2 1.0 copy-start.14
  7.4 2.2 copy-start.11
  43.4 29.7 %copy-start.7 = (bf16[2,2,16,256]{3,2,1,0:T(8,128)(2,1)S(1)}, bf16[2,2,16,256]{3,2,1,0:T(8,128)(2,1)}, u32[]{:S(2)}) copy-start(bf16[2,2,16,256]{3,2,1,0:T(8,128)(2,1)} %get-tuple-element.48) | copy-start | bytes 98308
  178.3 1.6 copy-start.2
  179.5 1.1 copy-start.1
  180.6 53.1 %copy-start.15 = (s32[4]{0:T(128)S(1)}, s32[4]{0:T(128)}, u32[]{:S(2)}) copy-start(s32[4]{0:T(128)} %lengths.1) | copy-start | bytes 52
  235.0 1.7 copy-start.9
  235.0 1.9 copy-start.8
  235.2 2.2 copy-start
  266.7 6.1 %copy-start.3 = (f32[2,160,768]{2,1,0:T(8,128)S(1)}, f32[2,160,768]{2,1,0:T(8,128)}, u32[]{:S(2)}) copy-start(f32[2,160,768]{2,1,0:T(8,128)} %get-tuple-element.73) | copy-start | bytes 2949124
  266.8 7.0 %copy-start.5 = (f32[2,4,24,768]{3,2,1,0:T(8,128)S(1)}, f32[2,4,24,768]{3,2,1,0:T(8,128)}, u32[]{:S(2)}) copy-start(f32[2,4,24,768]{3,2,1,0:T(8,128)} %get-tuple-element.112) | copy-start | bytes 1769476
  272.8 1.8 copy-start.4
